TPU v7x, 32 devices: a whole 2x2x4 slice. The times are simulated.
32 devices in a mesh: ha: 4 (over z), wa: 8 (over y, x, core).
Axes of the slice: x: 2, y: 2, z: 4, core: 2. Of those that a mesh axis runs over, the one named last changes fastest.
Arguments:
- queries: bfloat16 [4, 8, 384, 1536], P('ha', 'wa'), may hold values from -15 to 15
- keys_values: bfloat16 [4, 8, 3, 2, 384, 1536], P('ha', 'wa'), may hold values from -9 to 9
- far_offsets: int32 [8, 4, 12, 2], P('wa', 'ha'), may hold values from 0 to 6, all different within a row; in each aligned block of 12 rows (0 to 11, 12 to 23, ..., all dimensions but the last counted through in order) at most 5 rows name the same one
Outputs:
- attended: bfloat16 [4, 8, 384, 1536], P('ha', 'wa')
Inputs may be any that keep to these rules, and one draw needn't show every extreme that they name: `far_offsets`: within the rows of one device (one tile column w, its 1 tile rows, all heads) each offset is named by at most 5 of those rows; each row names 2 different offsets.
All inputs are finite; a program needn't handle non-finite values.
Results may differ from a plain program's by a relative error of at most 0.0048.
Values may be sent and summed in bfloat16 or wider, within the bound.
No kernel may reach another device: no remote copies, remote signals or barrier semaphores. Data moves between devices by JAX's collectives and lax.ppermute only.
A program may use at most 320 MiB of HBM per device.

v0:
```python
import jax
import jax.numpy as jnp
from jax import lax
from jax.sharding import PartitionSpec as P

HEADS = 12
HD = 128
TILE = 384
TT = 3
FAR = 2


def with_halo(array, sides, width):
    for axis, dim in sides:
        devices, length = (lax.axis_size(axis), array.shape[dim])
        up = [(i, (i + 1) % devices) for i in range(devices - 1)]
        down = [(j, i) for i, j in up]
        last = lax.slice_in_dim(array, length - width, length, axis=dim)
        first = lax.slice_in_dim(array, 0, width, axis=dim)
        before = lax.ppermute(last, axis, up)
        after = lax.ppermute(first, axis, down)
        array = jnp.concatenate([before, array, after], axis=dim)
    return array


def slot_table(offset_block, column, grid_width, capacity):
    flat_offsets = offset_block.reshape(-1)
    owners = (column + 1 + flat_offsets) % grid_width
    request_count = flat_offsets.shape[0]
    onehot = (owners[:, None] == jnp.arange(grid_width, dtype=jnp.int32)[None, :]).astype(jnp.int32)
    before = jnp.cumsum(onehot, axis=0) - onehot
    places = jnp.sum(onehot * before, axis=1)
    tile_codes = jnp.arange(request_count, dtype=jnp.int32) // FAR
    matches = onehot[:, :, None] * (
        places[:, None, None] == jnp.arange(capacity, dtype=jnp.int32)[None, None, :]
    ).astype(jnp.int32)
    wanted_table = jnp.sum(matches * (tile_codes[:, None, None] + 1), axis=0) - 1
    return (owners, places, wanted_table)


def fetch_tiles(kv_heads, wanted_table):
    clipped = jnp.clip(wanted_table, 0, kv_heads.shape[0] * HEADS - 1)
    return kv_heads[clipped // HEADS, :, :, clipped % HEADS, :]


def on_device(queries, keys_values, far_offsets):
    tile_rows = queries.shape[0]
    grid_width = lax.axis_size("wa")
    column = lax.axis_index("wa")
    first_row = lax.axis_index("ha") * tile_rows
    height = lax.axis_size("ha") * tile_rows
    capacity = max(2, 3 * tile_rows * HEADS * FAR // (2 * (grid_width - 1)))
    padded = with_halo(keys_values, (("ha", 0), ("wa", 1)), 1)
    kv_heads = keys_values[:, 0, 1].reshape(tile_rows, 2, TILE, HEADS, HD)
    owners, places, wanted_table = slot_table(far_offsets[0], column, grid_width, capacity)
    arrived = lax.all_to_all(
        fetch_tiles(
            kv_heads, lax.all_to_all(wanted_table, "wa", split_axis=0, concat_axis=0, tiled=True)
        ),
        "wa",
        split_axis=0,
        concat_axis=0,
        tiled=True,
    )
    far_kv = arrived[owners, places].reshape(tile_rows, HEADS, FAR, 2, TILE, HD)
    by_head = jnp.moveaxis(far_kv, 1, 0)
    steps_three = jnp.arange(3, dtype=jnp.int32)
    row_pos = first_row + jnp.arange(tile_rows, dtype=jnp.int32)[:, None] + steps_three[None, :] - 1
    row_inside = (row_pos >= 0) & (row_pos < height)
    col_pos = column + steps_three - 1
    col_inside = (col_pos >= 0) & (col_pos < grid_width)
    inside = row_inside[:, :, None] & col_inside[None, None, :]
    key_mask = jnp.concatenate(
        [
            jnp.repeat(inside.reshape(tile_rows, 9), TT * TILE, axis=1),
            jnp.ones((tile_rows, FAR * TILE), dtype=bool),
        ],
        axis=1,
    )[:, None, :]
    query_tiles = queries[:, 0]
    score_scale = 1.0 / HD**0.5

    def one_head(head_item):
        head_index, far_head = head_item
        head_queries = lax.dynamic_slice_in_dim(query_tiles, head_index * HD, HD, 2)
        head_kv = lax.dynamic_slice_in_dim(padded, head_index * HD, HD, 5)
        window = jnp.stack(
            [head_kv[row_step : row_step + tile_rows] for row_step in range(3)], axis=1
        )
        key_tiles = jnp.concatenate(
            [
                window[:, :, :, :, 0].reshape(tile_rows, 9 * TT * TILE, HD),
                far_head[:, :, 0].reshape(tile_rows, FAR * TILE, HD),
            ],
            axis=1,
        )
        value_tiles = jnp.concatenate(
            [
                window[:, :, :, :, 1].reshape(tile_rows, 9 * TT * TILE, HD),
                far_head[:, :, 1].reshape(tile_rows, FAR * TILE, HD),
            ],
            axis=1,
        )
        scores = (
            jnp.einsum("iqd,ikd->iqk", head_queries, key_tiles, preferred_element_type=jnp.float32)
            * score_scale
        )
        scores = jnp.where(key_mask, scores, -1e30)
        peak_score = jnp.max(scores, axis=2, keepdims=True)
        weights = jnp.exp(scores - peak_score)
        totals = jnp.sum(weights, axis=2, keepdims=True)
        summed = jnp.einsum(
            "iqk,ikd->iqd",
            weights.astype(jnp.bfloat16),
            value_tiles,
            preferred_element_type=jnp.float32,
        )
        return (summed / totals).astype(jnp.bfloat16)

    per_head = lax.map(one_head, (jnp.arange(HEADS, dtype=jnp.int32), by_head))
    attended = jnp.transpose(per_head, (1, 2, 0, 3)).reshape(tile_rows, 1, TILE, HEADS * HD)
    return attended


def solution(mesh):
    placed = (
        P("ha", "wa", None, None),
        P("ha", "wa", None, None, None, None),
        P("wa", "ha", None, None),
    )
    return jax.shard_map(
        on_device, mesh=mesh, in_specs=placed, out_specs=P("ha", "wa", None, None), check_vma=False
    )
```

profile of v0, /device:TPU:3, one launch (start us, length us, event | category | flops | bytes accessed | tf_op | source)
XLA Modules:
  0.0 1232.5 jit_solution(10357980939844142822)
XLA Ops:
  7.7 147.1 %collective-permute-done = bf16[1,1,3,2,384,1536]{5,4,3,2,1,0:T(8,128)(2,1)} collective-permute-done((bf16[1,1,3,2,384,1536]{5,4,3,2,1,0:T(8,128)(2,1)}, bf16[1,1,3,2,384,1536]{5,4,3,2,1,0:T(8,128)(2,1)}, u32[]{:S(2)}, u32[]{:S(2)}) %collective-permute-start) | collective-permute-done | bytes 7077920 | tf_op jit(solution)/shard_map/ppermute | solution.py:20
  176.2 10.5 all-to-all-start
  194.0 435.2 %all-to-all-done = s32[8,1,5]{2,1,0:T(1,128)S(1)} async-done(((s32[8,1,5]{2,1,0:T(1,128)}), s32[8,1,5]{2,1,0:T(1,128)S(1)}, u32[]{:S(2)}, u32[]{:S(2)}) %all-to-all-start) | async-done | bytes 192 | tf_op jit(solution)/shard_map/all_to_all | solution.py:58
  642.0 86.4 %all-to-all-done.1 = bf16[8,5,2,384,128]{4,3,2,1,0:T(8,128)(2,1)} async-done(((bf16[8,5,2,384,128]{4,3,2,1,0:T(8,128)(2,1)}), bf16[8,5,2,384,128]{4,3,2,1,0:T(8,128)(2,1)}, u32[]{:S(2)}, u32[]{:S(2)}) %all-to-all-start.1) | async-done | bytes 7864352 | tf_op jit(solution)/shard_map/all_to_all | solution.py:56
  735.2 42.5 %pad_maximum_fusion.1 = bf16[3,3,3,2,384,1536]{5,4,3,2,1,0:T(8,128)(2,1)} fusion(bf16[3,1,3,2,384,1536]{5,4,3,2,1,0:T(8,128)(2,1)} %collective-permute-done.3, bf16[3,1,3,2,384,1536]{5,4,3,2,1,0:T(8,128)(2,1)} %constant_dynamic-update-slice_fusion.1, bf16[3,1,3,2,384,1536]{5,4,3,2,1,0:T(8,128)(2,1)} %collective-permute-done.2), kind=kLoop, calls=%fused_computation.29 | loop fusion | flops 63700992 | bytes 127401984 | tf_op jit(solution)/shard_map/concatenate | solution.py:22
  777.8 452.4 %while.10 = (s32[]{:T(128)}, bf16[12,1,384,128]{2,3,0,1:T(8,128)(2,1)}, pred[1,1,11136]{2,1,0:T(4,128)(4,1)S(1)}, s32[12]{0:T(128)S(1)}, bf16[1,384,1536]{2,1,0:...) while((s32[]{:T(128)}, ...), condition=%wide.region_6.7_spmd, body=%wide.region_3.6_spmd.sunk | while | flops 2236169472 | bytes 101687688 | solution.py:120
  785.7 12.3 fusion.53
  797.9 8.4 fusion.54
  823.4 12.3 fusion.53
  835.6 8.4 fusion.54
  861.0 12.3 fusion.53
  873.3 8.4 fusion.54
  898.7 12.3 fusion.53
  911.0 8.4 fusion.54
  936.4 12.3 fusion.53
  948.7 8.4 fusion.54
  974.1 12.3 fusion.53
  1011.8 12.3 fusion.53
  1024.1 8.4 fusion.54
  1049.5 12.3 fusion.53
  1087.2 12.3 fusion.53
  1124.9 12.3 fusion.53
  1162.6 12.3 fusion.53
  1200.3 12.3 fusion.53
  (205 shorter events, 304.7 us)
Async XLA Ops:
  0.0 161.5 %copy-start.1 = (bf16[1,1,3,2,384,1536]{5,4,3,2,1,0:T(8,128)(2,1)S(1)}, bf16[1,1,3,2,384,1536]{5,4,3,2,1,0:T(8,128)(2,1)}, u32[]{:S(2)}) copy-start(bf16[1,1,3,2,384,1536]{5,4,3,2,1,0:T(8,128)(2,1)} %param.6) | copy-start | bytes 21233668
  0.0 154.8 %collective-permute-start = (bf16[1,1,3,2,384,1536]{5,4,3,2,1,0:T(8,128)(2,1)}, bf16[1,1,3,2,384,1536]{5,4,3,2,1,0:T(8,128)(2,1)}, u32[]{:S(2)}, u32[]{:S(2)}) collective-permute-start(bf16[1,1,3,2,384,1536]{5,4,3,2,1,0:T(8,128)(2,1)} %param.6), channel_id=1, source_target_pairs={{0,8},{8,16},{16,24},{1,9},{9,17},{17,25},{2,10},{10,18},{18,26},{... | collective-permute-start | bytes 21233672 | tf_op jit(solution)/shard_map/ppermute | solution.py:20
  6.4 158.4 %collective-permute-start.1 = (bf16[1,1,3,2,384,1536]{5,4,3,2,1,0:T(8,128)(2,1)}, bf16[1,1,3,2,384,1536]{5,4,3,2,1,0:T(8,128)(2,1)S(1)}, u32[]{:S(2)}, u32[]{:S(2)}) collective-permute-start(bf16[1,1,3,2,384,1536]{5,4,3,2,1,0:T(8,128)(2,1)} %param.6), channel_id=1, source_target_pairs={{8,0},{16,8},{24,16},{9,1},{17,9},{25,17},{10,2},{18,10},{26,18},{... | collective-permute-start | bytes 21233672 | tf_op jit(solution)/shard_map/ppermute | solution.py:21
  164.8 9.9 copy-start.2
  168.2 567.0 %collective-permute-start.3 = (bf16[3,1,3,2,384,1536]{5,4,3,2,1,0:T(8,128)(2,1)}, bf16[3,1,3,2,384,1536]{5,4,3,2,1,0:T(8,128)(2,1)}, u32[]{:S(2)}, u32[]{:S(2)}) collective-permute-start(bf16[3,1,3,2,384,1536]{5,4,3,2,1,0:T(8,128)(2,1)} %constant_dynamic-update-slice_fusion.1), channel_id=1, source_target_pairs={{1,0},{2,1},{3,2},{4,3},{5,4},{6,5},{7,6},{9,8},{10,9},{11,10},{12... | collective-permute-start | bytes 63701000 | tf_op jit(solution)/shard_map/ppermute | solution.py:21
  171.7 563.6 %collective-permute-start.2 = (bf16[3,1,3,2,384,1536]{5,4,3,2,1,0:T(8,128)(2,1)}, bf16[3,1,3,2,384,1536]{5,4,3,2,1,0:T(8,128)(2,1)}, u32[]{:S(2)}, u32[]{:S(2)}) collective-permute-start(bf16[3,1,3,2,384,1536]{5,4,3,2,1,0:T(8,128)(2,1)} %constant_dynamic-update-slice_fusion.1), channel_id=1, source_target_pairs={{0,1},{1,2},{2,3},{3,4},{4,5},{5,6},{6,7},{8,9},{9,10},{10,11},{11... | collective-permute-start | bytes 63701000 | tf_op jit(solution)/shard_map/ppermute | solution.py:20
  176.2 453.1 %all-to-all-start = ((s32[8,1,5]{2,1,0:T(1,128)}), s32[8,1,5]{2,1,0:T(1,128)S(1)}, u32[]{:S(2)}, u32[]{:S(2)}) async-start(s32[8,1,5]{2,1,0:T(1,128)} %copy.51), calls=%async_computation | async-start | bytes 8192 | tf_op jit(solution)/shard_map/all_to_all | solution.py:58
  635.7 92.7 %all-to-all-start.1 = ((bf16[8,5,2,384,128]{4,3,2,1,0:T(8,128)(2,1)}), bf16[8,5,2,384,128]{4,3,2,1,0:T(8,128)(2,1)}, u32[]{:S(2)}, u32[]{:S(2)}) async-start(bf16[8,5,2,384,128]{4,3,2,1,0:T(8,128)(2,1)} %bitcast.92), calls=%async_computation.1 | async-start | bytes 15728640 | tf_op jit(solution)/shard_map/all_to_all | solution.py:56
  797.9 8.4 copy-start
  835.6 8.4 copy-start
  873.3 8.4 copy-start
  911.0 8.4 copy-start
  948.7 8.4 copy-start
  986.4 8.4 copy-start
  1024.0 8.4 copy-start
  1061.7 8.4 copy-start
  1099.4 8.4 copy-start
  1137.1 8.4 copy-start
  1174.8 8.4 copy-start
  1212.6 8.4 copy-start
where the time goes:
time: 1240 us; the launch traced here: 1230 us
  waiting for transfers between devices  669 us (54%)
  matrix products  248 us (20%)
  other arithmetic  153 us (12%)
  local copies, waits for them, and re-layouts  124 us (10%)
  starting transfers between devices  30.3 us (2%)
    all_to_all x1, waiting for transfers between devices, on_device(): lax.all_to_all(wanted_table, 'wa', split_axis=0, concat_axis=0, tiled=True)  435 us
    dot_general x12, matrix products, one_head(): jnp.einsum('iqd,ikd->iqk', head_queries, key_tiles, preferred_element_typ...  147 us
    ppermute x2, waiting for transfers between devices, with_halo(): before = lax.ppermute(last, axis, up)  147 us
    reduce_sum x12, other arithmetic, one_head(): totals = jnp.sum(weights, axis=2, keepdims=True)  101 us
    dot_general x12, matrix products, one_head(): jnp.einsum('iqk,ikd->iqd', weights.astype(jnp.bfloat16), value_tiles, pre...  100 us
    all_to_all x1, waiting for transfers between devices, on_device(): lax.all_to_all(fetch_tiles(kv_heads, lax.all_to_all(wanted_table, 'wa', s...  86.4 us
    concatenate x1, other arithmetic, with_halo(): array = jnp.concatenate([before, array, after], axis=dim)  42.5 us
    another operation x12, local copies, waits for them, and re-layouts, one_head(): jnp.stack([head_kv[row_step:row_step + tile_rows] for row_step in range(3...  35.2 us
  transfers between devices with their start and end apart: 6, of which 3 were waited for; matrix products, arithmetic and copies ran while one was open for 3% of the time, Pallas kernels for 0%

commit v1 on v0

v1 whole, which is shorter than its diff:
```python
import functools

import jax
import jax.numpy as jnp
from jax import lax
from jax.experimental import pallas as pl
from jax.experimental.pallas import tpu as pltpu
from jax.sharding import PartitionSpec as P

HEADS = 12
HD = 128
TILE = 384
TT = 3
FAR = 2
NEG = -1e30
SCALE2 = 1.4426950408889634 / HD**0.5
VMEM = 48 * 2**20


def pad8(n):
    return -(-n // 8) * 8


def attention(q, keys, values):
    scores = [
        lax.dot_general(q, k, (((1,), (1,)), ((), ())), preferred_element_type=jnp.float32)
        for k in keys
    ]
    peak = functools.reduce(jnp.maximum, [jnp.max(s, axis=1, keepdims=True) for s in scores])
    weights = [jnp.exp2((s - peak) * SCALE2) for s in scores]
    total = functools.reduce(jnp.add, [jnp.sum(w, axis=1, keepdims=True) for w in weights])
    summed = functools.reduce(
        jnp.add,
        [
            jnp.dot(w.astype(jnp.bfloat16), v, preferred_element_type=jnp.float32)
            for w, v in zip(weights, values)
        ],
    )
    return summed, peak, total


def window_kernel(jobs, n_q, n_kv, nh, flags, *refs):
    q_refs = refs[:n_q]
    kv_refs = refs[n_q : n_q + n_kv]
    outs = refs[n_q + n_kv : n_q + n_kv + 2 * len(jobs)]
    logs = refs[n_q + n_kv + 2 * len(jobs) :]
    head = pl.program_id(0)
    lane = lax.broadcasted_iota(jnp.int32, (TILE, HD), 1)
    for number, (qi, kvs, flag) in enumerate(jobs):
        o_ref, lse_ref, log_ref = outs[2 * number], outs[2 * number + 1], logs[number]

        @pl.when(flags[flag] != 0)
        def _(qi=qi, kvs=kvs, o_ref=o_ref, lse_ref=lse_ref, log_ref=log_ref):
            keys = [kv_refs[i][t, 0] for i in kvs for t in range(TT)]
            values = [kv_refs[i][t, 1] for i in kvs for t in range(TT)]
            summed, peak, total = attention(q_refs[qi][...], keys, values)
            o_ref[...] = (summed / total).astype(o_ref.dtype)
            log_ref[...] = jnp.where(lane == head, peak * SCALE2 + jnp.log2(total), log_ref[...])

            @pl.when(head == nh - 1)
            def _():
                lse_ref[...] = log_ref[...].T[: lse_ref.shape[0]]


def window(name, flags, qs, kvs, jobs, h0, nh, q_base, out_types):
    rows = pad8(nh)
    specs = [pl.BlockSpec(memory_space=pltpu.SMEM)]
    specs += [
        pl.BlockSpec((TILE, HD), functools.partial(lambda h, d: (0, h + d), d=h0 - b)) for b in q_base
    ]
    specs += [pl.BlockSpec((TT, 2, TILE, HD), lambda h: (0, 0, 0, h + h0)) for _ in kvs]
    out_specs, out_shape = [], []
    for t in out_types:
        out_specs += [
            pl.BlockSpec((TILE, HD), lambda h: (0, h)),
            pl.BlockSpec((rows, TILE), lambda h: (0, 0)),
        ]
        out_shape += [
            jax.ShapeDtypeStruct((TILE, nh * HD), t),
            jax.ShapeDtypeStruct((rows, TILE), jnp.float32),
        ]
    pairs = sum(len(j[1]) for j in jobs) * TT * nh
    res = pl.pallas_call(
        functools.partial(window_kernel, jobs, len(qs), len(kvs), nh),
        grid=(nh,),
        in_specs=specs,
        out_specs=out_specs,
        out_shape=out_shape,
        scratch_shapes=[pltpu.VMEM((TILE, HD), jnp.float32) for _ in jobs],
        compiler_params=pltpu.CompilerParams(vmem_limit_bytes=VMEM),
        cost_estimate=pl.CostEstimate(
            flops=pairs * TILE * TILE * HD * 4 * 3,
            bytes_accessed=len(kvs) * nh * TT * 2 * TILE * HD * 2,
            transcendentals=pairs * TILE * TILE,
        ),
        name=name,
    )(flags, *qs, *kvs)
    return [(res[2 * i], res[2 * i + 1]) for i in range(len(jobs))]


def column(lse_ref, head):
    row = lse_ref[pl.ds(head, 1), :]
    return jnp.broadcast_to(row, (HD, TILE)).T


def merge_parts(parts):
    top = functools.reduce(jnp.maximum, [p[1] for p in parts])
    scales = [jnp.exp2(p[1] - top) for p in parts]
    total = functools.reduce(jnp.add, scales)
    summed = functools.reduce(
        jnp.add, [p[0].astype(jnp.float32) * s for p, s in zip(parts, scales)]
    )
    return summed, top, total


def merge_kernel(part_flags, nh, flags, *refs):
    n = len(part_flags)
    o_ref, lse_ref, log_ref = refs[2 * n :]
    head = pl.program_id(0)
    lane = lax.broadcasted_iota(jnp.int32, (TILE, HD), 1)
    parts = [
        (refs[2 * i][...], jnp.where(flags[f] != 0, column(refs[2 * i + 1], head), NEG))
        for i, f in enumerate(part_flags)
    ]
    summed, top, total = merge_parts(parts)
    o_ref[...] = (summed / total).astype(o_ref.dtype)
    log_ref[...] = jnp.where(lane == head, top + jnp.log2(total), log_ref[...])

    @pl.when(head == nh - 1)
    def _():
        lse_ref[...] = log_ref[...].T[: lse_ref.shape[0]]


def merge(name, flags, parts, part_flags, nh):
    rows = pad8(nh)
    o_spec = pl.BlockSpec((TILE, HD), lambda h: (0, h))
    l_spec = pl.BlockSpec((rows, TILE), lambda h: (0, 0))
    return pl.pallas_call(
        functools.partial(merge_kernel, part_flags, nh),
        grid=(nh,),
        in_specs=[pl.BlockSpec(memory_space=pltpu.SMEM)] + [o_spec, l_spec] * len(parts),
        out_specs=[o_spec, l_spec],
        out_shape=[
            jax.ShapeDtypeStruct((TILE, nh * HD), jnp.bfloat16),
            jax.ShapeDtypeStruct((rows, TILE), jnp.float32),
        ],
        scratch_shapes=[pltpu.VMEM((TILE, HD), jnp.float32)],
        compiler_params=pltpu.CompilerParams(vmem_limit_bytes=VMEM),
        cost_estimate=pl.CostEstimate(
            flops=TILE * HD * nh * 16, bytes_accessed=TILE * HD * nh * 12, transcendentals=0
        ),
        name=name,
    )(flags, *[a for p in parts for a in p])


def final_kernel(part_specs, n_tiles, groups, flags, places, q_ref, *refs):
    n_arrays = sum(2 * (groups if cut else 1) for _, cut in part_specs)
    arrays, tiles = refs[:n_arrays], refs[n_arrays : n_arrays + n_tiles]
    out_ref, buffer, sems = refs[n_arrays + n_tiles :]
    head = pl.program_id(0)
    per = HEADS // groups

    @pl.when(head == 0)
    def _():
        @pl.loop(0, HEADS * FAR)
        def _(i):
            cols = pl.ds(pl.multiple_of(i // FAR * HD, HD), HD)
            for d, tile in enumerate(tiles):

                @pl.when(places[i] == d)
                def _(tile=tile):
                    pltpu.make_async_copy(
                        tile.at[:, :, cols], buffer.at[i], sems.at[i]
                    ).start()

    for f in range(FAR):
        i = head * FAR + f
        pltpu.make_async_copy(buffer.at[i], buffer.at[i], sems.at[i]).wait()
    keys = [buffer[head * FAR + f, 0] for f in range(FAR)]
    values = [buffer[head * FAR + f, 1] for f in range(FAR)]
    summed, peak, total = attention(q_ref[...], keys, values)

    def finish(group):
        parts = [(summed / total, jnp.broadcast_to(peak * SCALE2 + jnp.log2(total), (TILE, HD)))]
        at = 0
        for flag, cut in part_specs:
            pick = at + (2 * group if cut else 0)
            at += 2 * (groups if cut else 1)
            log = column(arrays[pick + 1], head - group * per if cut else head)
            parts.append((arrays[pick][...], jnp.where(flags[flag] != 0, log, NEG)))
        merged, _, scale = merge_parts(parts)
        out_ref[...] = (merged / scale).astype(out_ref.dtype)

    for group in range(groups):

        @pl.when(head // per == group)
        def _(group=group):
            finish(group)


def final(flags, places, q, parts, tiles, groups):
    per = HEADS // groups
    specs, arrays, part_specs = [], [], []
    for flag, pairs in parts:
        cut = len(pairs) > 1 or groups == 1
        part_specs.append((flag, cut))
        for group, (o, lse) in enumerate(pairs):
            low = group * per if cut else 0
            high = per - 1 if cut else HEADS - 1
            specs += [
                pl.BlockSpec(
                    (TILE, HD),
                    functools.partial(
                        lambda h, low, high: (0, jnp.clip(h - low, 0, high)), low=low, high=high
                    ),
                ),
                pl.BlockSpec(lse.shape, lambda h: (0, 0)),
            ]
            arrays += [o, lse]
    block = pl.BlockSpec((TILE, HD), lambda h: (0, h))
    return pl.pallas_call(
        functools.partial(final_kernel, part_specs, len(tiles), groups),
        grid=(HEADS,),
        in_specs=[pl.BlockSpec(memory_space=pltpu.SMEM)] * 2
        + [block]
        + specs
        + [pl.BlockSpec(memory_space=pl.ANY)] * len(tiles),
        out_specs=block,
        out_shape=jax.ShapeDtypeStruct((TILE, HEADS * HD), jnp.bfloat16),
        scratch_shapes=[
            pltpu.VMEM((HEADS * FAR, 2, TILE, HD), jnp.bfloat16),
            pltpu.SemaphoreType.DMA((HEADS * FAR,)),
        ],
        compiler_params=pltpu.CompilerParams(vmem_limit_bytes=VMEM),
        cost_estimate=pl.CostEstimate(
            flops=HEADS * FAR * TILE * TILE * HD * 4 * 3,
            bytes_accessed=HEADS * FAR * 2 * TILE * HD * 2,
            transcendentals=HEADS * FAR * TILE * TILE,
        ),
        name="far_and_merge",
    )(flags, places, q, *arrays, *tiles)


def send(value, axis, perm):
    return jax.tree.map(lambda a: lax.ppermute(a, axis, perm), value)


def on_device(queries, keys_values, far_offsets):
    width, height = lax.axis_size("wa"), lax.axis_size("ha")
    col, row = lax.axis_index("wa"), lax.axis_index("ha")
    groups = 2
    per = HEADS // groups
    up = [(i, i + 1) for i in range(height - 1)]
    down = [(j, i) for i, j in up]
    mate = [(i, i ^ 1) for i in range(width)]
    across = [(i, i + 1) for i in range(1, width - 1, 2)]
    across = across + [(j, i) for i, j in across]

    q = queries.reshape(TILE, HEADS * HD)
    kv = keys_values.reshape(TT, 2, TILE, HEADS * HD)

    lo, hi = row > 0, row < height - 1
    side = (col > 0) & (col < width - 1)
    flags = jnp.stack([row >= 0, lo, hi, side, side & lo, side & hi]).astype(jnp.int32)
    owners = (col + 1 + far_offsets.reshape(-1)) % width
    places = (owners ^ col).astype(jnp.int32)

    kv_mate = send(kv, "wa", mate)
    q_lo = send(q, "ha", up)
    q_hi = send(q, "ha", down)
    q_side = send(q, "wa", across)
    qs_lo = send(q_side, "ha", up)
    qs_hi = send(q_side, "ha", down)

    tiles = {0: kv[1]}
    bit = 2
    while bit < width:
        hop = [(i, i ^ bit) for i in range(width)]
        for have in sorted(tiles):
            tiles[have | bit] = send(tiles[have], "wa", hop)
        bit *= 2
    for have in sorted(tiles):
        tiles[have | 1] = kv_mate[1] if have == 0 else send(tiles[have], "wa", mate)
    tiles = [tiles[d] for d in range(width)]

    bf, f32 = jnp.bfloat16, jnp.float32
    (own_own,) = window("own", flags, [q], [kv], [(0, (0,), 0)], 0, HEADS, [0], [f32])
    (own_mate,) = window("mate", flags, [q], [kv_mate], [(0, (0,), 0)], 0, HEADS, [0], [f32])
    from_lo, from_hi, side_parts = [], [], []
    for g in range(groups):
        o_lo, o_hi = window(
            "rows", flags, [q_lo, q_hi], [kv, kv_mate],
            [(0, (0, 1), 1), (1, (0, 1), 2)], g * per, per, [0, 0], [bf, bf],
        )
        from_lo.append(send(o_hi, "ha", up))
        from_hi.append(send(o_lo, "ha", down))
    for g in range(groups):
        s_lo, s_hi, s_own = window(
            "side", flags, [qs_lo, qs_hi, q_side], [kv],
            [(0, (0,), 4), (1, (0,), 5), (2, (0,), 3)], g * per, per, [0, 0, 0], [bf, bf, f32],
        )
        s_from_lo = send(s_hi, "ha", up)
        s_from_hi = send(s_lo, "ha", down)
        merged = merge("side_merge", flags, [s_own, s_from_lo, s_from_hi], [3, 4, 5], per)
        side_parts.append(send(tuple(merged), "wa", across))
    out = final(
        flags, places, q,
        [(0, [own_own]), (0, [own_mate]), (1, from_lo), (2, from_hi), (3, side_parts)],
        tiles, groups,
    )
    return out.reshape(queries.shape)


def solution(mesh):
    placed = (
        P("ha", "wa", None, None),
        P("ha", "wa", None, None, None, None),
        P("wa", "ha", None, None),
    )
    return jax.shard_map(
        on_device, mesh=mesh, in_specs=placed, out_specs=P("ha", "wa", None, None), check_vma=False
    )
```

time: 1240 us -> 358 us (0.29)
  waiting for transfers between devices: 669 us -> 140 us
  matrix products: 248 us -> 0 us
  other arithmetic: 153 us -> 1.88 us
  Pallas kernels: 0 us -> 103 us
  local copies, waits for them, and re-layouts: 124 us -> 21.5 us
  starting transfers between devices: 30.3 us -> 88.2 us
    all_to_all x2 -> x0, waiting for transfers between devices: 522 us -> none  [the longest x1 435 us: on_device(): lax.all_to_all(wanted_table, 'wa', split_axis=0, concat_axis=0, tiled=True)]
    dot_general x24 -> x0, matrix products: 248 us -> none  [the longest x12 147 us: one_head(): jnp.einsum('iqd,ikd->iqk', head_queries, key_tiles, preferred_element_typ...]
    pallas_call x0 -> x9, Pallas kernels: none -> 103 us  [the longest x6 75.3 us: window(): pl.pallas_call(functools.partial(window_kernel, jobs, len(qs), len(kvs),...]
    reduce_sum x14 -> x0, other arithmetic: 101 us -> none  [the longest x12 101 us: one_head(): totals = jnp.sum(weights, axis=2, keepdims=True)]
    ppermute x4 -> x32, starting transfers between devices: 14.1 us -> 88.2 us  [send(): return jax.tree.map(lambda a: lax.ppermute(a, axis, perm), value)]
    concatenate x3 -> x0, other arithmetic: 42.6 us -> none  [the longest x1 42.5 us: with_halo(): array = jnp.concatenate([before, array, after], axis=dim)]
    another operation x13 -> x1, local copies, waits for them, and re-layouts: 38.2 us -> 0.11 us  [on_device(): jnp.stack([row >= 0, lo, hi, side, side & lo, side & hi]).astype(jnp.int32)]
    slice x25 -> x0, local copies, waits for them, and re-layouts: 24 us -> none  [the longest x12 21.9 us: one_head(): window[:, :, :, :, 0].reshape(tile_rows, 9 * TT * TILE, HD)]
  transfers between devices with their start and end apart: 6 -> 32, of which waited for: 3 -> 10; matrix products, arithmetic and copies ran while one was open for 3% -> 3% of each run, Pallas kernels for 0% -> 23%
where the time goes in v1:
time: 358 us; the launch traced here: 356 us
  waiting for transfers between devices  140 us (39%)
  Pallas kernels  103 us (29%)
  starting transfers between devices  88.2 us (25%)
  local copies, waits for them, and re-layouts  21.5 us (6%)
    ppermute x32, waiting for transfers between devices, send(): return jax.tree.map(lambda a: lax.ppermute(a, axis, perm), value)  140 us
    ppermute x32, starting transfers between devices, send(): return jax.tree.map(lambda a: lax.ppermute(a, axis, perm), value)  88.2 us
    pallas_call x6, Pallas kernels, window(): pl.pallas_call(functools.partial(window_kernel, jobs, len(qs), len(kvs),...  75.3 us
    pallas_call x1, Pallas kernels, final(): pl.pallas_call(functools.partial(final_kernel, part_specs, len(tiles), gr...  19.8 us
    unnamed x54, local copies, waits for them, and re-layouts  12.2 us
    pallas_call x2, Pallas kernels, merge(): pl.pallas_call(functools.partial(merge_kernel, part_flags, nh), grid=(nh,...  7.74 us
  transfers between devices with their start and end apart: 32, of which 10 were waited for; matrix products, arithmetic and copies ran while one was open for 3% of the time, Pallas kernels for 23%

profile of v1, /device:TPU:3, one launch (start us, length us, event | category | flops | bytes accessed | tf_op | source)
XLA Modules:
  0.0 355.7 jit_solution(6542064194861867442)
XLA Ops:
  3.7 3.3 slice_bitcast_fusion.1.refs_16_
  7.2 24.6 %collective-permute-done.11.refs_2_ = bf16[384,1536]{1,0:T(8,128)(2,1)S(1)} collective-permute-done((bf16[384,1536]{1,0:T(8,128)(2,1)}, bf16[384,1536]{1,0:T(8,128)(2,1)S(1)}, u32[]{:S(2)}, u32[]{:S(2)}) %collective-permute-start.11) | collective-permute-done | bytes 1179680 | tf_op jit(solution)/shard_map/ppermute | solution.py:245
  31.9 3.3 collective-permute-start.12
  36.6 22.5 %collective-permute-done.12.refs_0_ = bf16[384,1536]{1,0:T(8,128)(2,1)S(1)} collective-permute-done((bf16[384,1536]{1,0:T(8,128)(2,1)S(1)}, bf16[384,1536]{1,0:T(8,128)(2,1)S(1)}, u32[]{:S(2)}, u32[]{:S(2)}) %collective-permute-start.12) | collective-permute-done | bytes 1179680 | tf_op jit(solution)/shard_map/ppermute | solution.py:245
  59.0 4.2 %collective-permute-done.13.refs_1_ = bf16[384,1536]{1,0:T(8,128)(2,1)S(1)} collective-permute-done((bf16[384,1536]{1,0:T(8,128)(2,1)S(1)}, bf16[384,1536]{1,0:T(8,128)(2,1)S(1)}, u32[]{:S(2)}, u32[]{:S(2)}) %collective-permute-start.13) | collective-permute-done | bytes 1179680 | tf_op jit(solution)/shard_map/ppermute | solution.py:245
  65.5 13.0 %side.3 = (bf16[384,768]{1,0:T(8,128)(2,1)S(1)}, f32[8,384]{1,0:T(8,128)S(1)}, bf16[384,768]{1,0:T(8,128)(2,1)S(1)}, f32[8,384]{1,0:T(8,128)S(1)}, f32[384,768]{1,0:T(8,128)S(1)}, /*index=5*/f32[8,384]{1,0:T(8,128)S(1)}) custom-call(s32[6]{0:T(128)S(1)} %convert_element_type.3.flags, bf16[384,1536]{1,0:T(8,128)(2,1)S(1)} %collective-permute-done.12.refs_0_, ...), custom_call_target="tpu_custom_call" | custom-call | flops 12230590464 | bytes 3538944 | tf_op jit(solution)/shard_map/side/pallas_call | solution.py:83
  78.5 8.7 %collective-permute-start.20 = (bf16[384,768]{1,0:T(8,128)(2,1)S(1)}, bf16[384,768]{1,0:T(8,128)(2,1)S(1)}, u32[]{:S(2)}, u32[]{:S(2)}) collective-permute-start(bf16[384,768]{1,0:T(8,128)(2,1)S(1)} %get-tuple-element.55), channel_id=1, source_target_pairs={{0,8},{8,16},{16,24},{1,9},{9,17},{17,25},{2,10},{10,18},{18,26},{... | collective-permute-start | bytes 1769480 | tf_op jit(solution)/shard_map/ppermute | solution.py:245
  88.5 4.0 %collective-permute-start.21 = (f32[8,384]{1,0:T(8,128)S(1)}, f32[8,384]{1,0:T(8,128)S(1)}, u32[]{:S(2)}, u32[]{:S(2)}) collective-permute-start(f32[8,384]{1,0:T(8,128)S(1)} %get-tuple-element.56), channel_id=1, source_target_pairs={{0,8},{8,16},{16,24},{1,9},{9,17},{17,25},{2,10},{10,18},{18,26},{... | collective-permute-start | bytes 36872 | tf_op jit(solution)/shard_map/ppermute | solution.py:245
  97.8 13.5 %side.2 = (bf16[384,768]{1,0:T(8,128)(2,1)}, f32[8,384]{1,0:T(8,128)S(1)}, bf16[384,768]{1,0:T(8,128)(2,1)}, f32[8,384]{1,0:T(8,128)S(1)}, f32[384,768]{1,0:T(8,128)S(1)}, /*index=5*/f32[8,384]{1,0:T(8,128)S(1)}) custom-call(s32[6]{0:T(128)S(1)} %convert_element_type.3.flags, bf16[384,1536]{1,0:T(8,128)(2,1)S(1)} %copy-done.20, ...), custom_call_target="tpu_custom_call" | custom-call | flops 12230590464 | bytes 3538944 | tf_op jit(solution)/shard_map/side/pallas_call | solution.py:83
  112.4 9.5 %collective-permute-start.15 = (f32[8,384]{1,0:T(8,128)S(1)}, f32[8,384]{1,0:T(8,128)S(1)}, u32[]{:S(2)}, u32[]{:S(2)}) collective-permute-start(f32[8,384]{1,0:T(8,128)S(1)} %get-tuple-element.48), channel_id=1, source_target_pairs={{0,8},{8,16},{16,24},{1,9},{9,17},{17,25},{2,10},{10,18},{18,26},{... | collective-permute-start | bytes 36872 | tf_op jit(solution)/shard_map/ppermute | solution.py:245
  128.4 4.0 %collective-permute-start.14 = (bf16[384,768]{1,0:T(8,128)(2,1)}, bf16[384,768]{1,0:T(8,128)(2,1)}, u32[]{:S(2)}, u32[]{:S(2)}) collective-permute-start(bf16[384,768]{1,0:T(8,128)(2,1)} %get-tuple-element.47), channel_id=1, source_target_pairs={{0,8},{8,16},{16,24},{1,9},{9,17},{17,25},{2,10},{10,18},{18,26},{... | collective-permute-start | bytes 1769480 | tf_op jit(solution)/shard_map/ppermute | solution.py:245
  134.6 8.3 %collective-permute-done.14.refs_2_ = bf16[384,768]{1,0:T(8,128)(2,1)} collective-permute-done((bf16[384,768]{1,0:T(8,128)(2,1)}, bf16[384,768]{1,0:T(8,128)(2,1)}, u32[]{:S(2)}, u32[]{:S(2)}) %collective-permute-start.14) | collective-permute-done | bytes 589856 | tf_op jit(solution)/shard_map/ppermute | solution.py:245
  142.9 5.1 %collective-permute-start.1 = (bf16[384,1536]{1,0:T(8,128)(2,1)S(1)}, bf16[384,1536]{1,0:T(8,128)(2,1)}, u32[]{:S(2)}, u32[]{:S(2)}) collective-permute-start(bf16[384,1536]{1,0:T(8,128)(2,1)S(1)} %bitcast.14), channel_id=1, source_target_pairs={{0,8},{8,16},{16,24},{1,9},{9,17},{17,25},{2,10},{10,18},{18,26},{... | collective-permute-start | bytes 3538952 | tf_op jit(solution)/shard_map/ppermute | solution.py:245
  154.2 13.4 %own.1 = (f32[384,1536]{1,0:T(8,128)S(1)}, f32[16,384]{1,0:T(8,128)S(1)}) custom-call(s32[6]{0:T(128)S(1)} %convert_element_type.3.flags, bf16[384,1536]{1,0:T(8,128)(2,1)S(1)} %bitcast.16, bf16[3,2,384,1536]{3,2,1,0:T(8,128)(2,1)} %bitcast.22), custom_call_target="tpu_custom_call" | custom-call | flops 8153726976 | bytes 7077888 | tf_op jit(solution)/shard_map/own/pallas_call | solution.py:83
  172.3 4.6 %side_merge.2 = (bf16[384,768]{1,0:T(8,128)(2,1)S(1)}, f32[8,384]{1,0:T(8,128)S(1)}) custom-call(s32[6]{0:T(128)S(1)} %convert_element_type.3.flags, f32[384,768]{1,0:T(8,128)S(1)} %get-tuple-element.45.refs_0_, f32[8,384]{1,0:T(8,128)S(1)} %copy-done.12, bf16[384,768]{1,0:T(8,128)(2,1)} %collective-permute-done.14.refs_2_, f32[8,384]{1,0:T(8,128)S(1)} %copy-done.14, ...), custom_call_target="tpu_custom_call" | custom-call | flops 4718592 | bytes 3538944 | tf_op jit(solution)/shard_map/side_merge/pallas_call | solution.py:138
  182.9 44.9 %collective-permute-done.30.refs_22_ = bf16[2,384,1536]{2,1,0:T(8,128)(2,1)} collective-permute-done((bf16[2,384,1536]{2,1,0:T(8,128)(2,1)}, bf16[2,384,1536]{2,1,0:T(8,128)(2,1)}, u32[]{:S(2)}, u32[]{:S(2)}) %collective-permute-start.30) | collective-permute-done | bytes 2359328 | tf_op jit(solution)/shard_map/ppermute | solution.py:245
  231.3 11.0 %rows.2 = (bf16[384,768]{1,0:T(8,128)(2,1)S(1)}, f32[8,384]{1,0:T(8,128)S(1)}, bf16[384,768]{1,0:T(8,128)(2,1)S(1)}, f32[8,384]{1,0:T(8,128)S(1)}) custom-call(s32[6]{0:T(128)S(1)} %convert_element_type.3.flags, bf16[384,1536]{1,0:T(8,128)(2,1)} %collective-permute-done.1.refs_0_, bf16[384,1536]{1,0:T(8,128)(2,1)} %collective-permute-done.2.refs_1_, ...), custom_call_target="tpu_custom_call" | custom-call | flops 16307453952 | bytes 7077888 | tf_op jit(solution)/shard_map/rows/pallas_call | solution.py:83
  248.8 11.1 %rows.3 = (bf16[384,768]{1,0:T(8,128)(2,1)S(1)}, f32[8,384]{1,0:T(8,128)S(1)}, bf16[384,768]{1,0:T(8,128)(2,1)S(1)}, f32[8,384]{1,0:T(8,128)S(1)}) custom-call(s32[6]{0:T(128)S(1)} %convert_element_type.3.flags, bf16[384,1536]{1,0:T(8,128)(2,1)} %collective-permute-done.1.refs_0_, bf16[384,1536]{1,0:T(8,128)(2,1)} %collective-permute-done.2.refs_1_, ...), custom_call_target="tpu_custom_call" | custom-call | flops 16307453952 | bytes 7077888 | tf_op jit(solution)/shard_map/rows/pallas_call | solution.py:83
  262.1 9.8 %collective-permute-done.18.refs_12_ = bf16[384,768]{1,0:T(8,128)(2,1)S(1)} collective-permute-done((bf16[384,768]{1,0:T(8,128)(2,1)S(1)}, bf16[384,768]{1,0:T(8,128)(2,1)S(1)}, u32[]{:S(2)}, u32[]{:S(2)}) %collective-permute-start.18) | collective-permute-done | bytes 589856 | tf_op jit(solution)/shard_map/ppermute | solution.py:245
  271.9 12.8 %collective-permute-start.4 = (f32[8,384]{1,0:T(8,128)S(1)}, f32[8,384]{1,0:T(8,128)S(1)}, u32[]{:S(2)}, u32[]{:S(2)}) collective-permute-start(f32[8,384]{1,0:T(8,128)S(1)} %get-tuple-element.38), channel_id=1, source_target_pairs={{0,8},{8,16},{16,24},{1,9},{9,17},{17,25},{2,10},{10,18},{18,26},{... | collective-permute-start | bytes 36872 | tf_op jit(solution)/shard_map/ppermute | solution.py:245
  288.0 13.4 %mate.1 = (f32[384,1536]{1,0:T(8,128)S(1)}, f32[16,384]{1,0:T(8,128)S(1)}) custom-call(s32[6]{0:T(128)S(1)} %convert_element_type.3.flags, bf16[384,1536]{1,0:T(8,128)(2,1)S(1)} %bitcast.17, bf16[3,2,384,1536]{3,2,1,0:T(8,128)(2,1)} %collective-permute-done.refs_1_.refs_3_), custom_call_target="tpu_custom_call" | custom-call | flops 8153726976 | bytes 7077888 | tf_op jit(solution)/shard_map/mate/pallas_call | solution.py:83
  310.1 3.2 slice_bitcast_fusion.refs_17_
  313.3 22.3 %collective-permute-done.8.refs_9_ = f32[8,384]{1,0:T(8,128)S(1)} collective-permute-done((f32[8,384]{1,0:T(8,128)S(1)}, f32[8,384]{1,0:T(8,128)S(1)}, u32[]{:S(2)}, u32[]{:S(2)}) %collective-permute-start.8) | collective-permute-done | bytes 12320 | tf_op jit(solution)/shard_map/ppermute | solution.py:245
  335.7 19.8 %far_and_merge.1 = bf16[384,1536]{1,0:T(8,128)(2,1)} custom-call(s32[6]{0:T(128)S(1)} %convert_element_type.3.flags, s32[24]{0:T(128)S(1)} %fusion.places, bf16[384,1536]{1,0:T(8,128)(2,1)S(1)} %bitcast.18, f32[384,1536]{1,0:T(8,128)} %copy-done, f32[16,384]{1,0:T(8,128)S(1)} %get-tuple-element.34.refs_1_, f32[384,1536]{1,0:T(8,128)} %copy-done.1, ...), custom_call_target="tpu_custom_call" | custom-call | flops 5435817984 | bytes 4718592 | tf_op jit(solution)/shard_map/far_and_merge/pallas_call | solution.py:221
  (111 shorter events, 64.7 us)
Async XLA Ops:
  0.0 229.9 %collective-permute-start = (bf16[3,2,384,1536]{3,2,1,0:T(8,128)(2,1)}, bf16[3,2,384,1536]{3,2,1,0:T(8,128)(2,1)}, u32[]{:S(2)}, u32[]{:S(2)}) collective-permute-start(bf16[3,2,384,1536]{3,2,1,0:T(8,128)(2,1)} %bitcast.19), channel_id=1, source_target_pairs={{0,1},{1,0},{2,3},{3,2},{4,5},{5,4},{6,7},{7,6},{8,9},{9,8},{10,11... | collective-permute-start | bytes 21233672 | tf_op jit(solution)/shard_map/ppermute | solution.py:245
  0.7 31.2 %collective-permute-start.11 = (bf16[384,1536]{1,0:T(8,128)(2,1)}, bf16[384,1536]{1,0:T(8,128)(2,1)S(1)}, u32[]{:S(2)}, u32[]{:S(2)}) collective-permute-start(bf16[384,1536]{1,0:T(8,128)(2,1)} %bitcast.13), channel_id=1, source_target_pairs={{1,2},{3,4},{5,6},{2,1},{4,3},{6,5},{9,10},{11,12},{13,14},{10,9},... | collective-permute-start | bytes 3538952 | tf_op jit(solution)/shard_map/ppermute | solution.py:245
  7.0 85.5 %collective-permute-start.26 = (bf16[2,384,1536]{2,1,0:T(8,128)(2,1)}, bf16[2,384,1536]{2,1,0:T(8,128)(2,1)}, u32[]{:S(2)}, u32[]{:S(2)}) collective-permute-start(bf16[2,384,1536]{2,1,0:T(8,128)(2,1)} %slice_bitcast_fusion.1.refs_16_), channel_id=1, source_target_pairs={{0,2},{1,3},{2,0},{3,1},{4,6},{5,7},{6,4},{7,5},{8,10},{9,11},{10,... | collective-permute-start | bytes 7077896 | tf_op jit(solution)/shard_map/ppermute | solution.py:245
  31.9 27.2 %collective-permute-start.12 = (bf16[384,1536]{1,0:T(8,128)(2,1)S(1)}, bf16[384,1536]{1,0:T(8,128)(2,1)S(1)}, u32[]{:S(2)}, u32[]{:S(2)}) collective-permute-start(bf16[384,1536]{1,0:T(8,128)(2,1)S(1)} %collective-permute-done.11.refs_2_), channel_id=1, source_target_pairs={{0,8},{8,16},{16,24},{1,9},{9,17},{17,25},{2,10},{10,18},{18,26},{... | collective-permute-start | bytes 3538952 | tf_op jit(solution)/shard_map/ppermute | solution.py:245
  35.2 28.1 %collective-permute-start.13 = (bf16[384,1536]{1,0:T(8,128)(2,1)S(1)}, bf16[384,1536]{1,0:T(8,128)(2,1)S(1)}, u32[]{:S(2)}, u32[]{:S(2)}) collective-permute-start(bf16[384,1536]{1,0:T(8,128)(2,1)S(1)} %collective-permute-done.11.refs_2_), channel_id=1, source_target_pairs={{8,0},{16,8},{24,16},{9,1},{17,9},{25,17},{10,2},{18,10},{26,18},{... | collective-permute-start | bytes 3538952 | tf_op jit(solution)/shard_map/ppermute | solution.py:245
  78.5 49.1 %collective-permute-start.20 = (bf16[384,768]{1,0:T(8,128)(2,1)S(1)}, bf16[384,768]{1,0:T(8,128)(2,1)S(1)}, u32[]{:S(2)}, u32[]{:S(2)}) collective-permute-start(bf16[384,768]{1,0:T(8,128)(2,1)S(1)} %get-tuple-element.55), channel_id=1, source_target_pairs={{0,8},{8,16},{16,24},{1,9},{9,17},{17,25},{2,10},{10,18},{18,26},{... | collective-permute-start | bytes 1769480 | tf_op jit(solution)/shard_map/ppermute | solution.py:245
  87.2 45.3 %collective-permute-start.22 = (bf16[384,768]{1,0:T(8,128)(2,1)S(1)}, bf16[384,768]{1,0:T(8,128)(2,1)S(1)}, u32[]{:S(2)}, u32[]{:S(2)}) collective-permute-start(bf16[384,768]{1,0:T(8,128)(2,1)S(1)} %get-tuple-element.57), channel_id=1, source_target_pairs={{8,0},{16,8},{24,16},{9,1},{17,9},{25,17},{10,2},{18,10},{26,18},{... | collective-permute-start | bytes 1769480 | tf_op jit(solution)/shard_map/ppermute | solution.py:245
  92.5 29.4 %collective-permute-start.23 = (f32[8,384]{1,0:T(8,128)S(1)}, f32[8,384]{1,0:T(8,128)S(1)}, u32[]{:S(2)}, u32[]{:S(2)}) collective-permute-start(f32[8,384]{1,0:T(8,128)S(1)} %get-tuple-element.58), channel_id=1, source_target_pairs={{8,0},{16,8},{24,16},{9,1},{17,9},{25,17},{10,2},{18,10},{26,18},{... | collective-permute-start | bytes 36872 | tf_op jit(solution)/shard_map/ppermute | solution.py:245
  124.5 55.4 %collective-permute-start.28 = (bf16[2,384,1536]{2,1,0:T(8,128)(2,1)}, bf16[2,384,1536]{2,1,0:T(8,128)(2,1)}, u32[]{:S(2)}, u32[]{:S(2)}) collective-permute-start(bf16[2,384,1536]{2,1,0:T(8,128)(2,1)} %slice_bitcast_fusion.1.refs_16_), channel_id=1, source_target_pairs={{0,4},{1,5},{2,6},{3,7},{4,0},{5,1},{6,2},{7,3},{8,12},{9,13},{10,... | collective-permute-start | bytes 7077896 | tf_op jit(solution)/shard_map/ppermute | solution.py:245
  127.6 100.2 %collective-permute-start.30 = (bf16[2,384,1536]{2,1,0:T(8,128)(2,1)}, bf16[2,384,1536]{2,1,0:T(8,128)(2,1)}, u32[]{:S(2)}, u32[]{:S(2)}) collective-permute-start(bf16[2,384,1536]{2,1,0:T(8,128)(2,1)} %collective-permute-done.26.refs_18_), channel_id=1, source_target_pairs={{0,4},{1,5},{2,6},{3,7},{4,0},{5,1},{6,2},{7,3},{8,12},{9,13},{10,... | collective-permute-start | bytes 7077896 | tf_op jit(solution)/shard_map/ppermute | solution.py:245
  142.9 34.0 %collective-permute-start.1 = (bf16[384,1536]{1,0:T(8,128)(2,1)S(1)}, bf16[384,1536]{1,0:T(8,128)(2,1)}, u32[]{:S(2)}, u32[]{:S(2)}) collective-permute-start(bf16[384,1536]{1,0:T(8,128)(2,1)S(1)} %bitcast.14), channel_id=1, source_target_pairs={{0,8},{8,16},{16,24},{1,9},{9,17},{17,25},{2,10},{10,18},{18,26},{... | collective-permute-start | bytes 3538952 | tf_op jit(solution)/shard_map/ppermute | solution.py:245
  148.4 31.5 %collective-permute-start.2 = (bf16[384,1536]{1,0:T(8,128)(2,1)S(1)}, bf16[384,1536]{1,0:T(8,128)(2,1)}, u32[]{:S(2)}, u32[]{:S(2)}) collective-permute-start(bf16[384,1536]{1,0:T(8,128)(2,1)S(1)} %bitcast.15), channel_id=1, source_target_pairs={{8,0},{16,8},{24,16},{9,1},{17,9},{25,17},{10,2},{18,10},{26,18},{... | collective-permute-start | bytes 3538952 | tf_op jit(solution)/shard_map/ppermute | solution.py:245
  176.9 107.8 %collective-permute-start.27 = (bf16[2,384,1536]{2,1,0:T(8,128)(2,1)}, bf16[2,384,1536]{2,1,0:T(8,128)(2,1)S(1)}, u32[]{:S(2)}, u32[]{:S(2)}) collective-permute-start(bf16[2,384,1536]{2,1,0:T(8,128)(2,1)} %collective-permute-done.26.refs_18_), channel_id=1, source_target_pairs={{0,1},{1,0},{2,3},{3,2},{4,5},{5,4},{6,7},{7,6},{8,9},{9,8},{10,11... | collective-permute-start | bytes 7077896 | tf_op jit(solution)/shard_map/ppermute | solution.py:245
  179.8 121.5 %collective-permute-start.29 = (bf16[2,384,1536]{2,1,0:T(8,128)(2,1)}, bf16[2,384,1536]{2,1,0:T(8,128)(2,1)S(1)}, u32[]{:S(2)}, u32[]{:S(2)}) collective-permute-start(bf16[2,384,1536]{2,1,0:T(8,128)(2,1)} %collective-permute-done.28.refs_20_), channel_id=1, source_target_pairs={{0,1},{1,0},{2,3},{3,2},{4,5},{5,4},{6,7},{7,6},{8,9},{9,8},{10,11... | collective-permute-start | bytes 7077896 | tf_op jit(solution)/shard_map/ppermute | solution.py:245
  179.9 62.4 %collective-permute-start.25 = (f32[8,384]{1,0:T(8,128)S(1)}, f32[8,384]{1,0:T(8,128)S(1)}, u32[]{:S(2)}, u32[]{:S(2)}) collective-permute-start(f32[8,384]{1,0:T(8,128)S(1)} %get-tuple-element.60), channel_id=1, source_target_pairs={{1,2},{3,4},{5,6},{2,1},{4,3},{6,5},{9,10},{11,12},{13,14},{10,9},... | collective-permute-start | bytes 36872 | tf_op jit(solution)/shard_map/ppermute | solution.py:245
  229.9 74.3 %collective-permute-start.31 = (bf16[2,384,1536]{2,1,0:T(8,128)(2,1)}, bf16[2,384,1536]{2,1,0:T(8,128)(2,1)S(1)}, u32[]{:S(2)}, u32[]{:S(2)}) collective-permute-start(bf16[2,384,1536]{2,1,0:T(8,128)(2,1)} %collective-permute-done.30.refs_22_), channel_id=1, source_target_pairs={{0,1},{1,0},{2,3},{3,2},{4,5},{5,4},{6,7},{7,6},{8,9},{9,8},{10,11... | collective-permute-start | bytes 7077896 | tf_op jit(solution)/shard_map/ppermute | solution.py:245
  245.6 26.3 %collective-permute-start.18 = (bf16[384,768]{1,0:T(8,128)(2,1)S(1)}, bf16[384,768]{1,0:T(8,128)(2,1)S(1)}, u32[]{:S(2)}, u32[]{:S(2)}) collective-permute-start(bf16[384,768]{1,0:T(8,128)(2,1)S(1)} %get-tuple-element.51), channel_id=1, source_target_pairs={{1,2},{3,4},{5,6},{2,1},{4,3},{6,5},{9,10},{11,12},{13,14},{10,9},... | collective-permute-start | bytes 1769480 | tf_op jit(solution)/shard_map/ppermute | solution.py:245
  260.8 45.3 %collective-permute-start.10 = (f32[8,384]{1,0:T(8,128)S(1)}, f32[8,384]{1,0:T(8,128)S(1)}, u32[]{:S(2)}, u32[]{:S(2)}) collective-permute-start(f32[8,384]{1,0:T(8,128)S(1)} %get-tuple-element.44), channel_id=1, source_target_pairs={{8,0},{16,8},{24,16},{9,1},{17,9},{25,17},{10,2},{18,10},{26,18},{... | collective-permute-start | bytes 36872 | tf_op jit(solution)/shard_map/ppermute | solution.py:245
  271.9 35.6 %collective-permute-start.4 = (f32[8,384]{1,0:T(8,128)S(1)}, f32[8,384]{1,0:T(8,128)S(1)}, u32[]{:S(2)}, u32[]{:S(2)}) collective-permute-start(f32[8,384]{1,0:T(8,128)S(1)} %get-tuple-element.38), channel_id=1, source_target_pairs={{0,8},{8,16},{16,24},{1,9},{9,17},{17,25},{2,10},{10,18},{18,26},{... | collective-permute-start | bytes 36872 | tf_op jit(solution)/shard_map/ppermute | solution.py:245
  301.4 34.3 %collective-permute-start.3 = (bf16[384,768]{1,0:T(8,128)(2,1)S(1)}, bf16[384,768]{1,0:T(8,128)(2,1)S(1)}, u32[]{:S(2)}, u32[]{:S(2)}) collective-permute-start(bf16[384,768]{1,0:T(8,128)(2,1)S(1)} %get-tuple-element.37), channel_id=1, source_target_pairs={{0,8},{8,16},{16,24},{1,9},{9,17},{17,25},{2,10},{10,18},{18,26},{... | collective-permute-start | bytes 1769480 | tf_op jit(solution)/shard_map/ppermute | solution.py:245
  304.2 31.4 %collective-permute-start.5 = (bf16[384,768]{1,0:T(8,128)(2,1)S(1)}, bf16[384,768]{1,0:T(8,128)(2,1)S(1)}, u32[]{:S(2)}, u32[]{:S(2)}) collective-permute-start(bf16[384,768]{1,0:T(8,128)(2,1)S(1)} %get-tuple-element.39), channel_id=1, source_target_pairs={{0,8},{8,16},{16,24},{1,9},{9,17},{17,25},{2,10},{10,18},{18,26},{... | collective-permute-start | bytes 1769480 | tf_op jit(solution)/shard_map/ppermute | solution.py:245
  306.2 29.5 %collective-permute-start.7 = (bf16[384,768]{1,0:T(8,128)(2,1)S(1)}, bf16[384,768]{1,0:T(8,128)(2,1)S(1)}, u32[]{:S(2)}, u32[]{:S(2)}) collective-permute-start(bf16[384,768]{1,0:T(8,128)(2,1)S(1)} %get-tuple-element.41), channel_id=1, source_target_pairs={{8,0},{16,8},{24,16},{9,1},{17,9},{25,17},{10,2},{18,10},{26,18},{... | collective-permute-start | bytes 1769480 | tf_op jit(solution)/shard_map/ppermute | solution.py:245
  307.5 28.2 %collective-permute-start.9 = (bf16[384,768]{1,0:T(8,128)(2,1)S(1)}, bf16[384,768]{1,0:T(8,128)(2,1)S(1)}, u32[]{:S(2)}, u32[]{:S(2)}) collective-permute-start(bf16[384,768]{1,0:T(8,128)(2,1)S(1)} %get-tuple-element.43), channel_id=1, source_target_pairs={{8,0},{16,8},{24,16},{9,1},{17,9},{25,17},{10,2},{18,10},{26,18},{... | collective-permute-start | bytes 1769480 | tf_op jit(solution)/shard_map/ppermute | solution.py:245
  308.8 26.9 %collective-permute-start.8 = (f32[8,384]{1,0:T(8,128)S(1)}, f32[8,384]{1,0:T(8,128)S(1)}, u32[]{:S(2)}, u32[]{:S(2)}) collective-permute-start(f32[8,384]{1,0:T(8,128)S(1)} %get-tuple-element.42), channel_id=1, source_target_pairs={{8,0},{16,8},{24,16},{9,1},{17,9},{25,17},{10,2},{18,10},{26,18},{... | collective-permute-start | bytes 36872 | tf_op jit(solution)/shard_map/ppermute | solution.py:245
  (35 other events, 398.9 us)

commit v2 on v0

v2 whole, which is shorter than its diff:
```python
import functools

import jax
import jax.numpy as jnp
from jax import lax
from jax.experimental import pallas as pl
from jax.experimental.pallas import tpu as pltpu
from jax.sharding import PartitionSpec as P

HEADS = 12
HD = 128
TILE = 384
TT = 3
FAR = 2
NEG = -1e30
SCALE2 = 1.4426950408889634 / HD**0.5
VMEM = 127 * 2**19
ROW_GROUPS = 2
SIDE_GROUPS = 2
BF, F32 = jnp.bfloat16, jnp.float32
LOG_ROWS = 16
TERMS = 3


def pipelined(units, finish):
    def scores(unit):
        return lax.dot_general(
            unit[0](), unit[1], (((1,), (1,)), ((), ())), preferred_element_type=F32
        )

    coming = scores(units[0])
    for number, unit in enumerate(units):
        s = coming
        if number + 1 < len(units):
            coming = scores(units[number + 1])
        peak = jnp.max(s, axis=1, keepdims=True)
        weights = jnp.exp2((s - peak) * SCALE2)
        total = jnp.sum(weights, axis=1, keepdims=True)
        summed = jnp.dot(weights.astype(BF), unit[2], preferred_element_type=F32)
        finish(number, summed / total, peak * SCALE2 + jnp.log2(total))


def one_hot(c, transposed_rows):
    row = lax.broadcasted_iota(jnp.int32, (LOG_ROWS, HD), 0) - c * TERMS
    lane = lax.broadcasted_iota(jnp.int32, (LOG_ROWS, HD), 1)
    hit = (row >= 0) & (row < TERMS) if transposed_rows else (row == lane) & (row >= 0) & (row < TERMS)
    return jnp.where(hit, 1.0, 0.0).astype(BF)


def write_logs(ref, cols, log):
    lane = lax.broadcasted_iota(jnp.int32, (TILE, HD), 1)
    first = log.astype(BF).astype(F32)
    second = (log - first).astype(BF).astype(F32)
    terms = jnp.where(lane == 0, first, jnp.where(lane == 1, second, log - first - second)).astype(BF)
    block = functools.reduce(
        jnp.add,
        [
            lax.dot_general(
                one_hot(c, False), terms[c * HD : (c + 1) * HD], (((1,), (1,)), ((), ())),
                preferred_element_type=F32,
            )
            for c in range(TILE // HD)
        ],
    )
    ref[TILE:, cols] = block.astype(ref.dtype)


def read_logs(ref, cols):
    block = ref[TILE:, cols].astype(BF)
    return jnp.concatenate(
        [
            lax.dot_general(
                block, one_hot(c, True), (((0,), (0,)), ((), ())), preferred_element_type=F32
            )
            for c in range(TILE // HD)
        ],
        axis=0,
    )


def lanes(i):
    return slice(i * HD, (i + 1) * HD)


def pass_flags(flags, token):
    for i in range(8):
        token[i] = flags[i]


def window_kernel(jobs, n_q, n_kv, n_after, split, heads, flags, *refs):
    refs = refs[n_after:]
    q_refs = refs[:n_q]
    kv_refs = refs[n_q : n_q + n_kv]
    outs = refs[n_q + n_kv : n_q + n_kv + len(jobs)]
    token, log_ref = refs[n_q + n_kv + len(jobs) :]
    pass_flags(flags, token)
    size = TILE // split
    units, where = [], []
    for head in range(heads):
        at = lanes(head)
        for number, (qi, kvs) in enumerate(jobs):
            keys = jnp.concatenate([kv_refs[i][t, 0, :, at] for i in kvs for t in range(TT)], axis=0)
            values = jnp.concatenate([kv_refs[i][t, 1, :, at] for i in kvs for t in range(TT)], axis=0)
            for part in range(split):
                cut = slice(part * size, (part + 1) * size)
                units.append((lambda qi=qi, cut=cut, at=at: q_refs[qi][cut, at], keys, values))
                where.append((number, cut, at, part))

    def finish(unit, out, log):
        number, cut, at, part = where[unit]
        outs[number][cut, at] = out.astype(outs[number].dtype)
        log = jnp.broadcast_to(log, (size, HD))
        if split > 1:
            log_ref[unit // split, cut, :] = log
            log = log_ref[unit // split]
        if part == split - 1:
            write_logs(outs[number], at, log)

    pipelined(units, finish)


def window(name, flags, qs, kvs, jobs, h0, nh, out_types, split, step, flops=1000, after=()):
    smem = pl.BlockSpec(memory_space=pltpu.SMEM)
    base = h0 // step
    specs = [smem] + [pl.BlockSpec(memory_space=pl.ANY) for _ in after]
    specs += [pl.BlockSpec((TILE, step * HD), lambda h: (0, h + base)) for _ in qs]
    specs += [pl.BlockSpec((TT, 2, TILE, step * HD), lambda h: (0, 0, 0, h + base)) for _ in kvs]
    rows = TILE + LOG_ROWS
    res = pl.pallas_call(
        functools.partial(window_kernel, jobs, len(qs), len(kvs), len(after), split, step),
        grid=(nh // step,),
        in_specs=specs,
        out_specs=[pl.BlockSpec((rows, step * HD), lambda h: (0, h)) for _ in jobs] + [smem],
        out_shape=[jax.ShapeDtypeStruct((rows, nh * HD), t) for t in out_types]
        + [jax.ShapeDtypeStruct(flags.shape, flags.dtype)],
        scratch_shapes=[pltpu.VMEM((len(jobs) * step, TILE, HD), F32)],
        compiler_params=pltpu.CompilerParams(vmem_limit_bytes=VMEM),
        cost_estimate=pl.CostEstimate(flops=flops, bytes_accessed=1000, transcendentals=0),
        name=name,
    )(flags, *after, *qs, *kvs)
    return res[-1], res[:-1]


def merge_parts(parts):
    top = functools.reduce(jnp.maximum, [p[1] for p in parts])
    scales = [jnp.exp2(p[1] - top) for p in parts]
    total = functools.reduce(jnp.add, scales)
    summed = functools.reduce(jnp.add, [p[0].astype(F32) * s for p, s in zip(parts, scales)])
    return summed, top, total


def merge_kernel(part_flags, heads, flags, *refs):
    n = len(part_flags)
    out, token = refs[n:]
    pass_flags(flags, token)
    for head in range(heads):
        at = lanes(head)
        parts = [
            (refs[i][:TILE, at], jnp.where(flags[f] != 0, read_logs(refs[i], at), NEG))
            for i, f in enumerate(part_flags)
        ]
        summed, top, total = merge_parts(parts)
        out[:TILE, at] = (summed / total).astype(out.dtype)
        write_logs(out, at, top + jnp.log2(total))


def merge(name, flags, parts, part_flags, nh, step):
    smem = pl.BlockSpec(memory_space=pltpu.SMEM)
    block = pl.BlockSpec((TILE + LOG_ROWS, step * HD), lambda h: (0, h))
    res = pl.pallas_call(
        functools.partial(merge_kernel, part_flags, step),
        grid=(nh // step,),
        in_specs=[smem] + [block] * len(parts),
        out_specs=[block, smem],
        out_shape=[
            jax.ShapeDtypeStruct((TILE + LOG_ROWS, nh * HD), BF),
            jax.ShapeDtypeStruct(flags.shape, flags.dtype),
        ],
        compiler_params=pltpu.CompilerParams(vmem_limit_bytes=VMEM),
        cost_estimate=pl.CostEstimate(flops=1000, bytes_accessed=1000, transcendentals=0),
        name=name,
    )(flags, *parts)
    return res[1], res[0]


def far_kernel(width, heads, flags, offsets, q_ref, tiles, out_ref, token, buffer, sems):
    step = pl.program_id(0)
    pass_flags(flags, token)

    def copy(i):
        owner = lax.rem(flags[6] + 1 + offsets[i], width)
        cols = pl.ds(pl.multiple_of(i // FAR * HD, HD), HD)
        return pltpu.make_async_copy(tiles.at[owner, :, :, cols], buffer.at[i], sems.at[i])

    @pl.when(step == 0)
    def _():
        @pl.loop(0, HEADS * FAR)
        def _(i):
            copy(i).start()

    for i in range(heads * FAR):
        copy(step * (heads * FAR) + i).wait()
    units = []
    for head in range(heads):
        first = (step * heads + head) * FAR
        units.append(
            (
                lambda head=head: q_ref[:, lanes(head)],
                jnp.concatenate([buffer[first + f, 0] for f in range(FAR)], axis=0),
                jnp.concatenate([buffer[first + f, 1] for f in range(FAR)], axis=0),
            )
        )

    def finish(head, out, log):
        out_ref[:TILE, lanes(head)] = out
        write_logs(out_ref, lanes(head), jnp.broadcast_to(log, (TILE, HD)))

    pipelined(units, finish)


def far(flags, offsets, q, tiles, step):
    smem = pl.BlockSpec(memory_space=pltpu.SMEM)
    res = pl.pallas_call(
        functools.partial(far_kernel, tiles.shape[0], step),
        grid=(HEADS // step,),
        in_specs=[
            smem, smem, pl.BlockSpec((TILE, step * HD), lambda h: (0, h)), pl.BlockSpec(memory_space=pl.ANY)
        ],
        out_specs=[pl.BlockSpec((TILE + LOG_ROWS, step * HD), lambda h: (0, h)), smem],
        out_shape=[
            jax.ShapeDtypeStruct((TILE + LOG_ROWS, HEADS * HD), F32),
            jax.ShapeDtypeStruct(flags.shape, flags.dtype),
        ],
        scratch_shapes=[
            pltpu.VMEM((HEADS * FAR, 2, TILE, HD), BF),
            pltpu.SemaphoreType.DMA((HEADS * FAR,)),
        ],
        compiler_params=pltpu.CompilerParams(vmem_limit_bytes=VMEM),
        cost_estimate=pl.CostEstimate(flops=1000, bytes_accessed=1000, transcendentals=0),
        name="far",
    )(flags, offsets, q, tiles)
    return res[1], res[0]


def final_kernel(part_specs, heads, flags, *refs):
    arrays, out_ref = refs[:-1], refs[-1]
    step = pl.program_id(0)
    for head in range(heads):
        at = lanes(head)
        parts, place = [], 0
        for flag, groups in part_specs:
            per = HEADS // groups // heads
            sums, log = arrays[place][:TILE, at].astype(F32), read_logs(arrays[place], at)
            for g in range(1, groups):
                later = step >= g * per
                sums = jnp.where(later, arrays[place + g][:TILE, at].astype(F32), sums)
                log = jnp.where(later, read_logs(arrays[place + g], at), log)
            place += groups
            parts.append((sums, jnp.where(flags[flag] != 0, log, NEG)))
        merged, _, scale = merge_parts(parts)
        out_ref[:, at] = (merged / scale).astype(out_ref.dtype)


def final(flags, parts, step):
    specs, arrays = [], []
    for _, group_arrays in parts:
        per = HEADS // len(group_arrays) // step
        for g, array in enumerate(group_arrays):
            index = functools.partial(
                lambda h, low, top: (0, jnp.clip(h - low, 0, top)), low=g * per, top=per - 1
            )
            specs.append(pl.BlockSpec((TILE + LOG_ROWS, step * HD), index))
            arrays.append(array)
    return pl.pallas_call(
        functools.partial(final_kernel, [(f, len(a)) for f, a in parts], step),
        grid=(HEADS // step,),
        in_specs=[pl.BlockSpec(memory_space=pltpu.SMEM)] + specs,
        out_specs=pl.BlockSpec((TILE, step * HD), lambda h: (0, h)),
        out_shape=jax.ShapeDtypeStruct((TILE, HEADS * HD), BF),
        compiler_params=pltpu.CompilerParams(vmem_limit_bytes=VMEM),
        cost_estimate=pl.CostEstimate(flops=1000, bytes_accessed=1000, transcendentals=0),
        name="final",
    )(flags, *arrays)


def on_device(queries, keys_values, far_offsets):
    width, height = lax.axis_size("wa"), lax.axis_size("ha")
    col, row = lax.axis_index("wa"), lax.axis_index("ha")
    up = [(i, i + 1) for i in range(height - 1)]
    down = [(j, i) for i, j in up]
    mate = [(i, i ^ 1) for i in range(width)]
    across = [(i, i + 1) for i in range(1, width - 1, 2)]
    across = across + [(j, i) for i, j in across]

    q = queries.reshape(TILE, HEADS * HD)
    kv = keys_values.reshape(TT, 2, TILE, HEADS * HD)

    lo, hi = row > 0, row < height - 1
    side = (col > 0) & (col < width - 1)
    flags = jnp.stack(
        [jnp.int32(1)] + [f.astype(jnp.int32) for f in (lo, hi, side, side & lo, side & hi)] + [col, row]
    )

    q_side = lax.ppermute(q, "wa", across)
    q_lo = lax.ppermute(q, "ha", up)
    q_hi = lax.ppermute(q, "ha", down)
    kv_mate = lax.ppermute(kv, "wa", mate)

    flags, (own,) = window("own", flags, [q], [kv], [(0, (0,))], 0, HEADS, [F32], 2, 3)
    q_side, middle, flags = lax.optimization_barrier((q_side, kv[1], flags))
    qs_lo = lax.ppermute(q_side, "ha", up)
    qs_hi = lax.ppermute(q_side, "ha", down)
    tiles = lax.all_gather(middle, "wa")

    def rows(flags, name, q_there, flops=1000, after=()):
        flags, (o,) = window(
            name, flags, [q_there], [kv, kv_mate], [(0, (0, 1))], 0, HEADS, [BF], 2, 3, flops, after
        )
        return flags, o

    def side_part(flags, g):
        per = HEADS // SIDE_GROUPS
        flags, (s_lo, s_hi, s_own) = window(
            "side", flags, [qs_lo, qs_hi, q_side], [kv], [(0, (0,)), (1, (0,)), (2, (0,))],
            g * per, per, [BF, BF, F32], 1, 2,
        )
        return flags, [s_own, lax.ppermute(s_hi, "ha", up), lax.ppermute(s_lo, "ha", down)]

    flags, o_lo = rows(flags, "row_lo", q_lo, 10**13, [q_hi])
    from_hi = lax.ppermute(o_lo, "ha", down)
    pending, sides = [], []
    for g in range(SIDE_GROUPS):
        flags, parts = side_part(flags, g)
        pending.append(parts)
    flags, o_hi = rows(flags, "row_hi", q_hi)
    from_lo = lax.ppermute(o_hi, "ha", up)
    for parts in pending:
        flags, merged = merge("side_merge", flags, parts, [3, 4, 5], HEADS // SIDE_GROUPS, 6)
        sides.append(lax.ppermute(merged, "wa", across))
    flags, (mates,) = window("mate", flags, [q], [kv_mate], [(0, (0,))], 0, HEADS, [F32], 2, 3)
    flags, far_part = far(flags, far_offsets.reshape(-1), q, tiles, 4)
    out = final(
        flags,
        [(0, [own]), (0, [mates]), (0, [far_part]), (1, [from_lo]), (2, [from_hi]), (3, sides)],
        6,
    )
    return out.reshape(queries.shape)


def solution(mesh):
    placed = (
        P("ha", "wa", None, None),
        P("ha", "wa", None, None, None, None),
        P("wa", "ha", None, None),
    )
    return jax.shard_map(
        on_device, mesh=mesh, in_specs=placed, out_specs=P("ha", "wa", None, None), check_vma=False
    )
```

time: 1240 us -> 196 us (0.16)
  waiting for transfers between devices: 669 us -> 15.7 us
  matrix products: 248 us -> 0 us
  other arithmetic: 153 us -> 0 us
  Pallas kernels: 0 us -> 120 us
  local copies, waits for them, and re-layouts: 124 us -> 4.52 us
  between operations: 0.15 us -> 13.6 us
    all_to_all x2 -> x0, waiting for transfers between devices: 522 us -> none  [the longest x1 435 us: on_device(): lax.all_to_all(wanted_table, 'wa', split_axis=0, concat_axis=0, tiled=True)]
    dot_general x24 -> x0, matrix products: 248 us -> none  [the longest x12 147 us: one_head(): jnp.einsum('iqd,ikd->iqk', head_queries, key_tiles, preferred_element_typ...]
    ppermute x4 -> x14, waiting for transfers between devices: 147 us -> 15.7 us  [the longest x1 5.7 us: on_device(): q_side = lax.ppermute(q, 'wa', across)]
    pallas_call x0 -> x10, Pallas kernels: none -> 120 us  [the longest x6 91.2 us: window(): pl.pallas_call(functools.partial(window_kernel, jobs, len(qs), len(kvs),...]
    reduce_sum x14 -> x0, other arithmetic: 101 us -> none  [the longest x12 101 us: one_head(): totals = jnp.sum(weights, axis=2, keepdims=True)]
    concatenate x3 -> x0, other arithmetic: 42.6 us -> none  [the longest x1 42.5 us: with_halo(): array = jnp.concatenate([before, array, after], axis=dim)]
    another operation x13 -> x1, local copies, waits for them, and re-layouts: 38.2 us -> 0.59 us  [on_device(): jnp.stack([jnp.int32(1)] + [f.astype(jnp.int32) for f in (lo, hi, side, s...]
    ppermute x4 -> x14, starting transfers between devices: 14.1 us -> 38.8 us  [the longest x2 7.55 us: side_part(): lax.ppermute(s_hi, 'ha', up)]
  transfers between devices with their start and end apart: 6 -> 15, of which waited for: 3 -> 4; matrix products, arithmetic and copies ran while one was open for 3% -> 2% of each run, Pallas kernels for 0% -> 58%
where the time goes in v2:
time: 196 us; the launch traced here: 193 us
  Pallas kernels  120 us (61%)
  starting transfers between devices  38.8 us (20%)
  waiting for transfers between devices  15.7 us (8%)
  between operations  13.6 us (7%)
  local copies, waits for them, and re-layouts  4.52 us (2%)
    pallas_call x6, Pallas kernels, window(): pl.pallas_call(functools.partial(window_kernel, jobs, len(qs), len(kvs),...  91.2 us
    pallas_call x2, Pallas kernels, merge(): pl.pallas_call(functools.partial(merge_kernel, part_flags, step), grid=(n...  9.83 us
    pallas_call x1, Pallas kernels, far(): pl.pallas_call(functools.partial(far_kernel, tiles.shape[0], step), grid=...  9.82 us
    pallas_call x1, Pallas kernels, final(): pl.pallas_call(functools.partial(final_kernel, [(f, len(a)) for f, a in p...  9.17 us
    ppermute x2, starting transfers between devices, side_part(): lax.ppermute(s_hi, 'ha', up)  7.55 us
    ppermute x2, starting transfers between devices, on_device(): sides.append(lax.ppermute(merged, 'wa', across))  6.46 us
    ppermute x1, waiting for transfers between devices, on_device(): q_side = lax.ppermute(q, 'wa', across)  5.7 us
    ppermute x1, starting transfers between devices, on_device(): q_lo = lax.ppermute(q, 'ha', up)  5.07 us
  transfers between devices with their start and end apart: 15, of which 4 were waited for; matrix products, arithmetic and copies ran while one was open for 2% of the time, Pallas kernels for 58%

profile of v2, /device:TPU:3, one launch (start us, length us, event | category | flops | bytes accessed | tf_op | source)
XLA Modules:
  0.0 192.6 jit_solution(15078916560918636729)
XLA Ops:
  7.2 3.0 %collective-permute-start = (bf16[384,1536]{1,0:T(8,128)(2,1)}, bf16[384,1536]{1,0:T(8,128)(2,1)}, u32[]{:S(2)}, u32[]{:S(2)}) collective-permute-start(bf16[384,1536]{1,0:T(8,128)(2,1)} %bitcast.20), channel_id=1, source_target_pairs={{1,2},{3,4},{5,6},{2,1},{4,3},{6,5},{9,10},{11,12},{13,14},{10,9},... | collective-permute-start | bytes 3538952 | tf_op jit(solution)/shard_map/ppermute | solution.py:304
  11.5 5.1 %collective-permute-start.2 = (bf16[384,1536]{1,0:T(8,128)(2,1)}, bf16[384,1536]{1,0:T(8,128)(2,1)}, u32[]{:S(2)}, u32[]{:S(2)}) collective-permute-start(bf16[384,1536]{1,0:T(8,128)(2,1)} %bitcast.22), channel_id=1, source_target_pairs={{0,8},{8,16},{16,24},{1,9},{9,17},{17,25},{2,10},{10,18},{18,26},{... | collective-permute-start | bytes 3538952 | tf_op jit(solution)/shard_map/ppermute | solution.py:305
  17.2 11.9 %own.1 = (f32[400,1536]{1,0:T(8,128)}, s32[8]{0:T(128)}) custom-call(s32[8]{0:T(128)} %stack.51.flags, bf16[384,1536]{1,0:T(8,128)(2,1)} %bitcast.23, bf16[3,2,384,1536]{3,2,1,0:T(8,128)(2,1)} %bitcast.14), custom_call_target="tpu_custom_call" | custom-call | flops 1000 | bytes 1000 | tf_op jit(solution)/shard_map/own/pallas_call | solution.py:129
  29.1 3.2 %slice_bitcast_fusion = bf16[2,384,1536]{2,1,0:T(8,128)(2,1)} fusion(bf16[1,1,3,2,384,1536]{5,4,3,2,1,0:T(8,128)(2,1)} %param.4), kind=kLoop, calls=%fused_computation | loop fusion | bytes 4718592 | tf_op jit(solution)/shard_map/squeeze | solution.py:310
  32.2 5.7 %collective-permute-done.refs_2_ = bf16[384,1536]{1,0:T(8,128)(2,1)} collective-permute-done((bf16[384,1536]{1,0:T(8,128)(2,1)}, bf16[384,1536]{1,0:T(8,128)(2,1)}, u32[]{:S(2)}, u32[]{:S(2)}) %collective-permute-start) | collective-permute-done | bytes 1179680 | tf_op jit(solution)/shard_map/ppermute | solution.py:304
  38.0 4.2 %collective-permute-start.4 = (bf16[384,1536]{1,0:T(8,128)(2,1)}, bf16[384,1536]{1,0:T(8,128)(2,1)}, u32[]{:S(2)}, u32[]{:S(2)}) collective-permute-start(bf16[384,1536]{1,0:T(8,128)(2,1)} %collective-permute-done.refs_2_), channel_id=1, source_target_pairs={{0,8},{8,16},{16,24},{1,9},{9,17},{17,25},{2,10},{10,18},{18,26},{... | collective-permute-start | bytes 3538952 | tf_op jit(solution)/shard_map/ppermute | solution.py:311
  43.5 19.0 %row_lo.1 = (bf16[400,1536]{1,0:T(8,128)(2,1)}, s32[8]{0:T(128)}) custom-call(s32[8]{0:T(128)} %get-tuple-element.31.flags, bf16[384,1536]{1,0:T(8,128)(2,1)} %collective-permute-done.1.refs_0_, bf16[384,1536]{1,0:T(8,128)(2,1)} %collective-permute-done.2.refs_1_, bf16[3,2,384,1536]{3,2,1,0:T(8,128)(2,1)} %bitcast.15, ...), custom_call_target="tpu_custom_call" | custom-call | flops 9999999827968 | bytes 1000 | tf_op jit(solution)/shard_map/row_lo/pallas_call | solution.py:129
  62.5 4.3 %collective-permute-done.4.refs_0_ = bf16[384,1536]{1,0:T(8,128)(2,1)} collective-permute-done((bf16[384,1536]{1,0:T(8,128)(2,1)}, bf16[384,1536]{1,0:T(8,128)(2,1)}, u32[]{:S(2)}, u32[]{:S(2)}) %collective-permute-start.4) | collective-permute-done | bytes 1179680 | tf_op jit(solution)/shard_map/ppermute | solution.py:311
  66.7 4.6 %collective-permute-done.5.refs_1_ = bf16[384,1536]{1,0:T(8,128)(2,1)} collective-permute-done((bf16[384,1536]{1,0:T(8,128)(2,1)}, bf16[384,1536]{1,0:T(8,128)(2,1)}, u32[]{:S(2)}, u32[]{:S(2)}) %collective-permute-start.5) | collective-permute-done | bytes 1179680 | tf_op jit(solution)/shard_map/ppermute | solution.py:312
  71.3 14.4 %side.2 = (bf16[400,768]{1,0:T(8,128)(2,1)}, bf16[400,768]{1,0:T(8,128)(2,1)}, f32[400,768]{1,0:T(8,128)}, s32[8]{0:T(128)}) custom-call(s32[8]{0:T(128)} %get-tuple-element.32.flags, bf16[384,1536]{1,0:T(8,128)(2,1)} %collective-permute-done.4.refs_0_, bf16[384,1536]{1,0:T(8,128)(2,1)} %collective-permute-done.5.refs_1_, ...), custom_call_target="tpu_custom_call" | custom-call | flops 1000 | bytes 1000 | tf_op jit(solution)/shard_map/side/pallas_call | solution.py:129
  85.7 3.0 %collective-permute-start.6 = (bf16[400,768]{1,0:T(8,128)(2,1)}, bf16[400,768]{1,0:T(8,128)(2,1)}, u32[]{:S(2)}, u32[]{:S(2)}) collective-permute-start(bf16[400,768]{1,0:T(8,128)(2,1)} %get-tuple-element.38), channel_id=1, source_target_pairs={{0,8},{8,16},{16,24},{1,9},{9,17},{17,25},{2,10},{10,18},{18,26},{... | collective-permute-start | bytes 1843208 | tf_op jit(solution)/shard_map/ppermute | solution.py:327
  88.7 1.5 collective-permute-start.7
  90.2 15.1 %side.3 = (bf16[400,768]{1,0:T(8,128)(2,1)}, bf16[400,768]{1,0:T(8,128)(2,1)}, f32[400,768]{1,0:T(8,128)}, s32[8]{0:T(128)}) custom-call(s32[8]{0:T(128)} %get-tuple-element.34.flags, bf16[384,1536]{1,0:T(8,128)(2,1)} %collective-permute-done.4.refs_0_, bf16[384,1536]{1,0:T(8,128)(2,1)} %collective-permute-done.5.refs_1_, ...), custom_call_target="tpu_custom_call" | custom-call | flops 1000 | bytes 1000 | tf_op jit(solution)/shard_map/side/pallas_call | solution.py:129
  105.3 4.5 %collective-permute-start.8 = (bf16[400,768]{1,0:T(8,128)(2,1)}, bf16[400,768]{1,0:T(8,128)(2,1)}, u32[]{:S(2)}, u32[]{:S(2)}) collective-permute-start(bf16[400,768]{1,0:T(8,128)(2,1)} %get-tuple-element.42), channel_id=1, source_target_pairs={{0,8},{8,16},{16,24},{1,9},{9,17},{17,25},{2,10},{10,18},{18,26},{... | collective-permute-start | bytes 1843208 | tf_op jit(solution)/shard_map/ppermute | solution.py:327
  111.1 19.0 %row_hi.1 = (bf16[400,1536]{1,0:T(8,128)(2,1)}, s32[8]{0:T(128)}) custom-call(s32[8]{0:T(128)} %get-tuple-element.35.flags, bf16[384,1536]{1,0:T(8,128)(2,1)} %collective-permute-done.1.refs_0_, bf16[3,2,384,1536]{3,2,1,0:T(8,128)(2,1)} %bitcast.18, bf16[3,2,384,1536]{3,2,1,0:T(8,128)(2,1)} %collective-permute-done.3.refs_3_.refs_2_.refs_1_), custom_call_target="tpu_custom_call" | custom-call | flops 1000 | bytes 1000 | tf_op jit(solution)/shard_map/row_hi/pallas_call | solution.py:129
  130.0 5.0 %collective-permute-start.10 = (bf16[400,1536]{1,0:T(8,128)(2,1)}, bf16[400,1536]{1,0:T(8,128)(2,1)}, u32[]{:S(2)}, u32[]{:S(2)}) collective-permute-start(bf16[400,1536]{1,0:T(8,128)(2,1)} %get-tuple-element.51), channel_id=1, source_target_pairs={{0,8},{8,16},{16,24},{1,9},{9,17},{17,25},{2,10},{10,18},{18,26},{... | collective-permute-start | bytes 3686408 | tf_op jit(solution)/shard_map/ppermute | solution.py:336
  135.1 1.5 collective-permute-start.11
  136.6 4.8 %side_merge.2 = (bf16[400,768]{1,0:T(8,128)(2,1)}, s32[8]{0:T(128)}) custom-call(s32[8]{0:T(128)} %get-tuple-element.36.flags, f32[400,768]{1,0:T(8,128)} %get-tuple-element.37.refs_0_, bf16[400,768]{1,0:T(8,128)(2,1)} %collective-permute-done.6.refs_1_, bf16[400,768]{1,0:T(8,128)(2,1)} %collective-permute-done.7.refs_2_), custom_call_target="tpu_custom_call" | custom-call | flops 1000 | bytes 1000 | tf_op jit(solution)/shard_map/side_merge/pallas_call | solution.py:170
  141.4 5.1 %side_merge.3 = (bf16[400,768]{1,0:T(8,128)(2,1)}, s32[8]{0:T(128)}) custom-call(s32[8]{0:T(128)} %get-tuple-element.40.flags, f32[400,768]{1,0:T(8,128)} %get-tuple-element.41.refs_0_, bf16[400,768]{1,0:T(8,128)(2,1)} %collective-permute-done.8.refs_1_, bf16[400,768]{1,0:T(8,128)(2,1)} %collective-permute-done.9.refs_2_), custom_call_target="tpu_custom_call" | custom-call | flops 1000 | bytes 1000 | tf_op jit(solution)/shard_map/side_merge/pallas_call | solution.py:170
  146.5 3.7 %collective-permute-start.13 = (bf16[400,768]{1,0:T(8,128)(2,1)}, bf16[400,768]{1,0:T(8,128)(2,1)}, u32[]{:S(2)}, u32[]{:S(2)}) collective-permute-start(bf16[400,768]{1,0:T(8,128)(2,1)} %get-tuple-element.54), channel_id=1, source_target_pairs={{1,2},{3,4},{5,6},{2,1},{4,3},{6,5},{9,10},{11,12},{13,14},{10,9},... | collective-permute-start | bytes 1843208 | tf_op jit(solution)/shard_map/ppermute | solution.py:339
  150.2 2.8 %collective-permute-start.12 = (bf16[400,768]{1,0:T(8,128)(2,1)}, bf16[400,768]{1,0:T(8,128)(2,1)}, u32[]{:S(2)}, u32[]{:S(2)}) collective-permute-start(bf16[400,768]{1,0:T(8,128)(2,1)} %get-tuple-element.53), channel_id=1, source_target_pairs={{1,2},{3,4},{5,6},{2,1},{4,3},{6,5},{9,10},{11,12},{13,14},{10,9},... | collective-permute-start | bytes 1843208 | tf_op jit(solution)/shard_map/ppermute | solution.py:339
  153.7 11.9 %mate.1 = (f32[400,1536]{1,0:T(8,128)}, s32[8]{0:T(128)}) custom-call(s32[8]{0:T(128)} %get-tuple-element.44.flags, bf16[384,1536]{1,0:T(8,128)(2,1)} %bitcast.24, bf16[3,2,384,1536]{3,2,1,0:T(8,128)(2,1)} %collective-permute-done.3.refs_3_.refs_2_.refs_1_), custom_call_target="tpu_custom_call" | custom-call | flops 1000 | bytes 1000 | tf_op jit(solution)/shard_map/mate/pallas_call | solution.py:129
  165.6 9.8 %far.1 = (f32[400,1536]{1,0:T(8,128)}, s32[8]{0:T(128)}) custom-call(s32[8]{0:T(128)} %get-tuple-element.45.flags, s32[24]{0:T(128)} %reshape.16.offsets, bf16[384,1536]{1,0:T(8,128)(2,1)} %bitcast.25, bf16[8,2,384,1536]{3,2,1,0:T(8,128)(2,1)} %bitcast.19), custom_call_target="tpu_custom_call" | custom-call | flops 1000 | bytes 1000 | tf_op jit(solution)/shard_map/far/pallas_call | solution.py:223
  176.6 9.2 %final.1 = bf16[384,1536]{1,0:T(8,128)(2,1)} custom-call(s32[8]{0:T(128)} %get-tuple-element.47.flags, f32[400,1536]{1,0:T(8,128)} %get-tuple-element.48.refs_0_, f32[400,1536]{1,0:T(8,128)} %get-tuple-element.49.refs_1_, f32[400,1536]{1,0:T(8,128)} %get-tuple-element.50.refs_2_, bf16[400,1536]{1,0:T(8,128)(2,1)} %collective-permute-done.10.refs_3_, ...), custom_call_target="tpu_custom_call" | custom-call | flops 1000 | bytes 1000 | tf_op jit(solution)/shard_map/final/pallas_call | solution.py:274
  (23 shorter events, 7.0 us)
Async XLA Ops:
  6.5 159.0 %all-gather.3.cloned.1.call-start = ((), (), s32[]{:S(2)}) async-start(), calls=%async_computation | async-start | bytes 21233664 | tf_op jit(solution)/shard_map/all_gather | solution.py:313
  6.5 37.0 %collective-permute-start.3 = (bf16[3,2,384,1536]{3,2,1,0:T(8,128)(2,1)}, bf16[3,2,384,1536]{3,2,1,0:T(8,128)(2,1)}, u32[]{:S(2)}, u32[]{:S(2)}) collective-permute-start(bf16[3,2,384,1536]{3,2,1,0:T(8,128)(2,1)} %bitcast.13), channel_id=1, source_target_pairs={{0,1},{1,0},{2,3},{3,2},{4,5},{5,4},{6,7},{7,6},{8,9},{9,8},{10,11... | collective-permute-start | bytes 21233672 | tf_op jit(solution)/shard_map/ppermute | solution.py:307
  7.2 30.7 %collective-permute-start = (bf16[384,1536]{1,0:T(8,128)(2,1)}, bf16[384,1536]{1,0:T(8,128)(2,1)}, u32[]{:S(2)}, u32[]{:S(2)}) collective-permute-start(bf16[384,1536]{1,0:T(8,128)(2,1)} %bitcast.20), channel_id=1, source_target_pairs={{1,2},{3,4},{5,6},{2,1},{4,3},{6,5},{9,10},{11,12},{13,14},{10,9},... | collective-permute-start | bytes 3538952 | tf_op jit(solution)/shard_map/ppermute | solution.py:304
  10.2 33.3 %collective-permute-start.1 = (bf16[384,1536]{1,0:T(8,128)(2,1)}, bf16[384,1536]{1,0:T(8,128)(2,1)}, u32[]{:S(2)}, u32[]{:S(2)}) collective-permute-start(bf16[384,1536]{1,0:T(8,128)(2,1)} %bitcast.21), channel_id=1, source_target_pairs={{8,0},{16,8},{24,16},{9,1},{17,9},{25,17},{10,2},{18,10},{26,18},{... | collective-permute-start | bytes 3538952 | tf_op jit(solution)/shard_map/ppermute | solution.py:306
  11.5 32.0 %collective-permute-start.2 = (bf16[384,1536]{1,0:T(8,128)(2,1)}, bf16[384,1536]{1,0:T(8,128)(2,1)}, u32[]{:S(2)}, u32[]{:S(2)}) collective-permute-start(bf16[384,1536]{1,0:T(8,128)(2,1)} %bitcast.22), channel_id=1, source_target_pairs={{0,8},{8,16},{16,24},{1,9},{9,17},{17,25},{2,10},{10,18},{18,26},{... | collective-permute-start | bytes 3538952 | tf_op jit(solution)/shard_map/ppermute | solution.py:305
  38.0 28.8 %collective-permute-start.4 = (bf16[384,1536]{1,0:T(8,128)(2,1)}, bf16[384,1536]{1,0:T(8,128)(2,1)}, u32[]{:S(2)}, u32[]{:S(2)}) collective-permute-start(bf16[384,1536]{1,0:T(8,128)(2,1)} %collective-permute-done.refs_2_), channel_id=1, source_target_pairs={{0,8},{8,16},{16,24},{1,9},{9,17},{17,25},{2,10},{10,18},{18,26},{... | collective-permute-start | bytes 3538952 | tf_op jit(solution)/shard_map/ppermute | solution.py:311
  42.2 29.1 %collective-permute-start.5 = (bf16[384,1536]{1,0:T(8,128)(2,1)}, bf16[384,1536]{1,0:T(8,128)(2,1)}, u32[]{:S(2)}, u32[]{:S(2)}) collective-permute-start(bf16[384,1536]{1,0:T(8,128)(2,1)} %collective-permute-done.refs_2_), channel_id=1, source_target_pairs={{8,0},{16,8},{24,16},{9,1},{17,9},{25,17},{10,2},{18,10},{26,18},{... | collective-permute-start | bytes 3538952 | tf_op jit(solution)/shard_map/ppermute | solution.py:312
  85.7 49.4 %collective-permute-start.6 = (bf16[400,768]{1,0:T(8,128)(2,1)}, bf16[400,768]{1,0:T(8,128)(2,1)}, u32[]{:S(2)}, u32[]{:S(2)}) collective-permute-start(bf16[400,768]{1,0:T(8,128)(2,1)} %get-tuple-element.38), channel_id=1, source_target_pairs={{0,8},{8,16},{16,24},{1,9},{9,17},{17,25},{2,10},{10,18},{18,26},{... | collective-permute-start | bytes 1843208 | tf_op jit(solution)/shard_map/ppermute | solution.py:327
  88.7 47.9 %collective-permute-start.7 = (bf16[400,768]{1,0:T(8,128)(2,1)}, bf16[400,768]{1,0:T(8,128)(2,1)}, u32[]{:S(2)}, u32[]{:S(2)}) collective-permute-start(bf16[400,768]{1,0:T(8,128)(2,1)} %get-tuple-element.39), channel_id=1, source_target_pairs={{8,0},{16,8},{24,16},{9,1},{17,9},{25,17},{10,2},{18,10},{26,18},{... | collective-permute-start | bytes 1843208 | tf_op jit(solution)/shard_map/ppermute | solution.py:327
  105.3 36.1 %collective-permute-start.8 = (bf16[400,768]{1,0:T(8,128)(2,1)}, bf16[400,768]{1,0:T(8,128)(2,1)}, u32[]{:S(2)}, u32[]{:S(2)}) collective-permute-start(bf16[400,768]{1,0:T(8,128)(2,1)} %get-tuple-element.42), channel_id=1, source_target_pairs={{0,8},{8,16},{16,24},{1,9},{9,17},{17,25},{2,10},{10,18},{18,26},{... | collective-permute-start | bytes 1843208 | tf_op jit(solution)/shard_map/ppermute | solution.py:327
  109.8 31.6 %collective-permute-start.9 = (bf16[400,768]{1,0:T(8,128)(2,1)}, bf16[400,768]{1,0:T(8,128)(2,1)}, u32[]{:S(2)}, u32[]{:S(2)}) collective-permute-start(bf16[400,768]{1,0:T(8,128)(2,1)} %get-tuple-element.43), channel_id=1, source_target_pairs={{8,0},{16,8},{24,16},{9,1},{17,9},{25,17},{10,2},{18,10},{26,18},{... | collective-permute-start | bytes 1843208 | tf_op jit(solution)/shard_map/ppermute | solution.py:327
  130.0 46.5 %collective-permute-start.10 = (bf16[400,1536]{1,0:T(8,128)(2,1)}, bf16[400,1536]{1,0:T(8,128)(2,1)}, u32[]{:S(2)}, u32[]{:S(2)}) collective-permute-start(bf16[400,1536]{1,0:T(8,128)(2,1)} %get-tuple-element.51), channel_id=1, source_target_pairs={{0,8},{8,16},{16,24},{1,9},{9,17},{17,25},{2,10},{10,18},{18,26},{... | collective-permute-start | bytes 3686408 | tf_op jit(solution)/shard_map/ppermute | solution.py:336
  135.1 41.5 %collective-permute-start.11 = (bf16[400,1536]{1,0:T(8,128)(2,1)}, bf16[400,1536]{1,0:T(8,128)(2,1)}, u32[]{:S(2)}, u32[]{:S(2)}) collective-permute-start(bf16[400,1536]{1,0:T(8,128)(2,1)} %get-tuple-element.52), channel_id=1, source_target_pairs={{8,0},{16,8},{24,16},{9,1},{17,9},{25,17},{10,2},{18,10},{26,18},{... | collective-permute-start | bytes 3686408 | tf_op jit(solution)/shard_map/ppermute | solution.py:330
  141.4 11.6 %copy-start = (s32[1,1,12,2]{2,3,1,0:T(2,128)S(1)}, s32[1,1,12,2]{2,3,1,0:T(2,128)}, u32[]{:S(2)}) copy-start(s32[1,1,12,2]{2,3,1,0:T(2,128)} %param.5) | copy-start | bytes 292
  146.5 28.9 %collective-permute-start.13 = (bf16[400,768]{1,0:T(8,128)(2,1)}, bf16[400,768]{1,0:T(8,128)(2,1)}, u32[]{:S(2)}, u32[]{:S(2)}) collective-permute-start(bf16[400,768]{1,0:T(8,128)(2,1)} %get-tuple-element.54), channel_id=1, source_target_pairs={{1,2},{3,4},{5,6},{2,1},{4,3},{6,5},{9,10},{11,12},{13,14},{10,9},... | collective-permute-start | bytes 1843208 | tf_op jit(solution)/shard_map/ppermute | solution.py:339
  150.2 26.4 %collective-permute-start.12 = (bf16[400,768]{1,0:T(8,128)(2,1)}, bf16[400,768]{1,0:T(8,128)(2,1)}, u32[]{:S(2)}, u32[]{:S(2)}) collective-permute-start(bf16[400,768]{1,0:T(8,128)(2,1)} %get-tuple-element.53), channel_id=1, source_target_pairs={{1,2},{3,4},{5,6},{2,1},{4,3},{6,5},{9,10},{11,12},{13,14},{10,9},... | collective-permute-start | bytes 1843208 | tf_op jit(solution)/shard_map/ppermute | solution.py:339
Sparse Core Ops, SparseCore 0:
  43.6 100.4 all-gather.2

commit v3 on v2

v3 whole, which is shorter than its diff:
```python
import functools

import jax
import jax.numpy as jnp
from jax import lax
from jax.experimental import pallas as pl
from jax.experimental.pallas import tpu as pltpu
from jax.sharding import PartitionSpec as P

HEADS = 12
HD = 128
TILE = 384
TT = 3
FAR = 2
NEG = -1e30
SCALE2 = 1.4426950408889634 / HD**0.5
VMEM = 127 * 2**19
ROW_GROUPS = 2
SIDE_GROUPS = 2
BF, F32 = jnp.bfloat16, jnp.float32
LOG_ROWS = 16
BLOCK = HD + LOG_ROWS


SAMPLE = 128
LIMIT = 2.0**100


def attend(q, keys, values, peak):
    s = lax.dot_general(keys, q, (((1,), (1,)), ((), ())), preferred_element_type=F32)
    if peak is None:
        peak = jnp.max(s, axis=0, keepdims=True)
    weights = jnp.exp2((s - peak) * SCALE2)
    total = jnp.sum(weights, axis=0, keepdims=True)
    summed = jnp.dot(values, weights.astype(BF), preferred_element_type=F32)
    return summed, total, peak


def attend_all(heads, groups, get, finish):
    worst = None
    for head in range(heads):
        for group in range(groups):
            q, keys, values = get(head, group)
            some = lax.dot_general(
                keys[:SAMPLE], q, (((1,), (1,)), ((), ())), preferred_element_type=F32
            )
            peak = jnp.max(some, axis=0, keepdims=True)
            summed, total, _ = attend(q, keys, values, peak)
            finish(head, group, summed / total, peak * SCALE2 + jnp.log2(total))
            worst = total if worst is None else jnp.maximum(worst, total)

    @pl.when(jnp.logical_not(jnp.max(worst) < LIMIT))
    def _():
        @pl.loop(0, heads)
        def _(head):
            for group in range(groups):
                summed, total, peak = attend(*get(head, group), None)
                finish(head, group, summed / total, peak * SCALE2 + jnp.log2(total))


def rows_of(head, start, size):
    low = head * BLOCK + start
    return pl.ds(low if isinstance(head, int) else pl.multiple_of(low, 16), size)


def write_part(ref, head, out, log):
    first = log.astype(BF).astype(F32)
    second = (log - first).astype(BF).astype(F32)
    row = lax.broadcasted_iota(jnp.int32, (LOG_ROWS, log.shape[1]), 0)
    third = jnp.where(row == 2, log - first - second, 0.0)
    terms = jnp.where(row == 0, first, jnp.where(row == 1, second, third))
    ref[rows_of(head, 0, HD), :] = out.astype(ref.dtype)
    ref[rows_of(head, HD, LOG_ROWS), :] = terms.astype(ref.dtype)


def read_part(ref, head):
    low = head * BLOCK
    log = jnp.sum(ref[low + HD : low + BLOCK, :].astype(F32), axis=0, keepdims=True)
    return ref[low : low + HD, :].astype(F32), log


def lanes(i):
    return pl.ds(i * HD if isinstance(i, int) else pl.multiple_of(i * HD, HD), HD)


def pass_flags(flags, token):
    for i in range(8):
        token[i] = flags[i]


def window_kernel(jobs, n_q, n_kv, n_after, join, heads, flags, *refs):
    refs = refs[n_after:]
    q_refs = refs[:n_q]
    kv_refs = refs[n_q : n_q + n_kv]
    outs = refs[n_q + n_kv : n_q + n_kv + len(jobs)]
    pass_flags(flags, refs[n_q + n_kv + len(jobs)])
    groups = [list(range(i, min(i + join, len(jobs)))) for i in range(0, len(jobs), join)]

    def get(head, group):
        at = lanes(head)
        kvs = [kv_refs[i] for i in jobs[groups[group][0]][1]]
        q = jnp.concatenate([q_refs[jobs[j][0]][:, at] for j in groups[group]], axis=0)
        keys = jnp.concatenate([kv[t, 0, :, at] for kv in kvs for t in range(TT)], axis=0)
        values = jnp.concatenate([kv[t, 1, :, at].T for kv in kvs for t in range(TT)], axis=1)
        return q, keys, values

    def finish(head, group, out, log):
        for k, j in enumerate(groups[group]):
            cut = slice(k * TILE, (k + 1) * TILE)
            write_part(outs[j], head, out[:, cut], log[:, cut])

    attend_all(heads, len(groups), get, finish)


def window(name, flags, qs, kvs, jobs, h0, nh, out_types, join, step, flops=1000, after=()):
    smem = pl.BlockSpec(memory_space=pltpu.SMEM)
    base = h0 // step
    specs = [smem] + [pl.BlockSpec(memory_space=pl.ANY) for _ in after]
    specs += [pl.BlockSpec((TILE, step * HD), lambda h: (0, h + base)) for _ in qs]
    specs += [pl.BlockSpec((TT, 2, TILE, step * HD), lambda h: (0, 0, 0, h + base)) for _ in kvs]
    res = pl.pallas_call(
        functools.partial(window_kernel, jobs, len(qs), len(kvs), len(after), join, step),
        grid=(nh // step,),
        in_specs=specs,
        out_specs=[pl.BlockSpec((step * BLOCK, TILE), lambda h: (h, 0)) for _ in jobs] + [smem],
        out_shape=[jax.ShapeDtypeStruct((nh * BLOCK, TILE), t) for t in out_types]
        + [jax.ShapeDtypeStruct(flags.shape, flags.dtype)],
        compiler_params=pltpu.CompilerParams(vmem_limit_bytes=VMEM),
        cost_estimate=pl.CostEstimate(flops=flops, bytes_accessed=1000, transcendentals=0),
        name=name,
    )(flags, *after, *qs, *kvs)
    return res[-1], res[:-1]


def merge_parts(parts):
    top = functools.reduce(jnp.maximum, [p[1] for p in parts])
    scales = [jnp.exp2(p[1] - top) for p in parts]
    total = functools.reduce(jnp.add, scales)
    out = functools.reduce(jnp.add, [p[0] * (s / total) for p, s in zip(parts, scales)])
    return out, top + jnp.log2(total)


def masked(part, flag):
    return part[0], jnp.where(flag != 0, part[1], NEG)


def merge_kernel(part_flags, n_after, heads, flags, *refs):
    refs = refs[n_after:]
    n = len(part_flags)
    out, token = refs[n:]
    pass_flags(flags, token)
    for head in range(heads):
        write_part(
            out, head, *merge_parts([masked(read_part(refs[i], head), flags[f]) for i, f in enumerate(part_flags)])
        )


def merge(name, flags, parts, part_flags, nh, step, after=()):
    smem = pl.BlockSpec(memory_space=pltpu.SMEM)
    block = pl.BlockSpec((step * BLOCK, TILE), lambda h: (h, 0))
    res = pl.pallas_call(
        functools.partial(merge_kernel, part_flags, len(after), step),
        grid=(nh // step,),
        in_specs=[smem] + [pl.BlockSpec(memory_space=pl.ANY)] * len(after) + [block] * len(parts),
        out_specs=[block, smem],
        out_shape=[
            jax.ShapeDtypeStruct((nh * BLOCK, TILE), BF),
            jax.ShapeDtypeStruct(flags.shape, flags.dtype),
        ],
        compiler_params=pltpu.CompilerParams(vmem_limit_bytes=VMEM),
        cost_estimate=pl.CostEstimate(flops=1000, bytes_accessed=1000, transcendentals=0),
        name=name,
    )(flags, *after, *parts)
    return res[1], res[0]


def far_kernel(width, heads, flags, offsets, q_ref, tiles, _, out_ref, token, buffer, sems):
    step = pl.program_id(0)
    pass_flags(flags, token)

    def copy(i):
        owner = lax.rem(flags[6] + 1 + offsets[i], width)
        cols = pl.ds(pl.multiple_of(i // FAR * HD, HD), HD)
        return pltpu.make_async_copy(tiles.at[owner, :, :, cols], buffer.at[i], sems.at[i])

    @pl.when(step == 0)
    def _():
        @pl.loop(0, HEADS * FAR)
        def _(i):
            copy(i).start()

    for i in range(heads * FAR):
        copy(step * (heads * FAR) + i).wait()

    def get(head, _):
        first = (step * heads + head) * FAR
        keys = jnp.concatenate([buffer[first + f, 0] for f in range(FAR)], axis=0)
        values = jnp.concatenate([buffer[first + f, 1].T for f in range(FAR)], axis=1)
        return q_ref[:, lanes(head)], keys, values

    attend_all(heads, 1, get, lambda head, _, out, log: write_part(out_ref, head, out, log))


def far(flags, offsets, q, tiles, step, after):
    smem = pl.BlockSpec(memory_space=pltpu.SMEM)
    res = pl.pallas_call(
        functools.partial(far_kernel, tiles.shape[0], step),
        grid=(HEADS // step,),
        in_specs=[
            smem, smem, pl.BlockSpec((TILE, step * HD), lambda h: (0, h))
        ] + [pl.BlockSpec(memory_space=pl.ANY)] * 2,
        out_specs=[pl.BlockSpec((step * BLOCK, TILE), lambda h: (h, 0)), smem],
        out_shape=[
            jax.ShapeDtypeStruct((HEADS * BLOCK, TILE), F32),
            jax.ShapeDtypeStruct(flags.shape, flags.dtype),
        ],
        scratch_shapes=[
            pltpu.VMEM((HEADS * FAR, 2, TILE, HD), BF),
            pltpu.SemaphoreType.DMA((HEADS * FAR,)),
        ],
        compiler_params=pltpu.CompilerParams(vmem_limit_bytes=VMEM),
        cost_estimate=pl.CostEstimate(flops=10**13, bytes_accessed=1000, transcendentals=0),
        name="far",
    )(flags, offsets, q, tiles, after)
    return res[1], res[0]


def final_kernel(part_specs, heads, flags, *refs):
    arrays, out_ref = refs[:-1], refs[-1]
    step = pl.program_id(0)
    for head in range(heads):
        parts, place = [], 0
        for flag, groups in part_specs:
            per = HEADS // groups // heads
            part = read_part(arrays[place], head)
            for g in range(1, groups):
                later = read_part(arrays[place + g], head)
                part = tuple(jnp.where(step >= g * per, a, b) for a, b in zip(later, part))
            place += groups
            parts.append(masked(part, flags[flag]))
        out_ref[:, lanes(head)] = merge_parts(parts)[0].T.astype(out_ref.dtype)


def final(flags, parts, step):
    specs, arrays = [], []
    for _, group_arrays in parts:
        per = HEADS // len(group_arrays) // step
        for g, array in enumerate(group_arrays):
            index = functools.partial(
                lambda h, low, top: (jnp.clip(h - low, 0, top), 0), low=g * per, top=per - 1
            )
            specs.append(pl.BlockSpec((step * BLOCK, TILE), index))
            arrays.append(array)
    return pl.pallas_call(
        functools.partial(final_kernel, [(f, len(a)) for f, a in parts], step),
        grid=(HEADS // step,),
        in_specs=[pl.BlockSpec(memory_space=pltpu.SMEM)] + specs,
        out_specs=pl.BlockSpec((TILE, step * HD), lambda h: (0, h)),
        out_shape=jax.ShapeDtypeStruct((TILE, HEADS * HD), BF),
        compiler_params=pltpu.CompilerParams(vmem_limit_bytes=VMEM),
        cost_estimate=pl.CostEstimate(flops=1000, bytes_accessed=1000, transcendentals=0),
        name="final",
    )(flags, *arrays)


def on_device(queries, keys_values, far_offsets):
    width, height = lax.axis_size("wa"), lax.axis_size("ha")
    col, row = lax.axis_index("wa"), lax.axis_index("ha")
    up = [(i, i + 1) for i in range(height - 1)]
    down = [(j, i) for i, j in up]
    mate = [(i, i ^ 1) for i in range(width)]
    across = [(i, i + 1) for i in range(1, width - 1, 2)]
    across = across + [(j, i) for i, j in across]

    q = queries.reshape(TILE, HEADS * HD)
    kv = keys_values.reshape(TT, 2, TILE, HEADS * HD)

    lo, hi = row > 0, row < height - 1
    side = (col > 0) & (col < width - 1)
    flags = jnp.stack(
        [jnp.int32(1)] + [f.astype(jnp.int32) for f in (lo, hi, side, side & lo, side & hi)] + [col, row]
    )

    kv_mate = lax.ppermute(kv, "wa", mate)
    q_side = lax.ppermute(q, "wa", across)
    q_lo = lax.ppermute(q, "ha", up)
    q_hi = lax.ppermute(q, "ha", down)
    middle = kv[1]

    flags, (own,) = window("own", flags, [q], [kv, kv_mate], [(0, (0, 1))], 0, HEADS, [F32], 1, 3, after=[middle])
    tiles = lax.all_gather(middle, "wa")
    q_side, flags = lax.optimization_barrier((q_side, flags))
    qs_lo = lax.ppermute(q_side, "ha", up)
    qs_hi = lax.ppermute(q_side, "ha", down)

    def side_part(flags, g, flops):
        per = HEADS // SIDE_GROUPS
        flags, (s_lo, s_hi, s_own) = window(
            "side", flags, [qs_lo, qs_hi, q_side], [kv], [(0, (0,)), (1, (0,)), (2, (0,))],
            g * per, per, [BF, BF, F32], 3, 2, flops,
        )
        return flags, [s_own, lax.ppermute(s_hi, "ha", up), lax.ppermute(s_lo, "ha", down)]

    def side_return(flags, parts, after):
        flags, merged = merge("side_merge", flags, parts, [3, 4, 5], HEADS // SIDE_GROUPS, 6, after)
        return flags, lax.ppermute(merged, "wa", across)

    flags, (o_lo, o_hi) = window(
        "rows", flags, [q_lo, q_hi], [kv, kv_mate], [(0, (0, 1)), (1, (0, 1))], 0, HEADS, [BF, BF], 2, 2, 10**13
    )
    from_lo = lax.ppermute(o_hi, "ha", up)
    from_hi = lax.ppermute(o_lo, "ha", down)
    flags, first = side_part(flags, 0, 2 * 10**10)
    flags, second = side_part(flags, 1, 1000)
    flags, first = side_return(flags, first, [from_lo, from_hi])
    flags, second = side_return(flags, second, [])
    flags, far_part = far(flags, far_offsets.reshape(-1), q, tiles, 3, first)
    out = final(
        flags, [(0, [own]), (0, [far_part]), (1, [from_lo]), (2, [from_hi]), (3, [first, second])], 6
    )
    return out.reshape(queries.shape)


def solution(mesh):
    placed = (
        P("ha", "wa", None, None),
        P("ha", "wa", None, None, None, None),
        P("wa", "ha", None, None),
    )
    return jax.shard_map(
        on_device, mesh=mesh, in_specs=placed, out_specs=P("ha", "wa", None, None), check_vma=False
    )
```

time: 196 us -> 173 us (0.88); the launches traced: 193 us -> 172 us
  Pallas kernels: 120 us -> 81.5 us
  waiting for transfers between devices: 15.7 us -> 31.2 us
    pallas_call x6 -> x4, Pallas kernels: 91.2 us -> 60.4 us  [window(): pl.pallas_call(functools.partial(window_kernel, jobs, len(qs), len(kvs),...]
    ppermute x2, waiting for transfers between devices: 0.01 us -> 9.51 us  [side_part(): lax.ppermute(s_lo, 'ha', down)]
    ppermute x2, waiting for transfers between devices: 1.15 us -> 9.3 us  [side_return(): return (flags, lax.ppermute(merged, 'wa', across))]
    ppermute x2, waiting for transfers between devices: 0.01 us -> 6.57 us  [side_part(): lax.ppermute(s_hi, 'ha', up)]
    ppermute x1, waiting for transfers between devices: 4.56 us -> 0.01 us  [on_device(): qs_hi = lax.ppermute(q_side, 'ha', down)]
    ppermute x1, waiting for transfers between devices: 4.26 us -> 0.01 us  [on_device(): qs_lo = lax.ppermute(q_side, 'ha', up)]
    slice x0 -> x1, local copies, waits for them, and re-layouts: none -> 4.25 us  [on_device(): middle = kv[1]]
    pallas_call x1, Pallas kernels: 9.17 us -> 5.34 us  [final(): pl.pallas_call(functools.partial(final_kernel, [(f, len(a)) for f, a in p...]
  transfers between devices with their start and end apart: 15 -> 15, of which waited for: 4 -> 6; matrix products, arithmetic and copies ran while one was open for 2% -> 3% of each run, Pallas kernels for 58% -> 44%
where the time goes in v3:
time: 173 us; the launch traced here: 172 us
  Pallas kernels  81.5 us (47%)
  starting transfers between devices  40.4 us (23%)
  waiting for transfers between devices  31.2 us (18%)
  between operations  13.6 us (8%)
  local copies, waits for them, and re-layouts  5.67 us (3%)
    pallas_call x4, Pallas kernels, window(): pl.pallas_call(functools.partial(window_kernel, jobs, len(qs), len(kvs),...  60.4 us
    ppermute x2, starting transfers between devices, side_part(): lax.ppermute(s_hi, 'ha', up)  9.71 us
    pallas_call x1, Pallas kernels, far(): pl.pallas_call(functools.partial(far_kernel, tiles.shape[0], step), grid=...  9.63 us
    ppermute x2, waiting for transfers between devices, side_part(): lax.ppermute(s_lo, 'ha', down)  9.51 us
    ppermute x2, waiting for transfers between devices, side_return(): return (flags, lax.ppermute(merged, 'wa', across))  9.3 us
    ppermute x2, starting transfers between devices, side_return(): return (flags, lax.ppermute(merged, 'wa', across))  6.6 us
    ppermute x2, waiting for transfers between devices, side_part(): lax.ppermute(s_hi, 'ha', up)  6.57 us
    pallas_call x2, Pallas kernels, merge(): pl.pallas_call(functools.partial(merge_kernel, part_flags, len(after), st...  6.1 us
  transfers between devices with their start and end apart: 15, of which 6 were waited for; matrix products, arithmetic and copies ran while one was open for 3% of the time, Pallas kernels for 44%

profile of v3, /device:TPU:3, one launch (start us, length us, event | category | flops | bytes accessed | tf_op | source)
XLA Modules:
  0.0 172.2 jit_solution(4793714200307488375)
XLA Ops:
  7.2 3.0 %collective-permute-start = (bf16[384,1536]{1,0:T(8,128)(2,1)}, bf16[384,1536]{1,0:T(8,128)(2,1)}, u32[]{:S(2)}, u32[]{:S(2)}) collective-permute-start(bf16[384,1536]{1,0:T(8,128)(2,1)} %bitcast.18), channel_id=1, source_target_pairs={{1,2},{3,4},{5,6},{2,1},{4,3},{6,5},{9,10},{11,12},{13,14},{10,9},... | collective-permute-start | bytes 3538952 | tf_op jit(solution)/shard_map/ppermute | solution.py:285
  10.2 4.3 %collective-permute-start.2 = (bf16[384,1536]{1,0:T(8,128)(2,1)}, bf16[384,1536]{1,0:T(8,128)(2,1)}, u32[]{:S(2)}, u32[]{:S(2)}) collective-permute-start(bf16[384,1536]{1,0:T(8,128)(2,1)} %bitcast.19), channel_id=1, source_target_pairs={{0,8},{8,16},{16,24},{1,9},{9,17},{17,25},{2,10},{10,18},{18,26},{... | collective-permute-start | bytes 3538952 | tf_op jit(solution)/shard_map/ppermute | solution.py:286
  15.8 4.3 %fusion = (bf16[1,1,1,2,384,1536]{5,4,3,2,1,0:T(8,128)(2,1)}, bf16[2,384,1536]{2,1,0:T(8,128)(2,1)}) fusion(bf16[1,1,3,2,384,1536]{5,4,3,2,1,0:T(8,128)(2,1)} %param.4), kind=kLoop, calls=%fused_computation.1 | loop fusion | bytes 7077888 | tf_op jit(solution)/shard_map/slice | solution.py:288
  20.8 16.0 %own.1 = (f32[1728,384]{1,0:T(8,128)}, s32[8]{0:T(128)}) custom-call(s32[8]{0:T(128)} %stack.51.flags, bf16[2,384,1536]{2,1,0:T(8,128)(2,1)} %get-tuple-element.48.refs_0_, bf16[384,1536]{1,0:T(8,128)(2,1)} %bitcast.21, bf16[3,2,384,1536]{3,2,1,0:T(8,128)(2,1)} %bitcast.14, bf16[3,2,384,1536]{3,2,1,0:T(8,128)(2,1)} %collective-permute-done.1.refs_3_), custom_call_target="tpu_custom_call" | custom-call | flops 1000 | bytes 1000 | tf_op jit(solution)/shard_map/own/pallas_call | solution.py:121
  36.8 5.8 %collective-permute-done.refs_2_ = bf16[384,1536]{1,0:T(8,128)(2,1)} collective-permute-done((bf16[384,1536]{1,0:T(8,128)(2,1)}, bf16[384,1536]{1,0:T(8,128)(2,1)}, u32[]{:S(2)}, u32[]{:S(2)}) %collective-permute-start) | collective-permute-done | bytes 1179680 | tf_op jit(solution)/shard_map/ppermute | solution.py:285
  42.5 4.3 %collective-permute-start.4 = (bf16[384,1536]{1,0:T(8,128)(2,1)}, bf16[384,1536]{1,0:T(8,128)(2,1)}, u32[]{:S(2)}, u32[]{:S(2)}) collective-permute-start(bf16[384,1536]{1,0:T(8,128)(2,1)} %collective-permute-done.refs_2_), channel_id=1, source_target_pairs={{0,8},{8,16},{16,24},{1,9},{9,17},{17,25},{2,10},{10,18},{18,26},{... | collective-permute-start | bytes 3538952 | tf_op jit(solution)/shard_map/ppermute | solution.py:293
  48.1 22.5 %rows.1 = (bf16[1728,384]{1,0:T(8,128)(2,1)}, bf16[1728,384]{1,0:T(8,128)(2,1)}, s32[8]{0:T(128)}) custom-call(s32[8]{0:T(128)} %get-tuple-element.27.flags, bf16[384,1536]{1,0:T(8,128)(2,1)} %collective-permute-done.2.refs_0_, bf16[384,1536]{1,0:T(8,128)(2,1)} %collective-permute-done.3.refs_1_, bf16[3,2,384,1536]{3,2,1,0:T(8,128)(2,1)} %bitcast.15, ...), custom_call_target="tpu_custom_call" | custom-call | flops 9999999827968 | bytes 1000 | tf_op jit(solution)/shard_map/rows/pallas_call | solution.py:121
  70.6 5.2 %collective-permute-start.6 = (bf16[1728,384]{1,0:T(8,128)(2,1)}, bf16[1728,384]{1,0:T(8,128)(2,1)}, u32[]{:S(2)}, u32[]{:S(2)}) collective-permute-start(bf16[1728,384]{1,0:T(8,128)(2,1)} %get-tuple-element.32), channel_id=1, source_target_pairs={{0,8},{8,16},{16,24},{1,9},{9,17},{17,25},{2,10},{10,18},{18,26},{... | collective-permute-start | bytes 3981320 | tf_op jit(solution)/shard_map/ppermute | solution.py:311
  75.8 1.5 collective-permute-start.7
  77.3 11.0 %side.2 = (bf16[864,384]{1,0:T(8,128)(2,1)}, bf16[864,384]{1,0:T(8,128)(2,1)}, f32[864,384]{1,0:T(8,128)}, s32[8]{0:T(128)}) custom-call(s32[8]{0:T(128)} %get-tuple-element.28.flags, bf16[384,1536]{1,0:T(8,128)(2,1)} %collective-permute-done.4.refs_0_, bf16[384,1536]{1,0:T(8,128)(2,1)} %collective-permute-done.5.refs_1_, ...), custom_call_target="tpu_custom_call" | custom-call | flops 20000000000 | bytes 1000 | tf_op jit(solution)/shard_map/side/pallas_call | solution.py:121
  88.2 4.8 %collective-permute-start.8 = (bf16[864,384]{1,0:T(8,128)(2,1)}, bf16[864,384]{1,0:T(8,128)(2,1)}, u32[]{:S(2)}, u32[]{:S(2)}) collective-permute-start(bf16[864,384]{1,0:T(8,128)(2,1)} %get-tuple-element.35), channel_id=1, source_target_pairs={{0,8},{8,16},{16,24},{1,9},{9,17},{17,25},{2,10},{10,18},{18,26},{... | collective-permute-start | bytes 1990664 | tf_op jit(solution)/shard_map/ppermute | solution.py:302
  94.4 11.0 %side.3 = (bf16[864,384]{1,0:T(8,128)(2,1)}, bf16[864,384]{1,0:T(8,128)(2,1)}, f32[864,384]{1,0:T(8,128)}, s32[8]{0:T(128)}) custom-call(s32[8]{0:T(128)} %get-tuple-element.30.flags, bf16[384,1536]{1,0:T(8,128)(2,1)} %collective-permute-done.4.refs_0_, bf16[384,1536]{1,0:T(8,128)(2,1)} %collective-permute-done.5.refs_1_, ...), custom_call_target="tpu_custom_call" | custom-call | flops 1000 | bytes 1000 | tf_op jit(solution)/shard_map/side/pallas_call | solution.py:121
  105.4 4.9 %collective-permute-start.10 = (bf16[864,384]{1,0:T(8,128)(2,1)}, bf16[864,384]{1,0:T(8,128)(2,1)}, u32[]{:S(2)}, u32[]{:S(2)}) collective-permute-start(bf16[864,384]{1,0:T(8,128)(2,1)} %get-tuple-element.39), channel_id=1, source_target_pairs={{0,8},{8,16},{16,24},{1,9},{9,17},{17,25},{2,10},{10,18},{18,26},{... | collective-permute-start | bytes 1990664 | tf_op jit(solution)/shard_map/ppermute | solution.py:302
  111.6 6.6 %collective-permute-done.8.refs_3_ = bf16[864,384]{1,0:T(8,128)(2,1)} collective-permute-done((bf16[864,384]{1,0:T(8,128)(2,1)}, bf16[864,384]{1,0:T(8,128)(2,1)}, u32[]{:S(2)}, u32[]{:S(2)}) %collective-permute-start.8) | collective-permute-done | bytes 663584 | tf_op jit(solution)/shard_map/ppermute | solution.py:302
  118.1 5.3 %collective-permute-done.9.refs_4_ = bf16[864,384]{1,0:T(8,128)(2,1)} collective-permute-done((bf16[864,384]{1,0:T(8,128)(2,1)}, bf16[864,384]{1,0:T(8,128)(2,1)}, u32[]{:S(2)}, u32[]{:S(2)}) %collective-permute-start.9) | collective-permute-done | bytes 663584 | tf_op jit(solution)/shard_map/ppermute | solution.py:302
  123.4 3.0 %side_merge.2 = (bf16[864,384]{1,0:T(8,128)(2,1)}, s32[8]{0:T(128)}) custom-call(s32[8]{0:T(128)} %get-tuple-element.31.flags, bf16[1728,384]{1,0:T(8,128)(2,1)} %collective-permute-done.6.refs_0_.refs_2_, bf16[1728,384]{1,0:T(8,128)(2,1)} %collective-permute-done.7.refs_1_.refs_3_, f32[864,384]{1,0:T(8,128)} %get-tuple-element.34.refs_2_, ...), custom_call_target="tpu_custom_call" | custom-call | flops 1000 | bytes 1000 | tf_op jit(solution)/shard_map/side_merge/pallas_call | solution.py:161
  126.5 4.5 %collective-permute-start.12 = (bf16[864,384]{1,0:T(8,128)(2,1)}, bf16[864,384]{1,0:T(8,128)(2,1)}, u32[]{:S(2)}, u32[]{:S(2)}) collective-permute-start(bf16[864,384]{1,0:T(8,128)(2,1)} %get-tuple-element.42), channel_id=1, source_target_pairs={{1,2},{3,4},{5,6},{2,1},{4,3},{6,5},{9,10},{11,12},{13,14},{10,9},... | collective-permute-start | bytes 1990664 | tf_op jit(solution)/shard_map/ppermute | solution.py:306
  131.7 4.2 %collective-permute-done.11.refs_2_ = bf16[864,384]{1,0:T(8,128)(2,1)} collective-permute-done((bf16[864,384]{1,0:T(8,128)(2,1)}, bf16[864,384]{1,0:T(8,128)(2,1)}, u32[]{:S(2)}, u32[]{:S(2)}) %collective-permute-start.11) | collective-permute-done | bytes 663584 | tf_op jit(solution)/shard_map/ppermute | solution.py:302
  135.9 3.1 %side_merge.3 = (bf16[864,384]{1,0:T(8,128)(2,1)}, s32[8]{0:T(128)}) custom-call(s32[8]{0:T(128)} %get-tuple-element.37.flags, f32[864,384]{1,0:T(8,128)} %get-tuple-element.38.refs_0_, bf16[864,384]{1,0:T(8,128)(2,1)} %collective-permute-done.10.refs_1_, bf16[864,384]{1,0:T(8,128)(2,1)} %collective-permute-done.11.refs_2_), custom_call_target="tpu_custom_call" | custom-call | flops 1000 | bytes 1000 | tf_op jit(solution)/shard_map/side_merge/pallas_call | solution.py:161
  139.0 2.1 %collective-permute-start.13 = (bf16[864,384]{1,0:T(8,128)(2,1)}, bf16[864,384]{1,0:T(8,128)(2,1)}, u32[]{:S(2)}, u32[]{:S(2)}) collective-permute-start(bf16[864,384]{1,0:T(8,128)(2,1)} %get-tuple-element.46), channel_id=1, source_target_pairs={{1,2},{3,4},{5,6},{2,1},{4,3},{6,5},{9,10},{11,12},{13,14},{10,9},... | collective-permute-start | bytes 1990664 | tf_op jit(solution)/shard_map/ppermute | solution.py:306
  141.1 5.6 %collective-permute-done.12._.refs_4_ = bf16[864,384]{1,0:T(8,128)(2,1)} collective-permute-done((bf16[864,384]{1,0:T(8,128)(2,1)}, bf16[864,384]{1,0:T(8,128)(2,1)}, u32[]{:S(2)}, u32[]{:S(2)}) %collective-permute-start.12) | collective-permute-done | bytes 663584 | tf_op jit(solution)/shard_map/ppermute | solution.py:306
  146.8 9.6 %far.1 = (f32[1728,384]{1,0:T(8,128)}, s32[8]{0:T(128)}) custom-call(s32[8]{0:T(128)} %get-tuple-element.41.flags, s32[24]{0:T(128)} %reshape.16.offsets, bf16[384,1536]{1,0:T(8,128)(2,1)} %bitcast.22, bf16[8,2,384,1536]{3,2,1,0:T(8,128)(2,1)} %bitcast.23, bf16[864,384]{1,0:T(8,128)(2,1)} %collective-permute-done.12._.refs_4_), custom_call_target="tpu_custom_call" | custom-call | flops 9999999827968 | bytes 1000 | tf_op jit(solution)/shard_map/far/pallas_call | solution.py:206
  156.4 3.7 %collective-permute-done.13.refs_5_ = bf16[864,384]{1,0:T(8,128)(2,1)} collective-permute-done((bf16[864,384]{1,0:T(8,128)(2,1)}, bf16[864,384]{1,0:T(8,128)(2,1)}, u32[]{:S(2)}, u32[]{:S(2)}) %collective-permute-start.13) | collective-permute-done | bytes 663584 | tf_op jit(solution)/shard_map/ppermute | solution.py:306
  160.1 5.3 %final.1 = bf16[384,1536]{1,0:T(8,128)(2,1)} custom-call(s32[8]{0:T(128)} %get-tuple-element.43.flags, f32[1728,384]{1,0:T(8,128)} %get-tuple-element.44.refs_0_, f32[1728,384]{1,0:T(8,128)} %get-tuple-element.45.refs_1_, bf16[1728,384]{1,0:T(8,128)(2,1)} %collective-permute-done.6.refs_0_.refs_2_, bf16[1728,384]{1,0:T(8,128)(2,1)} %collective-permute-done.7.refs_1_.refs_3_, ...), custom_call_target="tpu_custom_call" | custom-call | flops 1000 | bytes 1000 | tf_op jit(solution)/shard_map/final/pallas_call | solution.py:254
  (21 shorter events, 7.2 us)
Async XLA Ops:
  6.5 140.2 %all-gather.3.cloned.1.call-start = ((), (), s32[]{:S(2)}) async-start(), calls=%async_computation | async-start | bytes 21233664 | tf_op jit(solution)/shard_map/all_gather | solution.py:291
  6.5 14.3 %collective-permute-start.1 = (bf16[3,2,384,1536]{3,2,1,0:T(8,128)(2,1)}, bf16[3,2,384,1536]{3,2,1,0:T(8,128)(2,1)}, u32[]{:S(2)}, u32[]{:S(2)}) collective-permute-start(bf16[3,2,384,1536]{3,2,1,0:T(8,128)(2,1)} %bitcast.13), channel_id=1, source_target_pairs={{0,1},{1,0},{2,3},{3,2},{4,5},{5,4},{6,7},{7,6},{8,9},{9,8},{10,11... | collective-permute-start | bytes 21233672 | tf_op jit(solution)/shard_map/ppermute | solution.py:284
  7.2 35.3 %collective-permute-start = (bf16[384,1536]{1,0:T(8,128)(2,1)}, bf16[384,1536]{1,0:T(8,128)(2,1)}, u32[]{:S(2)}, u32[]{:S(2)}) collective-permute-start(bf16[384,1536]{1,0:T(8,128)(2,1)} %bitcast.18), channel_id=1, source_target_pairs={{1,2},{3,4},{5,6},{2,1},{4,3},{6,5},{9,10},{11,12},{13,14},{10,9},... | collective-permute-start | bytes 3538952 | tf_op jit(solution)/shard_map/ppermute | solution.py:285
  10.2 37.9 %collective-permute-start.2 = (bf16[384,1536]{1,0:T(8,128)(2,1)}, bf16[384,1536]{1,0:T(8,128)(2,1)}, u32[]{:S(2)}, u32[]{:S(2)}) collective-permute-start(bf16[384,1536]{1,0:T(8,128)(2,1)} %bitcast.19), channel_id=1, source_target_pairs={{0,8},{8,16},{16,24},{1,9},{9,17},{17,25},{2,10},{10,18},{18,26},{... | collective-permute-start | bytes 3538952 | tf_op jit(solution)/shard_map/ppermute | solution.py:286
  14.5 33.6 %collective-permute-start.3 = (bf16[384,1536]{1,0:T(8,128)(2,1)}, bf16[384,1536]{1,0:T(8,128)(2,1)}, u32[]{:S(2)}, u32[]{:S(2)}) collective-permute-start(bf16[384,1536]{1,0:T(8,128)(2,1)} %bitcast.20), channel_id=1, source_target_pairs={{8,0},{16,8},{24,16},{9,1},{17,9},{25,17},{10,2},{18,10},{26,18},{... | collective-permute-start | bytes 3538952 | tf_op jit(solution)/shard_map/ppermute | solution.py:287
  42.5 34.7 %collective-permute-start.4 = (bf16[384,1536]{1,0:T(8,128)(2,1)}, bf16[384,1536]{1,0:T(8,128)(2,1)}, u32[]{:S(2)}, u32[]{:S(2)}) collective-permute-start(bf16[384,1536]{1,0:T(8,128)(2,1)} %collective-permute-done.refs_2_), channel_id=1, source_target_pairs={{0,8},{8,16},{16,24},{1,9},{9,17},{17,25},{2,10},{10,18},{18,26},{... | collective-permute-start | bytes 3538952 | tf_op jit(solution)/shard_map/ppermute | solution.py:293
  46.8 30.4 %collective-permute-start.5 = (bf16[384,1536]{1,0:T(8,128)(2,1)}, bf16[384,1536]{1,0:T(8,128)(2,1)}, u32[]{:S(2)}, u32[]{:S(2)}) collective-permute-start(bf16[384,1536]{1,0:T(8,128)(2,1)} %collective-permute-done.refs_2_), channel_id=1, source_target_pairs={{8,0},{16,8},{24,16},{9,1},{17,9},{25,17},{10,2},{18,10},{26,18},{... | collective-permute-start | bytes 3538952 | tf_op jit(solution)/shard_map/ppermute | solution.py:294
  70.6 39.7 %collective-permute-start.6 = (bf16[1728,384]{1,0:T(8,128)(2,1)}, bf16[1728,384]{1,0:T(8,128)(2,1)}, u32[]{:S(2)}, u32[]{:S(2)}) collective-permute-start(bf16[1728,384]{1,0:T(8,128)(2,1)} %get-tuple-element.32), channel_id=1, source_target_pairs={{0,8},{8,16},{16,24},{1,9},{9,17},{17,25},{2,10},{10,18},{18,26},{... | collective-permute-start | bytes 3981320 | tf_op jit(solution)/shard_map/ppermute | solution.py:311
  75.8 35.8 %collective-permute-start.7 = (bf16[1728,384]{1,0:T(8,128)(2,1)}, bf16[1728,384]{1,0:T(8,128)(2,1)}, u32[]{:S(2)}, u32[]{:S(2)}) collective-permute-start(bf16[1728,384]{1,0:T(8,128)(2,1)} %get-tuple-element.33), channel_id=1, source_target_pairs={{8,0},{16,8},{24,16},{9,1},{17,9},{25,17},{10,2},{18,10},{26,18},{... | collective-permute-start | bytes 3981320 | tf_op jit(solution)/shard_map/ppermute | solution.py:312
  88.2 29.9 %collective-permute-start.8 = (bf16[864,384]{1,0:T(8,128)(2,1)}, bf16[864,384]{1,0:T(8,128)(2,1)}, u32[]{:S(2)}, u32[]{:S(2)}) collective-permute-start(bf16[864,384]{1,0:T(8,128)(2,1)} %get-tuple-element.35), channel_id=1, source_target_pairs={{0,8},{8,16},{16,24},{1,9},{9,17},{17,25},{2,10},{10,18},{18,26},{... | collective-permute-start | bytes 1990664 | tf_op jit(solution)/shard_map/ppermute | solution.py:302
  93.1 30.3 %collective-permute-start.9 = (bf16[864,384]{1,0:T(8,128)(2,1)}, bf16[864,384]{1,0:T(8,128)(2,1)}, u32[]{:S(2)}, u32[]{:S(2)}) collective-permute-start(bf16[864,384]{1,0:T(8,128)(2,1)} %get-tuple-element.36), channel_id=1, source_target_pairs={{8,0},{16,8},{24,16},{9,1},{17,9},{25,17},{10,2},{18,10},{26,18},{... | collective-permute-start | bytes 1990664 | tf_op jit(solution)/shard_map/ppermute | solution.py:302
  105.4 26.3 %collective-permute-start.10 = (bf16[864,384]{1,0:T(8,128)(2,1)}, bf16[864,384]{1,0:T(8,128)(2,1)}, u32[]{:S(2)}, u32[]{:S(2)}) collective-permute-start(bf16[864,384]{1,0:T(8,128)(2,1)} %get-tuple-element.39), channel_id=1, source_target_pairs={{0,8},{8,16},{16,24},{1,9},{9,17},{17,25},{2,10},{10,18},{18,26},{... | collective-permute-start | bytes 1990664 | tf_op jit(solution)/shard_map/ppermute | solution.py:302
  110.3 25.6 %collective-permute-start.11 = (bf16[864,384]{1,0:T(8,128)(2,1)}, bf16[864,384]{1,0:T(8,128)(2,1)}, u32[]{:S(2)}, u32[]{:S(2)}) collective-permute-start(bf16[864,384]{1,0:T(8,128)(2,1)} %get-tuple-element.40), channel_id=1, source_target_pairs={{8,0},{16,8},{24,16},{9,1},{17,9},{25,17},{10,2},{18,10},{26,18},{... | collective-permute-start | bytes 1990664 | tf_op jit(solution)/shard_map/ppermute | solution.py:302
  123.4 7.5 %copy-start = (s32[1,1,12,2]{2,3,1,0:T(2,128)S(1)}, s32[1,1,12,2]{2,3,1,0:T(2,128)}, u32[]{:S(2)}) copy-start(s32[1,1,12,2]{2,3,1,0:T(2,128)} %param.5) | copy-start | bytes 292
  126.5 20.3 %collective-permute-start.12 = (bf16[864,384]{1,0:T(8,128)(2,1)}, bf16[864,384]{1,0:T(8,128)(2,1)}, u32[]{:S(2)}, u32[]{:S(2)}) collective-permute-start(bf16[864,384]{1,0:T(8,128)(2,1)} %get-tuple-element.42), channel_id=1, source_target_pairs={{1,2},{3,4},{5,6},{2,1},{4,3},{6,5},{9,10},{11,12},{13,14},{10,9},... | collective-permute-start | bytes 1990664 | tf_op jit(solution)/shard_map/ppermute | solution.py:306
  139.0 21.1 %collective-permute-start.13 = (bf16[864,384]{1,0:T(8,128)(2,1)}, bf16[864,384]{1,0:T(8,128)(2,1)}, u32[]{:S(2)}, u32[]{:S(2)}) collective-permute-start(bf16[864,384]{1,0:T(8,128)(2,1)} %get-tuple-element.46), channel_id=1, source_target_pairs={{1,2},{3,4},{5,6},{2,1},{4,3},{6,5},{9,10},{11,12},{13,14},{10,9},... | collective-permute-start | bytes 1990664 | tf_op jit(solution)/shard_map/ppermute | solution.py:306
Sparse Core Ops, SparseCore 0:
  20.2 104.5 all-gather.2

commit v4 on v3

--- a/solution.py
+++ b/solution.py
@@ -155,37 +155,40 @@
         )
 
 
-def merge(name, flags, parts, part_flags, nh, step, after=()):
+def merge(name, flags, own, h0, parts, part_flags, nh, step, flops, after):
     smem = pl.BlockSpec(memory_space=pltpu.SMEM)
     block = pl.BlockSpec((step * BLOCK, TILE), lambda h: (h, 0))
     res = pl.pallas_call(
         functools.partial(merge_kernel, part_flags, len(after), step),
         grid=(nh // step,),
-        in_specs=[smem] + [pl.BlockSpec(memory_space=pl.ANY)] * len(after) + [block] * len(parts),
+        in_specs=[smem] + [pl.BlockSpec(memory_space=pl.ANY)] * len(after)
+        + [pl.BlockSpec((step * BLOCK, TILE), lambda h: (h + h0 // step, 0))]
+        + [block] * len(parts),
         out_specs=[block, smem],
         out_shape=[
             jax.ShapeDtypeStruct((nh * BLOCK, TILE), BF),
             jax.ShapeDtypeStruct(flags.shape, flags.dtype),
         ],
         compiler_params=pltpu.CompilerParams(vmem_limit_bytes=VMEM),
-        cost_estimate=pl.CostEstimate(flops=1000, bytes_accessed=1000, transcendentals=0),
+        cost_estimate=pl.CostEstimate(flops=flops, bytes_accessed=1000, transcendentals=0),
         name=name,
-    )(flags, *after, *parts)
+    )(flags, *after, own, *parts)
     return res[1], res[0]
 
 
-def far_kernel(width, heads, flags, offsets, q_ref, tiles, _, out_ref, token, buffer, sems):
+def far_kernel(width, h0, nh, heads, flags, offsets, q_ref, tiles, *refs):
+    out_ref, token, buffer, sems = refs[-4:]
     step = pl.program_id(0)
     pass_flags(flags, token)
 
     def copy(i):
-        owner = lax.rem(flags[6] + 1 + offsets[i], width)
-        cols = pl.ds(pl.multiple_of(i // FAR * HD, HD), HD)
+        owner = lax.rem(flags[6] + 1 + offsets[h0 * FAR + i], width)
+        cols = pl.ds(pl.multiple_of(h0 * HD + i // FAR * HD, HD), HD)
         return pltpu.make_async_copy(tiles.at[owner, :, :, cols], buffer.at[i], sems.at[i])
 
     @pl.when(step == 0)
     def _():
-        @pl.loop(0, HEADS * FAR)
+        @pl.loop(0, nh * FAR)
         def _(i):
             copy(i).start()
 
@@ -201,66 +204,60 @@
     attend_all(heads, 1, get, lambda head, _, out, log: write_part(out_ref, head, out, log))
 
 
-def far(flags, offsets, q, tiles, step, after):
+def far(flags, offsets, q, tiles, h0, nh, step, flops, after):
     smem = pl.BlockSpec(memory_space=pltpu.SMEM)
     res = pl.pallas_call(
-        functools.partial(far_kernel, tiles.shape[0], step),
-        grid=(HEADS // step,),
+        functools.partial(far_kernel, tiles.shape[0], h0, nh, step),
+        grid=(nh // step,),
         in_specs=[
-            smem, smem, pl.BlockSpec((TILE, step * HD), lambda h: (0, h))
-        ] + [pl.BlockSpec(memory_space=pl.ANY)] * 2,
+            smem, smem, pl.BlockSpec((TILE, step * HD), lambda h: (0, h + h0 // step))
+        ] + [pl.BlockSpec(memory_space=pl.ANY)] * (1 + len(after)),
         out_specs=[pl.BlockSpec((step * BLOCK, TILE), lambda h: (h, 0)), smem],
         out_shape=[
-            jax.ShapeDtypeStruct((HEADS * BLOCK, TILE), F32),
+            jax.ShapeDtypeStruct((nh * BLOCK, TILE), F32),
             jax.ShapeDtypeStruct(flags.shape, flags.dtype),
         ],
         scratch_shapes=[
-            pltpu.VMEM((HEADS * FAR, 2, TILE, HD), BF),
-            pltpu.SemaphoreType.DMA((HEADS * FAR,)),
+            pltpu.VMEM((nh * FAR, 2, TILE, HD), BF),
+            pltpu.SemaphoreType.DMA((nh * FAR,)),
         ],
         compiler_params=pltpu.CompilerParams(vmem_limit_bytes=VMEM),
-        cost_estimate=pl.CostEstimate(flops=10**13, bytes_accessed=1000, transcendentals=0),
+        cost_estimate=pl.CostEstimate(flops=flops, bytes_accessed=1000, transcendentals=0),
         name="far",
-    )(flags, offsets, q, tiles, after)
+    )(flags, offsets, q, tiles, *after)
     return res[1], res[0]
 
 
-def final_kernel(part_specs, heads, flags, *refs):
-    arrays, out_ref = refs[:-1], refs[-1]
-    step = pl.program_id(0)
+def final_kernel(part_flags, heads, flags, *refs):
+    n = len(part_flags)
+    arrays, out_ref, token = refs[:n], refs[-2], refs[-1]
+    pass_flags(flags, token)
     for head in range(heads):
-        parts, place = [], 0
-        for flag, groups in part_specs:
-            per = HEADS // groups // heads
-            part = read_part(arrays[place], head)
-            for g in range(1, groups):
-                later = read_part(arrays[place + g], head)
-                part = tuple(jnp.where(step >= g * per, a, b) for a, b in zip(later, part))
-            place += groups
-            parts.append(masked(part, flags[flag]))
+        parts = [masked(read_part(a, head), flags[f]) for a, f in zip(arrays, part_flags)]
         out_ref[:, lanes(head)] = merge_parts(parts)[0].T.astype(out_ref.dtype)
 
 
-def final(flags, parts, step):
-    specs, arrays = [], []
-    for _, group_arrays in parts:
-        per = HEADS // len(group_arrays) // step
-        for g, array in enumerate(group_arrays):
-            index = functools.partial(
-                lambda h, low, top: (jnp.clip(h - low, 0, top), 0), low=g * per, top=per - 1
-            )
-            specs.append(pl.BlockSpec((step * BLOCK, TILE), index))
-            arrays.append(array)
+def final(flags, parts, h0, nh, step, out):
+    smem = pl.BlockSpec(memory_space=pltpu.SMEM)
+    specs = [
+        pl.BlockSpec((step * BLOCK, TILE), functools.partial(lambda h, d: (h + d, 0), d=(h0 - base) // step))
+        for _, base, _ in parts
+    ]
+    before = [] if out is None else [out]
     return pl.pallas_call(
-        functools.partial(final_kernel, [(f, len(a)) for f, a in parts], step),
-        grid=(HEADS // step,),
-        in_specs=[pl.BlockSpec(memory_space=pltpu.SMEM)] + specs,
-        out_specs=pl.BlockSpec((TILE, step * HD), lambda h: (0, h)),
-        out_shape=jax.ShapeDtypeStruct((TILE, HEADS * HD), BF),
+        functools.partial(final_kernel, [f for f, _, _ in parts], step),
+        grid=(nh // step,),
+        in_specs=[smem] + specs + [pl.BlockSpec(memory_space=pl.ANY)] * len(before),
+        out_specs=[pl.BlockSpec((TILE, step * HD), lambda h: (0, h + h0 // step)), smem],
+        out_shape=[
+            jax.ShapeDtypeStruct((TILE, HEADS * HD), BF),
+            jax.ShapeDtypeStruct(flags.shape, flags.dtype),
+        ],
+        input_output_aliases={} if out is None else {1 + len(parts): 0},
         compiler_params=pltpu.CompilerParams(vmem_limit_bytes=VMEM),
         cost_estimate=pl.CostEstimate(flops=1000, bytes_accessed=1000, transcendentals=0),
         name="final",
-    )(flags, *arrays)
+    )(flags, *[a for _, _, a in parts], *before)
 
 
 def on_device(queries, keys_values, far_offsets):
@@ -293,16 +290,16 @@
     qs_lo = lax.ppermute(q_side, "ha", up)
     qs_hi = lax.ppermute(q_side, "ha", down)
 
-    def side_part(flags, g, flops):
-        per = HEADS // SIDE_GROUPS
-        flags, (s_lo, s_hi, s_own) = window(
-            "side", flags, [qs_lo, qs_hi, q_side], [kv], [(0, (0,)), (1, (0,)), (2, (0,))],
-            g * per, per, [BF, BF, F32], 3, 2, flops,
+    per = HEADS // SIDE_GROUPS
+
+    def side_rows(flags, g, flops):
+        flags, (s_lo, s_hi) = window(
+            "side_rows", flags, [qs_lo, qs_hi], [kv], [(0, (0,)), (1, (0,))], g * per, per, [BF, BF], 2, 2, flops
         )
-        return flags, [s_own, lax.ppermute(s_hi, "ha", up), lax.ppermute(s_lo, "ha", down)]
-
-    def side_return(flags, parts, after):
-        flags, merged = merge("side_merge", flags, parts, [3, 4, 5], HEADS // SIDE_GROUPS, 6, after)
+        return flags, [lax.ppermute(s_hi, "ha", up), lax.ppermute(s_lo, "ha", down)]
+
+    def side_return(flags, g, parts, flops, after):
+        flags, merged = merge("side_merge", flags, s_own, g * per, parts, [3, 4, 5], per, 6, flops, after)
         return flags, lax.ppermute(merged, "wa", across)
 
     flags, (o_lo, o_hi) = window(
@@ -310,14 +307,22 @@
     )
     from_lo = lax.ppermute(o_hi, "ha", up)
     from_hi = lax.ppermute(o_lo, "ha", down)
-    flags, first = side_part(flags, 0, 2 * 10**10)
-    flags, second = side_part(flags, 1, 1000)
-    flags, first = side_return(flags, first, [from_lo, from_hi])
-    flags, second = side_return(flags, second, [])
-    flags, far_part = far(flags, far_offsets.reshape(-1), q, tiles, 3, first)
-    out = final(
-        flags, [(0, [own]), (0, [far_part]), (1, [from_lo]), (2, [from_hi]), (3, [first, second])], 6
-    )
+    flags, first = side_rows(flags, 0, 2 * 10**10)
+    flags, second = side_rows(flags, 1, 1000)
+    flags, (s_own,) = window("side_own", flags, [q_side], [kv], [(0, (0,))], 0, HEADS, [F32], 1, 3)
+    flags, first = side_return(flags, 0, first, 1000, [from_lo, from_hi])
+    flags, second = side_return(flags, 1, second, 3 * 10**10, [])
+    offsets = far_offsets.reshape(-1)
+    flags, far_first = far(flags, offsets, q, tiles, 0, per, 3, 1000, [])
+    flags, far_second = far(flags, offsets, q, tiles, per, per, 3, 10**13, [first])
+    out = None
+    for g, (side_merged, far_part) in enumerate([(first, far_first), (second, far_second)]):
+        low = g * per
+        out, flags = final(
+            flags,
+            [(0, 0, own), (0, low, far_part), (1, 0, from_lo), (2, 0, from_hi), (3, low, side_merged)],
+            low, per, 3, out,
+        )
     return out.reshape(queries.shape)
 
 

time: 173 us -> 171 us (0.988)
  waiting for transfers between devices: 31.2 us -> 21.1 us
  Pallas kernels: 81.5 us -> 90 us
    ppermute x2, waiting for transfers between devices: 9.3 us -> 2.55 us  [side_return(): return (flags, lax.ppermute(merged, 'wa', across))]
    pallas_call x2 -> x4, Pallas kernels: 15 us -> 19.7 us  [the longest x2 12.9 us: far(): pl.pallas_call(functools.partial(far_kernel, tiles.shape[0], h0, nh, step...]
    ppermute x4, waiting for transfers between devices: 16.1 us -> 12.1 us  [the longest x2 10.2 us: side_rows(): lax.ppermute(s_lo, 'ha', down)]
    pallas_call x4 -> x5, Pallas kernels: 60.4 us -> 64.2 us  [window(): pl.pallas_call(functools.partial(window_kernel, jobs, len(qs), len(kvs),...]
  transfers between devices with their start and end apart: 15 -> 15, of which waited for: 6 -> 6; matrix products, arithmetic and copies ran while one was open for 3% -> 3% of each run, Pallas kernels for 44% -> 51%
where the time goes in v4:
time: 171 us; the launch traced here: 170 us
  Pallas kernels  90 us (53%)
  starting transfers between devices  40.1 us (23%)
  waiting for transfers between devices  21.1 us (12%)
  between operations  13.6 us (8%)
  local copies, waits for them, and re-layouts  5.53 us (3%)
    pallas_call x5, Pallas kernels, window(): pl.pallas_call(functools.partial(window_kernel, jobs, len(qs), len(kvs),...  64.2 us
    pallas_call x2, Pallas kernels, far(): pl.pallas_call(functools.partial(far_kernel, tiles.shape[0], h0, nh, step...  12.9 us
    ppermute x2, waiting for transfers between devices, side_rows(): lax.ppermute(s_lo, 'ha', down)  10.2 us
    ppermute x2, starting transfers between devices, side_rows(): lax.ppermute(s_hi, 'ha', up)  9.64 us
    pallas_call x2, Pallas kernels, final(): pl.pallas_call(functools.partial(final_kernel, [f for f, _, _ in parts],...  6.88 us
    ppermute x2, starting transfers between devices, side_return(): return (flags, lax.ppermute(merged, 'wa', across))  6.6 us
    ppermute x1, waiting for transfers between devices, on_device(): q_side = lax.ppermute(q, 'wa', across)  6.12 us
    pallas_call x2, Pallas kernels, merge(): pl.pallas_call(functools.partial(merge_kernel, part_flags, len(after), st...  6.11 us
  transfers between devices with their start and end apart: 15, of which 6 were waited for; matrix products, arithmetic and copies ran while one was open for 3% of the time, Pallas kernels for 51%

profile of v4, /device:TPU:3, one launch (start us, length us, event | category | flops | bytes accessed | tf_op | source)
XLA Modules:
  0.0 170.4 jit_solution(5714165623145186660)
XLA Ops:
  7.2 3.0 %collective-permute-start = (bf16[384,1536]{1,0:T(8,128)(2,1)}, bf16[384,1536]{1,0:T(8,128)(2,1)}, u32[]{:S(2)}, u32[]{:S(2)}) collective-permute-start(bf16[384,1536]{1,0:T(8,128)(2,1)} %bitcast.21), channel_id=1, source_target_pairs={{1,2},{3,4},{5,6},{2,1},{4,3},{6,5},{9,10},{11,12},{13,14},{10,9},... | collective-permute-start | bytes 3538952 | tf_op jit(solution)/shard_map/ppermute | solution.py:282
  10.2 4.2 %collective-permute-start.2 = (bf16[384,1536]{1,0:T(8,128)(2,1)}, bf16[384,1536]{1,0:T(8,128)(2,1)}, u32[]{:S(2)}, u32[]{:S(2)}) collective-permute-start(bf16[384,1536]{1,0:T(8,128)(2,1)} %bitcast.22), channel_id=1, source_target_pairs={{0,8},{8,16},{16,24},{1,9},{9,17},{17,25},{2,10},{10,18},{18,26},{... | collective-permute-start | bytes 3538952 | tf_op jit(solution)/shard_map/ppermute | solution.py:283
  15.7 4.1 %fusion = (bf16[1,1,1,2,384,1536]{5,4,3,2,1,0:T(8,128)(2,1)}, bf16[2,384,1536]{2,1,0:T(8,128)(2,1)}) fusion(bf16[1,1,3,2,384,1536]{5,4,3,2,1,0:T(8,128)(2,1)} %param.4), kind=kLoop, calls=%fused_computation.1 | loop fusion | bytes 7077888 | tf_op jit(solution)/shard_map/slice | solution.py:285
  20.6 16.0 %own.1 = (f32[1728,384]{1,0:T(8,128)}, s32[8]{0:T(128)}) custom-call(s32[8]{0:T(128)} %stack.51.flags, bf16[2,384,1536]{2,1,0:T(8,128)(2,1)} %get-tuple-element.58.refs_0_, bf16[384,1536]{1,0:T(8,128)(2,1)} %bitcast.24, bf16[3,2,384,1536]{3,2,1,0:T(8,128)(2,1)} %bitcast.14, bf16[3,2,384,1536]{3,2,1,0:T(8,128)(2,1)} %collective-permute-done.1.refs_3_), custom_call_target="tpu_custom_call" | custom-call | flops 1000 | bytes 1000 | tf_op jit(solution)/shard_map/own/pallas_call | solution.py:121
  36.6 6.1 %collective-permute-done.refs_0_ = bf16[384,1536]{1,0:T(8,128)(2,1)} collective-permute-done((bf16[384,1536]{1,0:T(8,128)(2,1)}, bf16[384,1536]{1,0:T(8,128)(2,1)}, u32[]{:S(2)}, u32[]{:S(2)}) %collective-permute-start) | collective-permute-done | bytes 1179680 | tf_op jit(solution)/shard_map/ppermute | solution.py:282
  42.7 4.3 %collective-permute-start.4 = (bf16[384,1536]{1,0:T(8,128)(2,1)}, bf16[384,1536]{1,0:T(8,128)(2,1)}, u32[]{:S(2)}, u32[]{:S(2)}) collective-permute-start(bf16[384,1536]{1,0:T(8,128)(2,1)} %collective-permute-done.refs_0_), channel_id=1, source_target_pairs={{0,8},{8,16},{16,24},{1,9},{9,17},{17,25},{2,10},{10,18},{18,26},{... | collective-permute-start | bytes 3538952 | tf_op jit(solution)/shard_map/ppermute | solution.py:290
  48.3 22.4 %rows.1 = (bf16[1728,384]{1,0:T(8,128)(2,1)}, bf16[1728,384]{1,0:T(8,128)(2,1)}, s32[8]{0:T(128)}) custom-call(s32[8]{0:T(128)} %get-tuple-element.32.flags, bf16[384,1536]{1,0:T(8,128)(2,1)} %collective-permute-done.2.refs_0_, bf16[384,1536]{1,0:T(8,128)(2,1)} %collective-permute-done.3.refs_1_, bf16[3,2,384,1536]{3,2,1,0:T(8,128)(2,1)} %bitcast.15, ...), custom_call_target="tpu_custom_call" | custom-call | flops 9999999827968 | bytes 1000 | tf_op jit(solution)/shard_map/rows/pallas_call | solution.py:121
  70.7 5.1 %collective-permute-start.6 = (bf16[1728,384]{1,0:T(8,128)(2,1)}, bf16[1728,384]{1,0:T(8,128)(2,1)}, u32[]{:S(2)}, u32[]{:S(2)}) collective-permute-start(bf16[1728,384]{1,0:T(8,128)(2,1)} %get-tuple-element.38), channel_id=1, source_target_pairs={{0,8},{8,16},{16,24},{1,9},{9,17},{17,25},{2,10},{10,18},{18,26},{... | collective-permute-start | bytes 3981320 | tf_op jit(solution)/shard_map/ppermute | solution.py:308
  77.3 7.7 %side_rows.2 = (bf16[864,384]{1,0:T(8,128)(2,1)}, bf16[864,384]{1,0:T(8,128)(2,1)}, s32[8]{0:T(128)}) custom-call(s32[8]{0:T(128)} %get-tuple-element.33.flags, bf16[384,1536]{1,0:T(8,128)(2,1)} %collective-permute-done.4.refs_0_, bf16[384,1536]{1,0:T(8,128)(2,1)} %collective-permute-done.5.refs_1_, bf16[3,2,384,1536]{3,2,1,0:T(8,128)(2,1)} %bitcast.16), custom_call_target="tpu_custom_call" | custom-call | flops 20000000000 | bytes 1000 | tf_op jit(solution)/shard_map/side_rows/pallas_call | solution.py:121
  85.1 4.8 %collective-permute-start.8 = (bf16[864,384]{1,0:T(8,128)(2,1)}, bf16[864,384]{1,0:T(8,128)(2,1)}, u32[]{:S(2)}, u32[]{:S(2)}) collective-permute-start(bf16[864,384]{1,0:T(8,128)(2,1)} %get-tuple-element.41), channel_id=1, source_target_pairs={{0,8},{8,16},{16,24},{1,9},{9,17},{17,25},{2,10},{10,18},{18,26},{... | collective-permute-start | bytes 1990664 | tf_op jit(solution)/shard_map/ppermute | solution.py:299
  91.1 7.7 %side_rows.3 = (bf16[864,384]{1,0:T(8,128)(2,1)}, bf16[864,384]{1,0:T(8,128)(2,1)}, s32[8]{0:T(128)}) custom-call(s32[8]{0:T(128)} %get-tuple-element.35.flags, bf16[384,1536]{1,0:T(8,128)(2,1)} %collective-permute-done.4.refs_0_, bf16[384,1536]{1,0:T(8,128)(2,1)} %collective-permute-done.5.refs_1_, bf16[3,2,384,1536]{3,2,1,0:T(8,128)(2,1)} %bitcast.17), custom_call_target="tpu_custom_call" | custom-call | flops 1000 | bytes 1000 | tf_op jit(solution)/shard_map/side_rows/pallas_call | solution.py:121
  98.9 4.8 %collective-permute-start.10 = (bf16[864,384]{1,0:T(8,128)(2,1)}, bf16[864,384]{1,0:T(8,128)(2,1)}, u32[]{:S(2)}, u32[]{:S(2)}) collective-permute-start(bf16[864,384]{1,0:T(8,128)(2,1)} %get-tuple-element.44), channel_id=1, source_target_pairs={{0,8},{8,16},{16,24},{1,9},{9,17},{17,25},{2,10},{10,18},{18,26},{... | collective-permute-start | bytes 1990664 | tf_op jit(solution)/shard_map/ppermute | solution.py:299
  106.0 10.3 %side_own.1 = (f32[1728,384]{1,0:T(8,128)}, s32[8]{0:T(128)}) custom-call(s32[8]{0:T(128)} %get-tuple-element.36.flags, bf16[384,1536]{1,0:T(8,128)(2,1)} %collective-permute-done.refs_0_, bf16[3,2,384,1536]{3,2,1,0:T(8,128)(2,1)} %bitcast.18), custom_call_target="tpu_custom_call" | custom-call | flops 1000 | bytes 1000 | tf_op jit(solution)/shard_map/side_own/pallas_call | solution.py:121
  118.3 5.2 %collective-permute-done.9.refs_4_ = bf16[864,384]{1,0:T(8,128)(2,1)} collective-permute-done((bf16[864,384]{1,0:T(8,128)(2,1)}, bf16[864,384]{1,0:T(8,128)(2,1)}, u32[]{:S(2)}, u32[]{:S(2)}) %collective-permute-start.9) | collective-permute-done | bytes 663584 | tf_op jit(solution)/shard_map/ppermute | solution.py:299
  123.5 3.0 %side_merge.2 = (bf16[864,384]{1,0:T(8,128)(2,1)}, s32[8]{0:T(128)}) custom-call(s32[8]{0:T(128)} %get-tuple-element.37.flags, bf16[1728,384]{1,0:T(8,128)(2,1)} %collective-permute-done.6.refs_0_.refs_2_, bf16[1728,384]{1,0:T(8,128)(2,1)} %collective-permute-done.7.refs_1_.refs_3_, f32[1728,384]{1,0:T(8,128)} %get-tuple-element.40.refs_2_.refs_0_, ...), custom_call_target="tpu_custom_call" | custom-call | flops 1000 | bytes 1000 | tf_op jit(solution)/shard_map/side_merge/pallas_call | solution.py:161
  126.5 4.5 %collective-permute-start.12 = (bf16[864,384]{1,0:T(8,128)(2,1)}, bf16[864,384]{1,0:T(8,128)(2,1)}, u32[]{:S(2)}, u32[]{:S(2)}) collective-permute-start(bf16[864,384]{1,0:T(8,128)(2,1)} %get-tuple-element.48), channel_id=1, source_target_pairs={{1,2},{3,4},{5,6},{2,1},{4,3},{6,5},{9,10},{11,12},{13,14},{10,9},... | collective-permute-start | bytes 1990664 | tf_op jit(solution)/shard_map/ppermute | solution.py:303
  131.0 5.0 %collective-permute-done.11.refs_2_ = bf16[864,384]{1,0:T(8,128)(2,1)} collective-permute-done((bf16[864,384]{1,0:T(8,128)(2,1)}, bf16[864,384]{1,0:T(8,128)(2,1)}, u32[]{:S(2)}, u32[]{:S(2)}) %collective-permute-start.11) | collective-permute-done | bytes 663584 | tf_op jit(solution)/shard_map/ppermute | solution.py:299
  136.0 3.1 %side_merge.3 = (bf16[864,384]{1,0:T(8,128)(2,1)}, s32[8]{0:T(128)}) custom-call(s32[8]{0:T(128)} %get-tuple-element.43.flags, f32[1728,384]{1,0:T(8,128)} %get-tuple-element.40.refs_2_.refs_0_, bf16[864,384]{1,0:T(8,128)(2,1)} %collective-permute-done.10.refs_1_, bf16[864,384]{1,0:T(8,128)(2,1)} %collective-permute-done.11.refs_2_), custom_call_target="tpu_custom_call" | custom-call | flops 30000001024 | bytes 1000 | tf_op jit(solution)/shard_map/side_merge/pallas_call | solution.py:161
  139.1 2.1 %collective-permute-start.13 = (bf16[864,384]{1,0:T(8,128)(2,1)}, bf16[864,384]{1,0:T(8,128)(2,1)}, u32[]{:S(2)}, u32[]{:S(2)}) collective-permute-start(bf16[864,384]{1,0:T(8,128)(2,1)} %get-tuple-element.54), channel_id=1, source_target_pairs={{1,2},{3,4},{5,6},{2,1},{4,3},{6,5},{9,10},{11,12},{13,14},{10,9},... | collective-permute-start | bytes 1990664 | tf_op jit(solution)/shard_map/ppermute | solution.py:303
  141.2 6.4 %far.2 = (f32[864,384]{1,0:T(8,128)}, s32[8]{0:T(128)}) custom-call(s32[8]{0:T(128)} %get-tuple-element.46.flags, s32[24]{0:T(128)} %reshape.16.offsets, bf16[384,1536]{1,0:T(8,128)(2,1)} %bitcast.25, bf16[8,2,384,1536]{3,2,1,0:T(8,128)(2,1)} %bitcast.19), custom_call_target="tpu_custom_call" | custom-call | flops 1000 | bytes 1000 | tf_op jit(solution)/shard_map/far/pallas_call | solution.py:209
  147.7 6.4 %far.3 = (f32[864,384]{1,0:T(8,128)}, s32[8]{0:T(128)}) custom-call(s32[8]{0:T(128)} %get-tuple-element.47.flags, s32[24]{0:T(128)} %reshape.16.offsets, bf16[384,1536]{1,0:T(8,128)(2,1)} %bitcast.26, bf16[8,2,384,1536]{3,2,1,0:T(8,128)(2,1)} %bitcast.20, bf16[864,384]{1,0:T(8,128)(2,1)} %collective-permute-done.12.refs_0_.refs_4_), custom_call_target="tpu_custom_call" | custom-call | flops 9999999827968 | bytes 1000 | tf_op jit(solution)/shard_map/far/pallas_call | solution.py:209
  154.1 3.4 %final.2 = (bf16[384,1536]{1,0:T(8,128)(2,1)}, s32[8]{0:T(128)}) custom-call(s32[8]{0:T(128)} %get-tuple-element.49.flags, f32[1728,384]{1,0:T(8,128)} %get-tuple-element.50.refs_0_, f32[864,384]{1,0:T(8,128)} %get-tuple-element.51.refs_1_, bf16[1728,384]{1,0:T(8,128)(2,1)} %collective-permute-done.6.refs_0_.refs_2_, ...), custom_call_target="tpu_custom_call" | custom-call | flops 1000 | bytes 1000 | tf_op jit(solution)/shard_map/final/pallas_call | solution.py:247
  157.6 2.6 %collective-permute-done.13.refs_4_ = bf16[864,384]{1,0:T(8,128)(2,1)} collective-permute-done((bf16[864,384]{1,0:T(8,128)(2,1)}, bf16[864,384]{1,0:T(8,128)(2,1)}, u32[]{:S(2)}, u32[]{:S(2)}) %collective-permute-start.13) | collective-permute-done | bytes 663584 | tf_op jit(solution)/shard_map/ppermute | solution.py:303
  160.1 3.4 %final.3 = (bf16[384,1536]{1,0:T(8,128)(2,1)}, s32[8]{0:T(128)}) custom-call(s32[8]{0:T(128)} %get-tuple-element.52.flags, f32[1728,384]{1,0:T(8,128)} %get-tuple-element.50.refs_0_, f32[864,384]{1,0:T(8,128)} %get-tuple-element.53.refs_1_, bf16[1728,384]{1,0:T(8,128)(2,1)} %collective-permute-done.6.refs_0_.refs_2_, ...), custom_call_target="tpu_custom_call", output_to_operand_aliasing={{0}: (6, {})} | custom-call | flops 1000 | bytes 1000 | tf_op jit(solution)/shard_map/final/pallas_call | solution.py:247
  (24 shorter events, 10.9 us)
Async XLA Ops:
  6.5 134.7 %all-gather.3.cloned.1.call-start = ((), (), s32[]{:S(2)}) async-start(), calls=%async_computation | async-start | bytes 21233664 | tf_op jit(solution)/shard_map/all_gather | solution.py:288
  6.5 14.0 %collective-permute-start.1 = (bf16[3,2,384,1536]{3,2,1,0:T(8,128)(2,1)}, bf16[3,2,384,1536]{3,2,1,0:T(8,128)(2,1)}, u32[]{:S(2)}, u32[]{:S(2)}) collective-permute-start(bf16[3,2,384,1536]{3,2,1,0:T(8,128)(2,1)} %bitcast.13), channel_id=1, source_target_pairs={{0,1},{1,0},{2,3},{3,2},{4,5},{5,4},{6,7},{7,6},{8,9},{9,8},{10,11... | collective-permute-start | bytes 21233672 | tf_op jit(solution)/shard_map/ppermute | solution.py:281
  7.2 35.5 %collective-permute-start = (bf16[384,1536]{1,0:T(8,128)(2,1)}, bf16[384,1536]{1,0:T(8,128)(2,1)}, u32[]{:S(2)}, u32[]{:S(2)}) collective-permute-start(bf16[384,1536]{1,0:T(8,128)(2,1)} %bitcast.21), channel_id=1, source_target_pairs={{1,2},{3,4},{5,6},{2,1},{4,3},{6,5},{9,10},{11,12},{13,14},{10,9},... | collective-permute-start | bytes 3538952 | tf_op jit(solution)/shard_map/ppermute | solution.py:282
  10.2 38.1 %collective-permute-start.2 = (bf16[384,1536]{1,0:T(8,128)(2,1)}, bf16[384,1536]{1,0:T(8,128)(2,1)}, u32[]{:S(2)}, u32[]{:S(2)}) collective-permute-start(bf16[384,1536]{1,0:T(8,128)(2,1)} %bitcast.22), channel_id=1, source_target_pairs={{0,8},{8,16},{16,24},{1,9},{9,17},{17,25},{2,10},{10,18},{18,26},{... | collective-permute-start | bytes 3538952 | tf_op jit(solution)/shard_map/ppermute | solution.py:283
  14.4 33.9 %collective-permute-start.3 = (bf16[384,1536]{1,0:T(8,128)(2,1)}, bf16[384,1536]{1,0:T(8,128)(2,1)}, u32[]{:S(2)}, u32[]{:S(2)}) collective-permute-start(bf16[384,1536]{1,0:T(8,128)(2,1)} %bitcast.23), channel_id=1, source_target_pairs={{8,0},{16,8},{24,16},{9,1},{17,9},{25,17},{10,2},{18,10},{26,18},{... | collective-permute-start | bytes 3538952 | tf_op jit(solution)/shard_map/ppermute | solution.py:284
  42.7 34.6 %collective-permute-start.4 = (bf16[384,1536]{1,0:T(8,128)(2,1)}, bf16[384,1536]{1,0:T(8,128)(2,1)}, u32[]{:S(2)}, u32[]{:S(2)}) collective-permute-start(bf16[384,1536]{1,0:T(8,128)(2,1)} %collective-permute-done.refs_0_), channel_id=1, source_target_pairs={{0,8},{8,16},{16,24},{1,9},{9,17},{17,25},{2,10},{10,18},{18,26},{... | collective-permute-start | bytes 3538952 | tf_op jit(solution)/shard_map/ppermute | solution.py:290
  47.0 30.3 %collective-permute-start.5 = (bf16[384,1536]{1,0:T(8,128)(2,1)}, bf16[384,1536]{1,0:T(8,128)(2,1)}, u32[]{:S(2)}, u32[]{:S(2)}) collective-permute-start(bf16[384,1536]{1,0:T(8,128)(2,1)} %collective-permute-done.refs_0_), channel_id=1, source_target_pairs={{8,0},{16,8},{24,16},{9,1},{17,9},{25,17},{10,2},{18,10},{26,18},{... | collective-permute-start | bytes 3538952 | tf_op jit(solution)/shard_map/ppermute | solution.py:291
  70.7 33.3 %collective-permute-start.6 = (bf16[1728,384]{1,0:T(8,128)(2,1)}, bf16[1728,384]{1,0:T(8,128)(2,1)}, u32[]{:S(2)}, u32[]{:S(2)}) collective-permute-start(bf16[1728,384]{1,0:T(8,128)(2,1)} %get-tuple-element.38), channel_id=1, source_target_pairs={{0,8},{8,16},{16,24},{1,9},{9,17},{17,25},{2,10},{10,18},{18,26},{... | collective-permute-start | bytes 3981320 | tf_op jit(solution)/shard_map/ppermute | solution.py:308
  75.8 40.5 %collective-permute-start.7 = (bf16[1728,384]{1,0:T(8,128)(2,1)}, bf16[1728,384]{1,0:T(8,128)(2,1)}, u32[]{:S(2)}, u32[]{:S(2)}) collective-permute-start(bf16[1728,384]{1,0:T(8,128)(2,1)} %get-tuple-element.39), channel_id=1, source_target_pairs={{8,0},{16,8},{24,16},{9,1},{17,9},{25,17},{10,2},{18,10},{26,18},{... | collective-permute-start | bytes 3981320 | tf_op jit(solution)/shard_map/ppermute | solution.py:309
  85.1 33.2 %collective-permute-start.8 = (bf16[864,384]{1,0:T(8,128)(2,1)}, bf16[864,384]{1,0:T(8,128)(2,1)}, u32[]{:S(2)}, u32[]{:S(2)}) collective-permute-start(bf16[864,384]{1,0:T(8,128)(2,1)} %get-tuple-element.41), channel_id=1, source_target_pairs={{0,8},{8,16},{16,24},{1,9},{9,17},{17,25},{2,10},{10,18},{18,26},{... | collective-permute-start | bytes 1990664 | tf_op jit(solution)/shard_map/ppermute | solution.py:299
  89.8 33.6 %collective-permute-start.9 = (bf16[864,384]{1,0:T(8,128)(2,1)}, bf16[864,384]{1,0:T(8,128)(2,1)}, u32[]{:S(2)}, u32[]{:S(2)}) collective-permute-start(bf16[864,384]{1,0:T(8,128)(2,1)} %get-tuple-element.42), channel_id=1, source_target_pairs={{8,0},{16,8},{24,16},{9,1},{17,9},{25,17},{10,2},{18,10},{26,18},{... | collective-permute-start | bytes 1990664 | tf_op jit(solution)/shard_map/ppermute | solution.py:299
  91.1 14.2 %copy-start = (s32[1,1,12,2]{2,3,1,0:T(2,128)S(1)}, s32[1,1,12,2]{2,3,1,0:T(2,128)}, u32[]{:S(2)}) copy-start(s32[1,1,12,2]{2,3,1,0:T(2,128)} %param.5) | copy-start | bytes 292
  98.9 32.1 %collective-permute-start.10 = (bf16[864,384]{1,0:T(8,128)(2,1)}, bf16[864,384]{1,0:T(8,128)(2,1)}, u32[]{:S(2)}, u32[]{:S(2)}) collective-permute-start(bf16[864,384]{1,0:T(8,128)(2,1)} %get-tuple-element.44), channel_id=1, source_target_pairs={{0,8},{8,16},{16,24},{1,9},{9,17},{17,25},{2,10},{10,18},{18,26},{... | collective-permute-start | bytes 1990664 | tf_op jit(solution)/shard_map/ppermute | solution.py:299
  104.0 31.9 %collective-permute-start.11 = (bf16[864,384]{1,0:T(8,128)(2,1)}, bf16[864,384]{1,0:T(8,128)(2,1)}, u32[]{:S(2)}, u32[]{:S(2)}) collective-permute-start(bf16[864,384]{1,0:T(8,128)(2,1)} %get-tuple-element.45), channel_id=1, source_target_pairs={{8,0},{16,8},{24,16},{9,1},{17,9},{25,17},{10,2},{18,10},{26,18},{... | collective-permute-start | bytes 1990664 | tf_op jit(solution)/shard_map/ppermute | solution.py:299
  126.5 21.1 %collective-permute-start.12 = (bf16[864,384]{1,0:T(8,128)(2,1)}, bf16[864,384]{1,0:T(8,128)(2,1)}, u32[]{:S(2)}, u32[]{:S(2)}) collective-permute-start(bf16[864,384]{1,0:T(8,128)(2,1)} %get-tuple-element.48), channel_id=1, source_target_pairs={{1,2},{3,4},{5,6},{2,1},{4,3},{6,5},{9,10},{11,12},{13,14},{10,9},... | collective-permute-start | bytes 1990664 | tf_op jit(solution)/shard_map/ppermute | solution.py:303
  139.1 21.1 %collective-permute-start.13 = (bf16[864,384]{1,0:T(8,128)(2,1)}, bf16[864,384]{1,0:T(8,128)(2,1)}, u32[]{:S(2)}, u32[]{:S(2)}) collective-permute-start(bf16[864,384]{1,0:T(8,128)(2,1)} %get-tuple-element.54), channel_id=1, source_target_pairs={{1,2},{3,4},{5,6},{2,1},{4,3},{6,5},{9,10},{11,12},{13,14},{10,9},... | collective-permute-start | bytes 1990664 | tf_op jit(solution)/shard_map/ppermute | solution.py:303
Sparse Core Ops, SparseCore 0:
  20.0 104.7 all-gather.2

commit v5 on v4

--- a/solution.py
+++ b/solution.py
@@ -15,8 +15,7 @@
 NEG = -1e30
 SCALE2 = 1.4426950408889634 / HD**0.5
 VMEM = 127 * 2**19
-ROW_GROUPS = 2
-SIDE_GROUPS = 2
+GROUPS = ((0, 6), (6, 6))
 BF, F32 = jnp.bfloat16, jnp.float32
 LOG_ROWS = 16
 BLOCK = HD + LOG_ROWS
@@ -74,9 +73,8 @@
 
 
 def read_part(ref, head):
-    low = head * BLOCK
-    log = jnp.sum(ref[low + HD : low + BLOCK, :].astype(F32), axis=0, keepdims=True)
-    return ref[low : low + HD, :].astype(F32), log
+    log = jnp.sum(ref[rows_of(head, HD, LOG_ROWS), :].astype(F32), axis=0, keepdims=True)
+    return ref[rows_of(head, 0, HD), :].astype(F32), log
 
 
 def lanes(i):
@@ -176,6 +174,49 @@
     return res[1], res[0]
 
 
+def side_kernel(heads, flags, q_ref, kv_ref, lo_ref, hi_ref, out_ref, token):
+    pass_flags(flags, token)
+
+    def get(head, _):
+        at = lanes(head)
+        keys = jnp.concatenate([kv_ref[t, 0, :, at] for t in range(TT)], axis=0)
+        values = jnp.concatenate([kv_ref[t, 1, :, at].T for t in range(TT)], axis=1)
+        return q_ref[:, at], keys, values
+
+    def finish(head, _, out, log):
+        parts = [masked((out, log), flags[3])]
+        parts += [masked(read_part(r, head), flags[f]) for r, f in ((lo_ref, 4), (hi_ref, 5))]
+        write_part(out_ref, head, *merge_parts(parts))
+
+    attend_all(heads, 1, get, finish)
+
+
+def side_and_merge(flags, q, kv, parts, h0, nh, step, flops):
+    smem = pl.BlockSpec(memory_space=pltpu.SMEM)
+    block = pl.BlockSpec((step * BLOCK, TILE), lambda h: (h, 0))
+    base = h0 // step
+    res = pl.pallas_call(
+        functools.partial(side_kernel, step),
+        grid=(nh // step,),
+        in_specs=[
+            smem,
+            pl.BlockSpec((TILE, step * HD), lambda h: (0, h + base)),
+            pl.BlockSpec((TT, 2, TILE, step * HD), lambda h: (0, 0, 0, h + base)),
+            block,
+            block,
+        ],
+        out_specs=[block, smem],
+        out_shape=[
+            jax.ShapeDtypeStruct((nh * BLOCK, TILE), BF),
+            jax.ShapeDtypeStruct(flags.shape, flags.dtype),
+        ],
+        compiler_params=pltpu.CompilerParams(vmem_limit_bytes=VMEM),
+        cost_estimate=pl.CostEstimate(flops=flops, bytes_accessed=1000, transcendentals=0),
+        name="side",
+    )(flags, q, kv, *parts)
+    return res[1], res[0]
+
+
 def far_kernel(width, h0, nh, heads, flags, offsets, q_ref, tiles, *refs):
     out_ref, token, buffer, sems = refs[-4:]
     step = pl.program_id(0)
@@ -237,7 +278,7 @@
         out_ref[:, lanes(head)] = merge_parts(parts)[0].T.astype(out_ref.dtype)
 
 
-def final(flags, parts, h0, nh, step, out):
+def final(flags, parts, h0, nh, step, out, flops):
     smem = pl.BlockSpec(memory_space=pltpu.SMEM)
     specs = [
         pl.BlockSpec((step * BLOCK, TILE), functools.partial(lambda h, d: (h + d, 0), d=(h0 - base) // step))
@@ -255,7 +296,7 @@
         ],
         input_output_aliases={} if out is None else {1 + len(parts): 0},
         compiler_params=pltpu.CompilerParams(vmem_limit_bytes=VMEM),
-        cost_estimate=pl.CostEstimate(flops=1000, bytes_accessed=1000, transcendentals=0),
+        cost_estimate=pl.CostEstimate(flops=flops, bytes_accessed=1000, transcendentals=0),
         name="final",
     )(flags, *[a for _, _, a in parts], *before)
 
@@ -290,38 +331,36 @@
     qs_lo = lax.ppermute(q_side, "ha", up)
     qs_hi = lax.ppermute(q_side, "ha", down)
 
-    per = HEADS // SIDE_GROUPS
-
     def side_rows(flags, g, flops):
         flags, (s_lo, s_hi) = window(
-            "side_rows", flags, [qs_lo, qs_hi], [kv], [(0, (0,)), (1, (0,))], g * per, per, [BF, BF], 2, 2, flops
+            "side_rows", flags, [qs_lo, qs_hi], [kv], [(0, (0,)), (1, (0,))], *GROUPS[g], [BF, BF], 2, 2, flops
         )
         return flags, [lax.ppermute(s_hi, "ha", up), lax.ppermute(s_lo, "ha", down)]
-
-    def side_return(flags, g, parts, flops, after):
-        flags, merged = merge("side_merge", flags, s_own, g * per, parts, [3, 4, 5], per, 6, flops, after)
-        return flags, lax.ppermute(merged, "wa", across)
 
     flags, (o_lo, o_hi) = window(
         "rows", flags, [q_lo, q_hi], [kv, kv_mate], [(0, (0, 1)), (1, (0, 1))], 0, HEADS, [BF, BF], 2, 2, 10**13
     )
+    flags, (s_own,) = window("side_own", flags, [q_side], [kv], [(0, (0,))], *GROUPS[0], [F32], 1, 3)
+    flags, first = side_rows(flags, 0, 1000)
+    flags, second = side_rows(flags, 1, 1000)
+    o_lo, o_hi, flags = lax.optimization_barrier((o_lo, o_hi, flags))
     from_lo = lax.ppermute(o_hi, "ha", up)
     from_hi = lax.ppermute(o_lo, "ha", down)
-    flags, first = side_rows(flags, 0, 2 * 10**10)
-    flags, second = side_rows(flags, 1, 1000)
-    flags, (s_own,) = window("side_own", flags, [q_side], [kv], [(0, (0,))], 0, HEADS, [F32], 1, 3)
-    flags, first = side_return(flags, 0, first, 1000, [from_lo, from_hi])
-    flags, second = side_return(flags, 1, second, 3 * 10**10, [])
+    flags, first = merge("side_merge", flags, s_own, 0, first, [3, 4, 5], GROUPS[0][1], 6, 1000, [])
+    first = lax.ppermute(first, "wa", across)
+    flags, second = side_and_merge(flags, q_side, kv, second, *GROUPS[1], 3, 8 * 10**9)
+    second = lax.ppermute(second, "wa", across)
     offsets = far_offsets.reshape(-1)
-    flags, far_first = far(flags, offsets, q, tiles, 0, per, 3, 1000, [])
-    flags, far_second = far(flags, offsets, q, tiles, per, per, 3, 10**13, [first])
+    flags, far_first = far(flags, offsets, q, tiles, *GROUPS[0], 3, 1000, [])
+    flags, far_second = far(flags, offsets, q, tiles, *GROUPS[1], 3, 1000, [])
     out = None
-    for g, (side_merged, far_part) in enumerate([(first, far_first), (second, far_second)]):
-        low = g * per
+    for (low, count), side_merged, far_part, flops in zip(
+        GROUPS, (first, second), (far_first, far_second), (30 * 10**9, 1000)
+    ):
         out, flags = final(
             flags,
             [(0, 0, own), (0, low, far_part), (1, 0, from_lo), (2, 0, from_hi), (3, low, side_merged)],
-            low, per, 3, out,
+            low, count, 3, out, flops,
         )
     return out.reshape(queries.shape)
 

time: 171 us -> 165 us (0.965)
  waiting for transfers between devices: 21.1 us -> 12.1 us
  starting transfers between devices: 40.1 us -> 43.3 us
    ppermute x2, waiting for transfers between devices: 10.2 us -> 2.97 us  [side_rows(): lax.ppermute(s_lo, 'ha', down)]
    pallas_call x0 -> x1, Pallas kernels: none -> 6.39 us  [side_and_merge(): pl.pallas_call(functools.partial(side_kernel, step), grid=(nh // step,),...]
    pallas_call x5, Pallas kernels: 64.2 us -> 60.8 us  [window(): pl.pallas_call(functools.partial(window_kernel, jobs, len(qs), len(kvs),...]
    ppermute x2, starting transfers between devices: 6.6 us -> 9.75 us  [the longest x1 5.06 us: on_device(): second = lax.ppermute(second, 'wa', across)]
    pallas_call x2 -> x1, Pallas kernels: 6.11 us -> 3.03 us  [merge(): pl.pallas_call(functools.partial(merge_kernel, part_flags, len(after), st...]
    ppermute x1, waiting for transfers between devices: 0.01 us -> 2.95 us  [on_device(): from_hi = lax.ppermute(o_lo, 'ha', down)]
    ppermute x2, waiting for transfers between devices: 2.55 us -> 0.01 us  [the longest x1 0.01 us: on_device(): first = lax.ppermute(first, 'wa', across)]
    ppermute x2, waiting for transfers between devices: 1.92 us -> 0.01 us  [side_rows(): lax.ppermute(s_hi, 'ha', up)]
  transfers between devices with their start and end apart: 15 -> 15, of which waited for: 6 -> 3; matrix products, arithmetic and copies ran while one was open for 3% -> 3% of each run, Pallas kernels for 51% -> 53%
where the time goes in v5:
time: 165 us; the launch traced here: 164 us
  Pallas kernels  90 us (55%)
  starting transfers between devices  43.3 us (26%)
  between operations  13.6 us (8%)
  waiting for transfers between devices  12.1 us (7%)
  local copies, waits for them, and re-layouts  5.51 us (3%)
    pallas_call x5, Pallas kernels, window(): pl.pallas_call(functools.partial(window_kernel, jobs, len(qs), len(kvs),...  60.8 us
    pallas_call x2, Pallas kernels, far(): pl.pallas_call(functools.partial(far_kernel, tiles.shape[0], h0, nh, step...  12.9 us
    ppermute x2, starting transfers between devices, side_rows(): lax.ppermute(s_hi, 'ha', up)  9.42 us
    pallas_call x2, Pallas kernels, final(): pl.pallas_call(functools.partial(final_kernel, [f for f, _, _ in parts],...  6.88 us
    pallas_call x1, Pallas kernels, side_and_merge(): pl.pallas_call(functools.partial(side_kernel, step), grid=(nh // step,),...  6.39 us
    ppermute x1, waiting for transfers between devices, on_device(): q_side = lax.ppermute(q, 'wa', across)  6.12 us
    ppermute x1, starting transfers between devices, on_device(): from_lo = lax.ppermute(o_hi, 'ha', up)  5.1 us
    ppermute x1, starting transfers between devices, on_device(): second = lax.ppermute(second, 'wa', across)  5.06 us
  transfers between devices with their start and end apart: 15, of which 3 were waited for; matrix products, arithmetic and copies ran while one was open for 3% of the time, Pallas kernels for 53%

profile of v5, /device:TPU:3, one launch (start us, length us, event | category | flops | bytes accessed | tf_op | source)
XLA Modules:
  0.0 164.5 jit_solution(3358498859243727668)
XLA Ops:
  7.2 3.0 %collective-permute-start = (bf16[384,1536]{1,0:T(8,128)(2,1)}, bf16[384,1536]{1,0:T(8,128)(2,1)}, u32[]{:S(2)}, u32[]{:S(2)}) collective-permute-start(bf16[384,1536]{1,0:T(8,128)(2,1)} %bitcast.22), channel_id=1, source_target_pairs={{1,2},{3,4},{5,6},{2,1},{4,3},{6,5},{9,10},{11,12},{13,14},{10,9},... | collective-permute-start | bytes 3538952 | tf_op jit(solution)/shard_map/ppermute | solution.py:323
  10.2 4.2 %collective-permute-start.2 = (bf16[384,1536]{1,0:T(8,128)(2,1)}, bf16[384,1536]{1,0:T(8,128)(2,1)}, u32[]{:S(2)}, u32[]{:S(2)}) collective-permute-start(bf16[384,1536]{1,0:T(8,128)(2,1)} %bitcast.23), channel_id=1, source_target_pairs={{0,8},{8,16},{16,24},{1,9},{9,17},{17,25},{2,10},{10,18},{18,26},{... | collective-permute-start | bytes 3538952 | tf_op jit(solution)/shard_map/ppermute | solution.py:324
  15.7 4.1 %fusion = (bf16[1,1,1,2,384,1536]{5,4,3,2,1,0:T(8,128)(2,1)}, bf16[2,384,1536]{2,1,0:T(8,128)(2,1)}) fusion(bf16[1,1,3,2,384,1536]{5,4,3,2,1,0:T(8,128)(2,1)} %param.4), kind=kLoop, calls=%fused_computation.1 | loop fusion | bytes 7077888 | tf_op jit(solution)/shard_map/slice | solution.py:326
  20.6 16.0 %own.1 = (f32[1728,384]{1,0:T(8,128)}, s32[8]{0:T(128)}) custom-call(s32[8]{0:T(128)} %stack.51.flags, bf16[2,384,1536]{2,1,0:T(8,128)(2,1)} %get-tuple-element.64.refs_0_, bf16[384,1536]{1,0:T(8,128)(2,1)} %bitcast.25, bf16[3,2,384,1536]{3,2,1,0:T(8,128)(2,1)} %bitcast.14, bf16[3,2,384,1536]{3,2,1,0:T(8,128)(2,1)} %collective-permute-done.1.refs_3_), custom_call_target="tpu_custom_call" | custom-call | flops 1000 | bytes 1000 | tf_op jit(solution)/shard_map/own/pallas_call | solution.py:119
  36.6 6.1 %collective-permute-done.refs_0_.q_ref = bf16[384,1536]{1,0:T(8,128)(2,1)} collective-permute-done((bf16[384,1536]{1,0:T(8,128)(2,1)}, bf16[384,1536]{1,0:T(8,128)(2,1)}, u32[]{:S(2)}, u32[]{:S(2)}) %collective-permute-start) | collective-permute-done | bytes 1179680 | tf_op jit(solution)/shard_map/ppermute | solution.py:323
  42.7 4.3 %collective-permute-start.4 = (bf16[384,1536]{1,0:T(8,128)(2,1)}, bf16[384,1536]{1,0:T(8,128)(2,1)}, u32[]{:S(2)}, u32[]{:S(2)}) collective-permute-start(bf16[384,1536]{1,0:T(8,128)(2,1)} %collective-permute-done.refs_0_.q_ref), channel_id=1, source_target_pairs={{0,8},{8,16},{16,24},{1,9},{9,17},{17,25},{2,10},{10,18},{18,26},{... | collective-permute-start | bytes 3538952 | tf_op jit(solution)/shard_map/ppermute | solution.py:331
  48.5 22.4 %rows.1 = (bf16[1728,384]{1,0:T(8,128)(2,1)}, bf16[1728,384]{1,0:T(8,128)(2,1)}, s32[8]{0:T(128)}) custom-call(s32[8]{0:T(128)} %get-tuple-element.35.flags, bf16[384,1536]{1,0:T(8,128)(2,1)} %collective-permute-done.2.refs_0_, bf16[384,1536]{1,0:T(8,128)(2,1)} %collective-permute-done.3.refs_1_, bf16[3,2,384,1536]{3,2,1,0:T(8,128)(2,1)} %bitcast.15, ...), custom_call_target="tpu_custom_call" | custom-call | flops 9999999827968 | bytes 1000 | tf_op jit(solution)/shard_map/rows/pallas_call | solution.py:119
  70.9 7.0 %side_own.1 = (f32[864,384]{1,0:T(8,128)}, s32[8]{0:T(128)}) custom-call(s32[8]{0:T(128)} %get-tuple-element.38.flags, bf16[384,1536]{1,0:T(8,128)(2,1)} %collective-permute-done.refs_0_.q_ref, bf16[3,2,384,1536]{3,2,1,0:T(8,128)(2,1)} %bitcast.16), custom_call_target="tpu_custom_call" | custom-call | flops 1000 | bytes 1000 | tf_op jit(solution)/shard_map/side_own/pallas_call | solution.py:119
  77.9 7.7 %side_rows.2 = (bf16[864,384]{1,0:T(8,128)(2,1)}, bf16[864,384]{1,0:T(8,128)(2,1)}, s32[8]{0:T(128)}) custom-call(s32[8]{0:T(128)} %get-tuple-element.40.flags, bf16[384,1536]{1,0:T(8,128)(2,1)} %collective-permute-done.4.refs_0_, bf16[384,1536]{1,0:T(8,128)(2,1)} %collective-permute-done.5.refs_1_, bf16[3,2,384,1536]{3,2,1,0:T(8,128)(2,1)} %bitcast.17), custom_call_target="tpu_custom_call" | custom-call | flops 1000 | bytes 1000 | tf_op jit(solution)/shard_map/side_rows/pallas_call | solution.py:119
  85.6 4.5 %collective-permute-start.6 = (bf16[864,384]{1,0:T(8,128)(2,1)}, bf16[864,384]{1,0:T(8,128)(2,1)}, u32[]{:S(2)}, u32[]{:S(2)}) collective-permute-start(bf16[864,384]{1,0:T(8,128)(2,1)} %get-tuple-element.45), channel_id=1, source_target_pairs={{0,8},{8,16},{16,24},{1,9},{9,17},{17,25},{2,10},{10,18},{18,26},{... | collective-permute-start | bytes 1990664 | tf_op jit(solution)/shard_map/ppermute | solution.py:338
  90.2 1.5 collective-permute-start.7
  91.7 7.7 %side_rows.3 = (bf16[864,384]{1,0:T(8,128)(2,1)}, bf16[864,384]{1,0:T(8,128)(2,1)}, s32[8]{0:T(128)}) custom-call(s32[8]{0:T(128)} %get-tuple-element.41.flags, bf16[384,1536]{1,0:T(8,128)(2,1)} %collective-permute-done.4.refs_0_, bf16[384,1536]{1,0:T(8,128)(2,1)} %collective-permute-done.5.refs_1_, bf16[3,2,384,1536]{3,2,1,0:T(8,128)(2,1)} %bitcast.18), custom_call_target="tpu_custom_call" | custom-call | flops 1000 | bytes 1000 | tf_op jit(solution)/shard_map/side_rows/pallas_call | solution.py:119
  99.4 4.9 %collective-permute-start.8 = (bf16[864,384]{1,0:T(8,128)(2,1)}, bf16[864,384]{1,0:T(8,128)(2,1)}, u32[]{:S(2)}, u32[]{:S(2)}) collective-permute-start(bf16[864,384]{1,0:T(8,128)(2,1)} %get-tuple-element.48), channel_id=1, source_target_pairs={{0,8},{8,16},{16,24},{1,9},{9,17},{17,25},{2,10},{10,18},{18,26},{... | collective-permute-start | bytes 1990664 | tf_op jit(solution)/shard_map/ppermute | solution.py:338
  105.6 5.1 %collective-permute-start.10 = (bf16[1728,384]{1,0:T(8,128)(2,1)}, bf16[1728,384]{1,0:T(8,128)(2,1)}, u32[]{:S(2)}, u32[]{:S(2)}) collective-permute-start(bf16[1728,384]{1,0:T(8,128)(2,1)} %get-tuple-element.55), channel_id=1, source_target_pairs={{0,8},{8,16},{16,24},{1,9},{9,17},{17,25},{2,10},{10,18},{18,26},{... | collective-permute-start | bytes 3981320 | tf_op jit(solution)/shard_map/ppermute | solution.py:347
  112.7 3.0 %side_merge.1 = (bf16[864,384]{1,0:T(8,128)(2,1)}, s32[8]{0:T(128)}) custom-call(s32[8]{0:T(128)} %get-tuple-element.43.flags, f32[864,384]{1,0:T(8,128)} %get-tuple-element.44.refs_0_, bf16[864,384]{1,0:T(8,128)(2,1)} %collective-permute-done.6.refs_1_, bf16[864,384]{1,0:T(8,128)(2,1)} %collective-permute-done.7.refs_2_), custom_call_target="tpu_custom_call" | custom-call | flops 1000 | bytes 1000 | tf_op jit(solution)/shard_map/side_merge/pallas_call | solution.py:159
  115.7 4.7 %collective-permute-start.12 = (bf16[864,384]{1,0:T(8,128)(2,1)}, bf16[864,384]{1,0:T(8,128)(2,1)}, u32[]{:S(2)}, u32[]{:S(2)}) collective-permute-start(bf16[864,384]{1,0:T(8,128)(2,1)} %get-tuple-element.57), channel_id=1, source_target_pairs={{1,2},{3,4},{5,6},{2,1},{4,3},{6,5},{9,10},{11,12},{13,14},{10,9},... | collective-permute-start | bytes 1990664 | tf_op jit(solution)/shard_map/ppermute | solution.py:350
  120.4 3.0 %collective-permute-done.9.hi_ref = bf16[864,384]{1,0:T(8,128)(2,1)} collective-permute-done((bf16[864,384]{1,0:T(8,128)(2,1)}, bf16[864,384]{1,0:T(8,128)(2,1)}, u32[]{:S(2)}, u32[]{:S(2)}) %collective-permute-start.9) | collective-permute-done | bytes 663584 | tf_op jit(solution)/shard_map/ppermute | solution.py:338
  123.4 6.4 %side.1 = (bf16[864,384]{1,0:T(8,128)(2,1)}, s32[8]{0:T(128)}) custom-call(s32[8]{0:T(128)} %get-tuple-element.47.flags, bf16[384,1536]{1,0:T(8,128)(2,1)} %collective-permute-done.refs_0_.q_ref, bf16[3,2,384,1536]{3,2,1,0:T(8,128)(2,1)} %bitcast.19, bf16[864,384]{1,0:T(8,128)(2,1)} %collective-permute-done.8.lo_ref, ...), custom_call_target="tpu_custom_call" | custom-call | flops 8000000000 | bytes 1000 | tf_op jit(solution)/shard_map/side/pallas_call | solution.py:198
  129.8 5.1 %collective-permute-start.13 = (bf16[864,384]{1,0:T(8,128)(2,1)}, bf16[864,384]{1,0:T(8,128)(2,1)}, u32[]{:S(2)}, u32[]{:S(2)}) collective-permute-start(bf16[864,384]{1,0:T(8,128)(2,1)} %get-tuple-element.60), channel_id=1, source_target_pairs={{1,2},{3,4},{5,6},{2,1},{4,3},{6,5},{9,10},{11,12},{13,14},{10,9},... | collective-permute-start | bytes 1990664 | tf_op jit(solution)/shard_map/ppermute | solution.py:352
  134.9 6.4 %far.2 = (f32[864,384]{1,0:T(8,128)}, s32[8]{0:T(128)}) custom-call(s32[8]{0:T(128)} %get-tuple-element.50.flags, s32[24]{0:T(128)} %reshape.16.offsets, bf16[384,1536]{1,0:T(8,128)(2,1)} %bitcast.26, bf16[8,2,384,1536]{3,2,1,0:T(8,128)(2,1)} %bitcast.20), custom_call_target="tpu_custom_call" | custom-call | flops 1000 | bytes 1000 | tf_op jit(solution)/shard_map/far/pallas_call | solution.py:250
  141.3 6.5 %far.3 = (f32[864,384]{1,0:T(8,128)}, s32[8]{0:T(128)}) custom-call(s32[8]{0:T(128)} %get-tuple-element.51.flags, s32[24]{0:T(128)} %reshape.16.offsets, bf16[384,1536]{1,0:T(8,128)(2,1)} %bitcast.27, bf16[8,2,384,1536]{3,2,1,0:T(8,128)(2,1)} %bitcast.21), custom_call_target="tpu_custom_call" | custom-call | flops 1000 | bytes 1000 | tf_op jit(solution)/shard_map/far/pallas_call | solution.py:250
  147.8 3.0 %collective-permute-done.11.refs_3_ = bf16[1728,384]{1,0:T(8,128)(2,1)} collective-permute-done((bf16[1728,384]{1,0:T(8,128)(2,1)}, bf16[1728,384]{1,0:T(8,128)(2,1)}, u32[]{:S(2)}, u32[]{:S(2)}) %collective-permute-start.11) | collective-permute-done | bytes 1327136 | tf_op jit(solution)/shard_map/ppermute | solution.py:348
  150.7 3.4 %final.2 = (bf16[384,1536]{1,0:T(8,128)(2,1)}, s32[8]{0:T(128)}) custom-call(s32[8]{0:T(128)} %get-tuple-element.52.flags, f32[1728,384]{1,0:T(8,128)} %get-tuple-element.53.refs_0_, f32[864,384]{1,0:T(8,128)} %get-tuple-element.54.refs_1_, bf16[1728,384]{1,0:T(8,128)(2,1)} %collective-permute-done.10.refs_2_, ...), custom_call_target="tpu_custom_call" | custom-call | flops 30000001024 | bytes 1000 | tf_op jit(solution)/shard_map/final/pallas_call | solution.py:288
  154.2 3.5 %final.3 = (bf16[384,1536]{1,0:T(8,128)(2,1)}, s32[8]{0:T(128)}) custom-call(s32[8]{0:T(128)} %get-tuple-element.58.flags, f32[1728,384]{1,0:T(8,128)} %get-tuple-element.53.refs_0_, f32[864,384]{1,0:T(8,128)} %get-tuple-element.59.refs_1_, bf16[1728,384]{1,0:T(8,128)(2,1)} %collective-permute-done.10.refs_2_, ...), custom_call_target="tpu_custom_call", output_to_operand_aliasing={{0}: (6, {})} | custom-call | flops 1000 | bytes 1000 | tf_op jit(solution)/shard_map/final/pallas_call | solution.py:288
  (24 shorter events, 7.4 us)
Async XLA Ops:
  6.5 128.3 %all-gather.3.cloned.1.call-start = ((), (), s32[]{:S(2)}) async-start(), calls=%async_computation | async-start | bytes 21233664 | tf_op jit(solution)/shard_map/all_gather | solution.py:329
  6.5 14.0 %collective-permute-start.1 = (bf16[3,2,384,1536]{3,2,1,0:T(8,128)(2,1)}, bf16[3,2,384,1536]{3,2,1,0:T(8,128)(2,1)}, u32[]{:S(2)}, u32[]{:S(2)}) collective-permute-start(bf16[3,2,384,1536]{3,2,1,0:T(8,128)(2,1)} %bitcast.13), channel_id=1, source_target_pairs={{0,1},{1,0},{2,3},{3,2},{4,5},{5,4},{6,7},{7,6},{8,9},{9,8},{10,11... | collective-permute-start | bytes 21233672 | tf_op jit(solution)/shard_map/ppermute | solution.py:322
  7.2 35.5 %collective-permute-start = (bf16[384,1536]{1,0:T(8,128)(2,1)}, bf16[384,1536]{1,0:T(8,128)(2,1)}, u32[]{:S(2)}, u32[]{:S(2)}) collective-permute-start(bf16[384,1536]{1,0:T(8,128)(2,1)} %bitcast.22), channel_id=1, source_target_pairs={{1,2},{3,4},{5,6},{2,1},{4,3},{6,5},{9,10},{11,12},{13,14},{10,9},... | collective-permute-start | bytes 3538952 | tf_op jit(solution)/shard_map/ppermute | solution.py:323
  10.2 38.2 %collective-permute-start.2 = (bf16[384,1536]{1,0:T(8,128)(2,1)}, bf16[384,1536]{1,0:T(8,128)(2,1)}, u32[]{:S(2)}, u32[]{:S(2)}) collective-permute-start(bf16[384,1536]{1,0:T(8,128)(2,1)} %bitcast.23), channel_id=1, source_target_pairs={{0,8},{8,16},{16,24},{1,9},{9,17},{17,25},{2,10},{10,18},{18,26},{... | collective-permute-start | bytes 3538952 | tf_op jit(solution)/shard_map/ppermute | solution.py:324
  14.4 34.0 %collective-permute-start.3 = (bf16[384,1536]{1,0:T(8,128)(2,1)}, bf16[384,1536]{1,0:T(8,128)(2,1)}, u32[]{:S(2)}, u32[]{:S(2)}) collective-permute-start(bf16[384,1536]{1,0:T(8,128)(2,1)} %bitcast.24), channel_id=1, source_target_pairs={{8,0},{16,8},{24,16},{9,1},{17,9},{25,17},{10,2},{18,10},{26,18},{... | collective-permute-start | bytes 3538952 | tf_op jit(solution)/shard_map/ppermute | solution.py:325
  42.7 35.2 %collective-permute-start.4 = (bf16[384,1536]{1,0:T(8,128)(2,1)}, bf16[384,1536]{1,0:T(8,128)(2,1)}, u32[]{:S(2)}, u32[]{:S(2)}) collective-permute-start(bf16[384,1536]{1,0:T(8,128)(2,1)} %collective-permute-done.refs_0_.q_ref), channel_id=1, source_target_pairs={{0,8},{8,16},{16,24},{1,9},{9,17},{17,25},{2,10},{10,18},{18,26},{... | collective-permute-start | bytes 3538952 | tf_op jit(solution)/shard_map/ppermute | solution.py:331
  47.0 30.9 %collective-permute-start.5 = (bf16[384,1536]{1,0:T(8,128)(2,1)}, bf16[384,1536]{1,0:T(8,128)(2,1)}, u32[]{:S(2)}, u32[]{:S(2)}) collective-permute-start(bf16[384,1536]{1,0:T(8,128)(2,1)} %collective-permute-done.refs_0_.q_ref), channel_id=1, source_target_pairs={{8,0},{16,8},{24,16},{9,1},{17,9},{25,17},{10,2},{18,10},{26,18},{... | collective-permute-start | bytes 3538952 | tf_op jit(solution)/shard_map/ppermute | solution.py:332
  85.6 25.0 %collective-permute-start.6 = (bf16[864,384]{1,0:T(8,128)(2,1)}, bf16[864,384]{1,0:T(8,128)(2,1)}, u32[]{:S(2)}, u32[]{:S(2)}) collective-permute-start(bf16[864,384]{1,0:T(8,128)(2,1)} %get-tuple-element.45), channel_id=1, source_target_pairs={{0,8},{8,16},{16,24},{1,9},{9,17},{17,25},{2,10},{10,18},{18,26},{... | collective-permute-start | bytes 1990664 | tf_op jit(solution)/shard_map/ppermute | solution.py:338
  90.2 22.5 %collective-permute-start.7 = (bf16[864,384]{1,0:T(8,128)(2,1)}, bf16[864,384]{1,0:T(8,128)(2,1)}, u32[]{:S(2)}, u32[]{:S(2)}) collective-permute-start(bf16[864,384]{1,0:T(8,128)(2,1)} %get-tuple-element.46), channel_id=1, source_target_pairs={{8,0},{16,8},{24,16},{9,1},{17,9},{25,17},{10,2},{18,10},{26,18},{... | collective-permute-start | bytes 1990664 | tf_op jit(solution)/shard_map/ppermute | solution.py:338
  91.7 20.3 %copy-start = (s32[1,1,12,2]{2,3,1,0:T(2,128)S(1)}, s32[1,1,12,2]{2,3,1,0:T(2,128)}, u32[]{:S(2)}) copy-start(s32[1,1,12,2]{2,3,1,0:T(2,128)} %param.5) | copy-start | bytes 292
  99.4 21.0 %collective-permute-start.8 = (bf16[864,384]{1,0:T(8,128)(2,1)}, bf16[864,384]{1,0:T(8,128)(2,1)}, u32[]{:S(2)}, u32[]{:S(2)}) collective-permute-start(bf16[864,384]{1,0:T(8,128)(2,1)} %get-tuple-element.48), channel_id=1, source_target_pairs={{0,8},{8,16},{16,24},{1,9},{9,17},{17,25},{2,10},{10,18},{18,26},{... | collective-permute-start | bytes 1990664 | tf_op jit(solution)/shard_map/ppermute | solution.py:338
  104.3 19.1 %collective-permute-start.9 = (bf16[864,384]{1,0:T(8,128)(2,1)}, bf16[864,384]{1,0:T(8,128)(2,1)}, u32[]{:S(2)}, u32[]{:S(2)}) collective-permute-start(bf16[864,384]{1,0:T(8,128)(2,1)} %get-tuple-element.49), channel_id=1, source_target_pairs={{8,0},{16,8},{24,16},{9,1},{17,9},{25,17},{10,2},{18,10},{26,18},{... | collective-permute-start | bytes 1990664 | tf_op jit(solution)/shard_map/ppermute | solution.py:338
  105.6 42.2 %collective-permute-start.10 = (bf16[1728,384]{1,0:T(8,128)(2,1)}, bf16[1728,384]{1,0:T(8,128)(2,1)}, u32[]{:S(2)}, u32[]{:S(2)}) collective-permute-start(bf16[1728,384]{1,0:T(8,128)(2,1)} %get-tuple-element.55), channel_id=1, source_target_pairs={{0,8},{8,16},{16,24},{1,9},{9,17},{17,25},{2,10},{10,18},{18,26},{... | collective-permute-start | bytes 3981320 | tf_op jit(solution)/shard_map/ppermute | solution.py:347
  110.7 40.1 %collective-permute-start.11 = (bf16[1728,384]{1,0:T(8,128)(2,1)}, bf16[1728,384]{1,0:T(8,128)(2,1)}, u32[]{:S(2)}, u32[]{:S(2)}) collective-permute-start(bf16[1728,384]{1,0:T(8,128)(2,1)} %get-tuple-element.56), channel_id=1, source_target_pairs={{8,0},{16,8},{24,16},{9,1},{17,9},{25,17},{10,2},{18,10},{26,18},{... | collective-permute-start | bytes 3981320 | tf_op jit(solution)/shard_map/ppermute | solution.py:348
  115.7 32.1 %collective-permute-start.12 = (bf16[864,384]{1,0:T(8,128)(2,1)}, bf16[864,384]{1,0:T(8,128)(2,1)}, u32[]{:S(2)}, u32[]{:S(2)}) collective-permute-start(bf16[864,384]{1,0:T(8,128)(2,1)} %get-tuple-element.57), channel_id=1, source_target_pairs={{1,2},{3,4},{5,6},{2,1},{4,3},{6,5},{9,10},{11,12},{13,14},{10,9},... | collective-permute-start | bytes 1990664 | tf_op jit(solution)/shard_map/ppermute | solution.py:350
  129.8 24.4 %collective-permute-start.13 = (bf16[864,384]{1,0:T(8,128)(2,1)}, bf16[864,384]{1,0:T(8,128)(2,1)}, u32[]{:S(2)}, u32[]{:S(2)}) collective-permute-start(bf16[864,384]{1,0:T(8,128)(2,1)} %get-tuple-element.60), channel_id=1, source_target_pairs={{1,2},{3,4},{5,6},{2,1},{4,3},{6,5},{9,10},{11,12},{13,14},{10,9},... | collective-permute-start | bytes 1990664 | tf_op jit(solution)/shard_map/ppermute | solution.py:352
Sparse Core Ops, SparseCore 0:
  20.0 104.7 all-gather.2

commit v6 on v5

--- a/solution.py
+++ b/solution.py
@@ -142,38 +142,6 @@
     return part[0], jnp.where(flag != 0, part[1], NEG)
 
 
-def merge_kernel(part_flags, n_after, heads, flags, *refs):
-    refs = refs[n_after:]
-    n = len(part_flags)
-    out, token = refs[n:]
-    pass_flags(flags, token)
-    for head in range(heads):
-        write_part(
-            out, head, *merge_parts([masked(read_part(refs[i], head), flags[f]) for i, f in enumerate(part_flags)])
-        )
-
-
-def merge(name, flags, own, h0, parts, part_flags, nh, step, flops, after):
-    smem = pl.BlockSpec(memory_space=pltpu.SMEM)
-    block = pl.BlockSpec((step * BLOCK, TILE), lambda h: (h, 0))
-    res = pl.pallas_call(
-        functools.partial(merge_kernel, part_flags, len(after), step),
-        grid=(nh // step,),
-        in_specs=[smem] + [pl.BlockSpec(memory_space=pl.ANY)] * len(after)
-        + [pl.BlockSpec((step * BLOCK, TILE), lambda h: (h + h0 // step, 0))]
-        + [block] * len(parts),
-        out_specs=[block, smem],
-        out_shape=[
-            jax.ShapeDtypeStruct((nh * BLOCK, TILE), BF),
-            jax.ShapeDtypeStruct(flags.shape, flags.dtype),
-        ],
-        compiler_params=pltpu.CompilerParams(vmem_limit_bytes=VMEM),
-        cost_estimate=pl.CostEstimate(flops=flops, bytes_accessed=1000, transcendentals=0),
-        name=name,
-    )(flags, *after, own, *parts)
-    return res[1], res[0]
-
-
 def side_kernel(heads, flags, q_ref, kv_ref, lo_ref, hi_ref, out_ref, token):
     pass_flags(flags, token)
 
@@ -340,26 +308,22 @@
     flags, (o_lo, o_hi) = window(
         "rows", flags, [q_lo, q_hi], [kv, kv_mate], [(0, (0, 1)), (1, (0, 1))], 0, HEADS, [BF, BF], 2, 2, 10**13
     )
-    flags, (s_own,) = window("side_own", flags, [q_side], [kv], [(0, (0,))], *GROUPS[0], [F32], 1, 3)
     flags, first = side_rows(flags, 0, 1000)
     flags, second = side_rows(flags, 1, 1000)
     o_lo, o_hi, flags = lax.optimization_barrier((o_lo, o_hi, flags))
     from_lo = lax.ppermute(o_hi, "ha", up)
     from_hi = lax.ppermute(o_lo, "ha", down)
-    flags, first = merge("side_merge", flags, s_own, 0, first, [3, 4, 5], GROUPS[0][1], 6, 1000, [])
+    flags, first = side_and_merge(flags, q_side, kv, first, *GROUPS[0], 3, 1000)
     first = lax.ppermute(first, "wa", across)
     flags, second = side_and_merge(flags, q_side, kv, second, *GROUPS[1], 3, 8 * 10**9)
     second = lax.ppermute(second, "wa", across)
     offsets = far_offsets.reshape(-1)
-    flags, far_first = far(flags, offsets, q, tiles, *GROUPS[0], 3, 1000, [])
-    flags, far_second = far(flags, offsets, q, tiles, *GROUPS[1], 3, 1000, [])
+    flags, far_part = far(flags, offsets, q, tiles, 0, HEADS, 3, 1000, [])
     out = None
-    for (low, count), side_merged, far_part, flops in zip(
-        GROUPS, (first, second), (far_first, far_second), (30 * 10**9, 1000)
-    ):
+    for (low, count), side_merged, flops in zip(GROUPS, (first, second), (30 * 10**9, 1000)):
         out, flags = final(
             flags,
-            [(0, 0, own), (0, low, far_part), (1, 0, from_lo), (2, 0, from_hi), (3, low, side_merged)],
+            [(0, 0, own), (0, 0, far_part), (1, 0, from_lo), (2, 0, from_hi), (3, low, side_merged)],
             low, count, 3, out, flops,
         )
     return out.reshape(queries.shape)

time: 165 us -> 161 us (0.976)
  Pallas kernels: 90 us -> 83.2 us
  waiting for transfers between devices: 12.1 us -> 18.3 us
  starting transfers between devices: 43.3 us -> 40 us
    pallas_call x5 -> x4, Pallas kernels: 60.8 us -> 53.8 us  [window(): pl.pallas_call(functools.partial(window_kernel, jobs, len(qs), len(kvs),...]
    pallas_call x1 -> x2, Pallas kernels: 6.39 us -> 12.9 us  [side_and_merge(): pl.pallas_call(functools.partial(side_kernel, step), grid=(nh // step,),...]
    ppermute x1, waiting for transfers between devices: 0.01 us -> 4.03 us  [on_device(): qs_hi = lax.ppermute(q_side, 'ha', down)]
    pallas_call x2 -> x1, Pallas kernels: 12.9 us -> 9.68 us  [far(): pl.pallas_call(functools.partial(far_kernel, tiles.shape[0], h0, nh, step...]
    pallas_call x1 -> x0, Pallas kernels: 3.03 us -> none  [merge(): pl.pallas_call(functools.partial(merge_kernel, part_flags, len(after), st...]
    ppermute x2, waiting for transfers between devices: 2.97 us -> 0.21 us  [side_rows(): lax.ppermute(s_lo, 'ha', down)]
    ppermute x1, waiting for transfers between devices: 0.01 us -> 2.55 us  [on_device(): from_lo = lax.ppermute(o_hi, 'ha', up)]
    ppermute x1, waiting for transfers between devices: 2.95 us -> 4.95 us  [on_device(): from_hi = lax.ppermute(o_lo, 'ha', down)]
  transfers between devices with their start and end apart: 15 -> 15, of which waited for: 3 -> 6; matrix products, arithmetic and copies ran while one was open for 3% -> 3% of each run, Pallas kernels for 53% -> 50%
where the time goes in v6:
time: 161 us; the launch traced here: 160 us
  Pallas kernels  83.2 us (52%)
  starting transfers between devices  40 us (25%)
  waiting for transfers between devices  18.3 us (11%)
  between operations  13.6 us (8%)
  local copies, waits for them, and re-layouts  5.47 us (3%)
    pallas_call x4, Pallas kernels, window(): pl.pallas_call(functools.partial(window_kernel, jobs, len(qs), len(kvs),...  53.8 us
    pallas_call x2, Pallas kernels, side_and_merge(): pl.pallas_call(functools.partial(side_kernel, step), grid=(nh // step,),...  12.9 us
    pallas_call x1, Pallas kernels, far(): pl.pallas_call(functools.partial(far_kernel, tiles.shape[0], h0, nh, step...  9.68 us
    ppermute x2, starting transfers between devices, side_rows(): lax.ppermute(s_hi, 'ha', up)  8.03 us
    pallas_call x2, Pallas kernels, final(): pl.pallas_call(functools.partial(final_kernel, [f for f, _, _ in parts],...  6.88 us
    ppermute x1, waiting for transfers between devices, on_device(): q_side = lax.ppermute(q, 'wa', across)  6.17 us
    ppermute x1, starting transfers between devices, on_device(): from_lo = lax.ppermute(o_hi, 'ha', up)  5.09 us
    ppermute x1, waiting for transfers between devices, on_device(): from_hi = lax.ppermute(o_lo, 'ha', down)  4.95 us
  transfers between devices with their start and end apart: 15, of which 6 were waited for; matrix products, arithmetic and copies ran while one was open for 3% of the time, Pallas kernels for 50%

profile of v6, /device:TPU:3, one launch (start us, length us, event | category | flops | bytes accessed | tf_op | source)
XLA Modules:
  0.0 160.5 jit_solution(74513512357457038)
XLA Ops:
  7.2 3.0 %collective-permute-start = (bf16[384,1536]{1,0:T(8,128)(2,1)}, bf16[384,1536]{1,0:T(8,128)(2,1)}, u32[]{:S(2)}, u32[]{:S(2)}) collective-permute-start(bf16[384,1536]{1,0:T(8,128)(2,1)} %bitcast.21), channel_id=1, source_target_pairs={{1,2},{3,4},{5,6},{2,1},{4,3},{6,5},{9,10},{11,12},{13,14},{10,9},... | collective-permute-start | bytes 3538952 | tf_op jit(solution)/shard_map/ppermute | solution.py:291
  10.2 4.2 %collective-permute-start.2 = (bf16[384,1536]{1,0:T(8,128)(2,1)}, bf16[384,1536]{1,0:T(8,128)(2,1)}, u32[]{:S(2)}, u32[]{:S(2)}) collective-permute-start(bf16[384,1536]{1,0:T(8,128)(2,1)} %bitcast.22), channel_id=1, source_target_pairs={{0,8},{8,16},{16,24},{1,9},{9,17},{17,25},{2,10},{10,18},{18,26},{... | collective-permute-start | bytes 3538952 | tf_op jit(solution)/shard_map/ppermute | solution.py:292
  15.7 4.1 %fusion = (bf16[1,1,1,2,384,1536]{5,4,3,2,1,0:T(8,128)(2,1)}, bf16[2,384,1536]{2,1,0:T(8,128)(2,1)}) fusion(bf16[1,1,3,2,384,1536]{5,4,3,2,1,0:T(8,128)(2,1)} %param.4), kind=kLoop, calls=%fused_computation.1 | loop fusion | bytes 7077888 | tf_op jit(solution)/shard_map/slice | solution.py:294
  20.5 16.0 %own.1 = (f32[1728,384]{1,0:T(8,128)}, s32[8]{0:T(128)}) custom-call(s32[8]{0:T(128)} %stack.51.flags, bf16[2,384,1536]{2,1,0:T(8,128)(2,1)} %get-tuple-element.56.refs_0_, bf16[384,1536]{1,0:T(8,128)(2,1)} %bitcast.24, bf16[3,2,384,1536]{3,2,1,0:T(8,128)(2,1)} %bitcast.14, bf16[3,2,384,1536]{3,2,1,0:T(8,128)(2,1)} %collective-permute-done.1.refs_3_), custom_call_target="tpu_custom_call" | custom-call | flops 1000 | bytes 1000 | tf_op jit(solution)/shard_map/own/pallas_call | solution.py:119
  36.5 6.2 %collective-permute-done.q_ref = bf16[384,1536]{1,0:T(8,128)(2,1)} collective-permute-done((bf16[384,1536]{1,0:T(8,128)(2,1)}, bf16[384,1536]{1,0:T(8,128)(2,1)}, u32[]{:S(2)}, u32[]{:S(2)}) %collective-permute-start) | collective-permute-done | bytes 1179680 | tf_op jit(solution)/shard_map/ppermute | solution.py:291
  42.7 4.3 %collective-permute-start.4 = (bf16[384,1536]{1,0:T(8,128)(2,1)}, bf16[384,1536]{1,0:T(8,128)(2,1)}, u32[]{:S(2)}, u32[]{:S(2)}) collective-permute-start(bf16[384,1536]{1,0:T(8,128)(2,1)} %collective-permute-done.q_ref), channel_id=1, source_target_pairs={{0,8},{8,16},{16,24},{1,9},{9,17},{17,25},{2,10},{10,18},{18,26},{... | collective-permute-start | bytes 3538952 | tf_op jit(solution)/shard_map/ppermute | solution.py:299
  47.0 1.5 collective-permute-start.5
  48.5 22.5 %rows.1 = (bf16[1728,384]{1,0:T(8,128)(2,1)}, bf16[1728,384]{1,0:T(8,128)(2,1)}, s32[8]{0:T(128)}) custom-call(s32[8]{0:T(128)} %get-tuple-element.31.flags, bf16[384,1536]{1,0:T(8,128)(2,1)} %collective-permute-done.2.refs_0_, bf16[384,1536]{1,0:T(8,128)(2,1)} %collective-permute-done.3.refs_1_, bf16[3,2,384,1536]{3,2,1,0:T(8,128)(2,1)} %bitcast.15, ...), custom_call_target="tpu_custom_call" | custom-call | flops 9999999827968 | bytes 1000 | tf_op jit(solution)/shard_map/rows/pallas_call | solution.py:119
  70.9 4.0 %collective-permute-done.5.refs_1_ = bf16[384,1536]{1,0:T(8,128)(2,1)} collective-permute-done((bf16[384,1536]{1,0:T(8,128)(2,1)}, bf16[384,1536]{1,0:T(8,128)(2,1)}, u32[]{:S(2)}, u32[]{:S(2)}) %collective-permute-start.5) | collective-permute-done | bytes 1179680 | tf_op jit(solution)/shard_map/ppermute | solution.py:300
  75.0 7.7 %side_rows.2 = (bf16[864,384]{1,0:T(8,128)(2,1)}, bf16[864,384]{1,0:T(8,128)(2,1)}, s32[8]{0:T(128)}) custom-call(s32[8]{0:T(128)} %get-tuple-element.34.flags, bf16[384,1536]{1,0:T(8,128)(2,1)} %collective-permute-done.4.refs_0_, bf16[384,1536]{1,0:T(8,128)(2,1)} %collective-permute-done.5.refs_1_, bf16[3,2,384,1536]{3,2,1,0:T(8,128)(2,1)} %bitcast.16), custom_call_target="tpu_custom_call" | custom-call | flops 1000 | bytes 1000 | tf_op jit(solution)/shard_map/side_rows/pallas_call | solution.py:119
  82.6 3.2 %collective-permute-start.6 = (bf16[864,384]{1,0:T(8,128)(2,1)}, bf16[864,384]{1,0:T(8,128)(2,1)}, u32[]{:S(2)}, u32[]{:S(2)}) collective-permute-start(bf16[864,384]{1,0:T(8,128)(2,1)} %get-tuple-element.39), channel_id=1, source_target_pairs={{0,8},{8,16},{16,24},{1,9},{9,17},{17,25},{2,10},{10,18},{18,26},{... | collective-permute-start | bytes 1990664 | tf_op jit(solution)/shard_map/ppermute | solution.py:306
  87.1 7.7 %side_rows.3 = (bf16[864,384]{1,0:T(8,128)(2,1)}, bf16[864,384]{1,0:T(8,128)(2,1)}, s32[8]{0:T(128)}) custom-call(s32[8]{0:T(128)} %get-tuple-element.36.flags, bf16[384,1536]{1,0:T(8,128)(2,1)} %collective-permute-done.4.refs_0_, bf16[384,1536]{1,0:T(8,128)(2,1)} %collective-permute-done.5.refs_1_, bf16[3,2,384,1536]{3,2,1,0:T(8,128)(2,1)} %bitcast.17), custom_call_target="tpu_custom_call" | custom-call | flops 1000 | bytes 1000 | tf_op jit(solution)/shard_map/side_rows/pallas_call | solution.py:119
  94.8 4.8 %collective-permute-start.8 = (bf16[864,384]{1,0:T(8,128)(2,1)}, bf16[864,384]{1,0:T(8,128)(2,1)}, u32[]{:S(2)}, u32[]{:S(2)}) collective-permute-start(bf16[864,384]{1,0:T(8,128)(2,1)} %get-tuple-element.42), channel_id=1, source_target_pairs={{0,8},{8,16},{16,24},{1,9},{9,17},{17,25},{2,10},{10,18},{18,26},{... | collective-permute-start | bytes 1990664 | tf_op jit(solution)/shard_map/ppermute | solution.py:306
  100.9 5.1 %collective-permute-start.10 = (bf16[1728,384]{1,0:T(8,128)(2,1)}, bf16[1728,384]{1,0:T(8,128)(2,1)}, u32[]{:S(2)}, u32[]{:S(2)}) collective-permute-start(bf16[1728,384]{1,0:T(8,128)(2,1)} %get-tuple-element.48), channel_id=1, source_target_pairs={{0,8},{8,16},{16,24},{1,9},{9,17},{17,25},{2,10},{10,18},{18,26},{... | collective-permute-start | bytes 3981320 | tf_op jit(solution)/shard_map/ppermute | solution.py:314
  106.0 1.5 collective-permute-start.11
  108.2 6.4 %side.2 = (bf16[864,384]{1,0:T(8,128)(2,1)}, s32[8]{0:T(128)}) custom-call(s32[8]{0:T(128)} %get-tuple-element.38.flags, bf16[384,1536]{1,0:T(8,128)(2,1)} %collective-permute-done.q_ref, bf16[3,2,384,1536]{3,2,1,0:T(8,128)(2,1)} %bitcast.18, bf16[864,384]{1,0:T(8,128)(2,1)} %collective-permute-done.6.lo_ref, bf16[864,384]{1,0:T(8,128)(2,1)} %collective-permute-done.7.hi_ref), custom_call_target="tpu_custom_call" | custom-call | flops 1000 | bytes 1000 | tf_op jit(solution)/shard_map/side/pallas_call | solution.py:166
  114.7 3.8 %collective-permute-start.12 = (bf16[864,384]{1,0:T(8,128)(2,1)}, bf16[864,384]{1,0:T(8,128)(2,1)}, u32[]{:S(2)}, u32[]{:S(2)}) collective-permute-start(bf16[864,384]{1,0:T(8,128)(2,1)} %get-tuple-element.50), channel_id=1, source_target_pairs={{1,2},{3,4},{5,6},{2,1},{4,3},{6,5},{9,10},{11,12},{13,14},{10,9},... | collective-permute-start | bytes 1990664 | tf_op jit(solution)/shard_map/ppermute | solution.py:317
  118.7 6.4 %side.3 = (bf16[864,384]{1,0:T(8,128)(2,1)}, s32[8]{0:T(128)}) custom-call(s32[8]{0:T(128)} %get-tuple-element.41.flags, bf16[384,1536]{1,0:T(8,128)(2,1)} %collective-permute-done.q_ref, bf16[3,2,384,1536]{3,2,1,0:T(8,128)(2,1)} %bitcast.19, bf16[864,384]{1,0:T(8,128)(2,1)} %collective-permute-done.8.lo_ref, bf16[864,384]{1,0:T(8,128)(2,1)} %collective-permute-done.9.hi_ref), custom_call_target="tpu_custom_call" | custom-call | flops 8000000000 | bytes 1000 | tf_op jit(solution)/shard_map/side/pallas_call | solution.py:166
  125.1 4.1 %collective-permute-start.13 = (bf16[864,384]{1,0:T(8,128)(2,1)}, bf16[864,384]{1,0:T(8,128)(2,1)}, u32[]{:S(2)}, u32[]{:S(2)}) collective-permute-start(bf16[864,384]{1,0:T(8,128)(2,1)} %get-tuple-element.52), channel_id=1, source_target_pairs={{1,2},{3,4},{5,6},{2,1},{4,3},{6,5},{9,10},{11,12},{13,14},{10,9},... | collective-permute-start | bytes 1990664 | tf_op jit(solution)/shard_map/ppermute | solution.py:319
  129.2 9.7 %far.1 = (f32[1728,384]{1,0:T(8,128)}, s32[8]{0:T(128)}) custom-call(s32[8]{0:T(128)} %get-tuple-element.44.flags, s32[24]{0:T(128)} %reshape.16.offsets, bf16[384,1536]{1,0:T(8,128)(2,1)} %bitcast.25, bf16[8,2,384,1536]{3,2,1,0:T(8,128)(2,1)} %bitcast.20), custom_call_target="tpu_custom_call" | custom-call | flops 1000 | bytes 1000 | tf_op jit(solution)/shard_map/far/pallas_call | solution.py:218
  138.9 2.5 %collective-permute-done.10.refs_2_ = bf16[1728,384]{1,0:T(8,128)(2,1)} collective-permute-done((bf16[1728,384]{1,0:T(8,128)(2,1)}, bf16[1728,384]{1,0:T(8,128)(2,1)}, u32[]{:S(2)}, u32[]{:S(2)}) %collective-permute-start.10) | collective-permute-done | bytes 1327136 | tf_op jit(solution)/shard_map/ppermute | solution.py:314
  141.5 4.9 %collective-permute-done.11.refs_3_ = bf16[1728,384]{1,0:T(8,128)(2,1)} collective-permute-done((bf16[1728,384]{1,0:T(8,128)(2,1)}, bf16[1728,384]{1,0:T(8,128)(2,1)}, u32[]{:S(2)}, u32[]{:S(2)}) %collective-permute-start.11) | collective-permute-done | bytes 1327136 | tf_op jit(solution)/shard_map/ppermute | solution.py:315
  146.4 3.5 %final.2 = (bf16[384,1536]{1,0:T(8,128)(2,1)}, s32[8]{0:T(128)}) custom-call(s32[8]{0:T(128)} %get-tuple-element.45.flags, f32[1728,384]{1,0:T(8,128)} %get-tuple-element.46.refs_0_, f32[1728,384]{1,0:T(8,128)} %get-tuple-element.47.refs_1_, bf16[1728,384]{1,0:T(8,128)(2,1)} %collective-permute-done.10.refs_2_, ...), custom_call_target="tpu_custom_call" | custom-call | flops 30000001024 | bytes 1000 | tf_op jit(solution)/shard_map/final/pallas_call | solution.py:256
  150.2 3.4 %final.3 = (bf16[384,1536]{1,0:T(8,128)(2,1)}, s32[8]{0:T(128)}) custom-call(s32[8]{0:T(128)} %get-tuple-element.51.flags, f32[1728,384]{1,0:T(8,128)} %get-tuple-element.46.refs_0_, f32[1728,384]{1,0:T(8,128)} %get-tuple-element.47.refs_1_, bf16[1728,384]{1,0:T(8,128)(2,1)} %collective-permute-done.10.refs_2_, ...), custom_call_target="tpu_custom_call", output_to_operand_aliasing={{0}: (6, {})} | custom-call | flops 1000 | bytes 1000 | tf_op jit(solution)/shard_map/final/pallas_call | solution.py:256
  (22 shorter events, 6.4 us)
Async XLA Ops:
  6.5 122.7 %all-gather.3.cloned.1.call-start = ((), (), s32[]{:S(2)}) async-start(), calls=%async_computation | async-start | bytes 21233664 | tf_op jit(solution)/shard_map/all_gather | solution.py:297
  6.5 14.0 %collective-permute-start.1 = (bf16[3,2,384,1536]{3,2,1,0:T(8,128)(2,1)}, bf16[3,2,384,1536]{3,2,1,0:T(8,128)(2,1)}, u32[]{:S(2)}, u32[]{:S(2)}) collective-permute-start(bf16[3,2,384,1536]{3,2,1,0:T(8,128)(2,1)} %bitcast.13), channel_id=1, source_target_pairs={{0,1},{1,0},{2,3},{3,2},{4,5},{5,4},{6,7},{7,6},{8,9},{9,8},{10,11... | collective-permute-start | bytes 21233672 | tf_op jit(solution)/shard_map/ppermute | solution.py:290
  7.2 35.5 %collective-permute-start = (bf16[384,1536]{1,0:T(8,128)(2,1)}, bf16[384,1536]{1,0:T(8,128)(2,1)}, u32[]{:S(2)}, u32[]{:S(2)}) collective-permute-start(bf16[384,1536]{1,0:T(8,128)(2,1)} %bitcast.21), channel_id=1, source_target_pairs={{1,2},{3,4},{5,6},{2,1},{4,3},{6,5},{9,10},{11,12},{13,14},{10,9},... | collective-permute-start | bytes 3538952 | tf_op jit(solution)/shard_map/ppermute | solution.py:291
  10.2 38.2 %collective-permute-start.2 = (bf16[384,1536]{1,0:T(8,128)(2,1)}, bf16[384,1536]{1,0:T(8,128)(2,1)}, u32[]{:S(2)}, u32[]{:S(2)}) collective-permute-start(bf16[384,1536]{1,0:T(8,128)(2,1)} %bitcast.22), channel_id=1, source_target_pairs={{0,8},{8,16},{16,24},{1,9},{9,17},{17,25},{2,10},{10,18},{18,26},{... | collective-permute-start | bytes 3538952 | tf_op jit(solution)/shard_map/ppermute | solution.py:292
  14.4 34.0 %collective-permute-start.3 = (bf16[384,1536]{1,0:T(8,128)(2,1)}, bf16[384,1536]{1,0:T(8,128)(2,1)}, u32[]{:S(2)}, u32[]{:S(2)}) collective-permute-start(bf16[384,1536]{1,0:T(8,128)(2,1)} %bitcast.23), channel_id=1, source_target_pairs={{8,0},{16,8},{24,16},{9,1},{17,9},{25,17},{10,2},{18,10},{26,18},{... | collective-permute-start | bytes 3538952 | tf_op jit(solution)/shard_map/ppermute | solution.py:293
  42.7 28.2 %collective-permute-start.4 = (bf16[384,1536]{1,0:T(8,128)(2,1)}, bf16[384,1536]{1,0:T(8,128)(2,1)}, u32[]{:S(2)}, u32[]{:S(2)}) collective-permute-start(bf16[384,1536]{1,0:T(8,128)(2,1)} %collective-permute-done.q_ref), channel_id=1, source_target_pairs={{0,8},{8,16},{16,24},{1,9},{9,17},{17,25},{2,10},{10,18},{18,26},{... | collective-permute-start | bytes 3538952 | tf_op jit(solution)/shard_map/ppermute | solution.py:299
  47.0 28.0 %collective-permute-start.5 = (bf16[384,1536]{1,0:T(8,128)(2,1)}, bf16[384,1536]{1,0:T(8,128)(2,1)}, u32[]{:S(2)}, u32[]{:S(2)}) collective-permute-start(bf16[384,1536]{1,0:T(8,128)(2,1)} %collective-permute-done.q_ref), channel_id=1, source_target_pairs={{8,0},{16,8},{24,16},{9,1},{17,9},{25,17},{10,2},{18,10},{26,18},{... | collective-permute-start | bytes 3538952 | tf_op jit(solution)/shard_map/ppermute | solution.py:300
  82.6 23.4 %collective-permute-start.6 = (bf16[864,384]{1,0:T(8,128)(2,1)}, bf16[864,384]{1,0:T(8,128)(2,1)}, u32[]{:S(2)}, u32[]{:S(2)}) collective-permute-start(bf16[864,384]{1,0:T(8,128)(2,1)} %get-tuple-element.39), channel_id=1, source_target_pairs={{0,8},{8,16},{16,24},{1,9},{9,17},{17,25},{2,10},{10,18},{18,26},{... | collective-permute-start | bytes 1990664 | tf_op jit(solution)/shard_map/ppermute | solution.py:306
  85.8 22.4 %collective-permute-start.7 = (bf16[864,384]{1,0:T(8,128)(2,1)}, bf16[864,384]{1,0:T(8,128)(2,1)}, u32[]{:S(2)}, u32[]{:S(2)}) collective-permute-start(bf16[864,384]{1,0:T(8,128)(2,1)} %get-tuple-element.40), channel_id=1, source_target_pairs={{8,0},{16,8},{24,16},{9,1},{17,9},{25,17},{10,2},{18,10},{26,18},{... | collective-permute-start | bytes 1990664 | tf_op jit(solution)/shard_map/ppermute | solution.py:306
  87.1 20.4 %copy-start = (s32[1,1,12,2]{2,3,1,0:T(2,128)S(1)}, s32[1,1,12,2]{2,3,1,0:T(2,128)}, u32[]{:S(2)}) copy-start(s32[1,1,12,2]{2,3,1,0:T(2,128)} %param.5) | copy-start | bytes 292
  94.8 23.7 %collective-permute-start.8 = (bf16[864,384]{1,0:T(8,128)(2,1)}, bf16[864,384]{1,0:T(8,128)(2,1)}, u32[]{:S(2)}, u32[]{:S(2)}) collective-permute-start(bf16[864,384]{1,0:T(8,128)(2,1)} %get-tuple-element.42), channel_id=1, source_target_pairs={{0,8},{8,16},{16,24},{1,9},{9,17},{17,25},{2,10},{10,18},{18,26},{... | collective-permute-start | bytes 1990664 | tf_op jit(solution)/shard_map/ppermute | solution.py:306
  99.6 19.0 %collective-permute-start.9 = (bf16[864,384]{1,0:T(8,128)(2,1)}, bf16[864,384]{1,0:T(8,128)(2,1)}, u32[]{:S(2)}, u32[]{:S(2)}) collective-permute-start(bf16[864,384]{1,0:T(8,128)(2,1)} %get-tuple-element.43), channel_id=1, source_target_pairs={{8,0},{16,8},{24,16},{9,1},{17,9},{25,17},{10,2},{18,10},{26,18},{... | collective-permute-start | bytes 1990664 | tf_op jit(solution)/shard_map/ppermute | solution.py:306
  100.9 40.6 %collective-permute-start.10 = (bf16[1728,384]{1,0:T(8,128)(2,1)}, bf16[1728,384]{1,0:T(8,128)(2,1)}, u32[]{:S(2)}, u32[]{:S(2)}) collective-permute-start(bf16[1728,384]{1,0:T(8,128)(2,1)} %get-tuple-element.48), channel_id=1, source_target_pairs={{0,8},{8,16},{16,24},{1,9},{9,17},{17,25},{2,10},{10,18},{18,26},{... | collective-permute-start | bytes 3981320 | tf_op jit(solution)/shard_map/ppermute | solution.py:314
  106.0 40.4 %collective-permute-start.11 = (bf16[1728,384]{1,0:T(8,128)(2,1)}, bf16[1728,384]{1,0:T(8,128)(2,1)}, u32[]{:S(2)}, u32[]{:S(2)}) collective-permute-start(bf16[1728,384]{1,0:T(8,128)(2,1)} %get-tuple-element.49), channel_id=1, source_target_pairs={{8,0},{16,8},{24,16},{9,1},{17,9},{25,17},{10,2},{18,10},{26,18},{... | collective-permute-start | bytes 3981320 | tf_op jit(solution)/shard_map/ppermute | solution.py:315
  114.7 24.3 %collective-permute-start.12 = (bf16[864,384]{1,0:T(8,128)(2,1)}, bf16[864,384]{1,0:T(8,128)(2,1)}, u32[]{:S(2)}, u32[]{:S(2)}) collective-permute-start(bf16[864,384]{1,0:T(8,128)(2,1)} %get-tuple-element.50), channel_id=1, source_target_pairs={{1,2},{3,4},{5,6},{2,1},{4,3},{6,5},{9,10},{11,12},{13,14},{10,9},... | collective-permute-start | bytes 1990664 | tf_op jit(solution)/shard_map/ppermute | solution.py:317
  125.1 25.1 %collective-permute-start.13 = (bf16[864,384]{1,0:T(8,128)(2,1)}, bf16[864,384]{1,0:T(8,128)(2,1)}, u32[]{:S(2)}, u32[]{:S(2)}) collective-permute-start(bf16[864,384]{1,0:T(8,128)(2,1)} %get-tuple-element.52), channel_id=1, source_target_pairs={{1,2},{3,4},{5,6},{2,1},{4,3},{6,5},{9,10},{11,12},{13,14},{10,9},... | collective-permute-start | bytes 1990664 | tf_op jit(solution)/shard_map/ppermute | solution.py:319
Sparse Core Ops, SparseCore 0:
  20.0 105.0 all-gather.2

commit v7 on v6

--- a/solution.py
+++ b/solution.py
@@ -292,8 +292,9 @@
     q_lo = lax.ppermute(q, "ha", up)
     q_hi = lax.ppermute(q, "ha", down)
     middle = kv[1]
-
-    flags, (own,) = window("own", flags, [q], [kv, kv_mate], [(0, (0, 1))], 0, HEADS, [F32], 1, 3, after=[middle])
+    offsets = far_offsets.reshape(-1)
+
+    flags, (own,) = window("own", flags, [q], [kv, kv_mate], [(0, (0, 1))], 0, HEADS, [F32], 1, 3, after=[middle, offsets])
     tiles = lax.all_gather(middle, "wa")
     q_side, flags = lax.optimization_barrier((q_side, flags))
     qs_lo = lax.ppermute(q_side, "ha", up)
@@ -317,7 +318,6 @@
     first = lax.ppermute(first, "wa", across)
     flags, second = side_and_merge(flags, q_side, kv, second, *GROUPS[1], 3, 8 * 10**9)
     second = lax.ppermute(second, "wa", across)
-    offsets = far_offsets.reshape(-1)
     flags, far_part = far(flags, offsets, q, tiles, 0, HEADS, 3, 1000, [])
     out = None
     for (low, count), side_merged, flops in zip(GROUPS, (first, second), (30 * 10**9, 1000)):

time: 161 us -> 161 us (level)
  no operation moved by 1% of the time
where the time goes in v7:
time: 161 us; the launch traced here: 160 us
  Pallas kernels  83.2 us (52%)
  starting transfers between devices  39.8 us (25%)
  waiting for transfers between devices  17.8 us (11%)
  between operations  13.5 us (8%)
  local copies, waits for them, and re-layouts  6.11 us (4%)
    pallas_call x4, Pallas kernels, window(): pl.pallas_call(functools.partial(window_kernel, jobs, len(qs), len(kvs),...  53.8 us
    pallas_call x2, Pallas kernels, side_and_merge(): pl.pallas_call(functools.partial(side_kernel, step), grid=(nh // step,),...  12.9 us
    pallas_call x1, Pallas kernels, far(): pl.pallas_call(functools.partial(far_kernel, tiles.shape[0], h0, nh, step...  9.68 us
    ppermute x2, starting transfers between devices, side_rows(): lax.ppermute(s_hi, 'ha', up)  8.03 us
    pallas_call x2, Pallas kernels, final(): pl.pallas_call(functools.partial(final_kernel, [f for f, _, _ in parts],...  6.88 us
    ppermute x1, starting transfers between devices, on_device(): from_lo = lax.ppermute(o_hi, 'ha', up)  5.09 us
    ppermute x1, waiting for transfers between devices, on_device(): from_hi = lax.ppermute(o_lo, 'ha', down)  4.95 us
    ppermute x1, waiting for transfers between devices, on_device(): q_side = lax.ppermute(q, 'wa', across)  4.79 us
  transfers between devices with their start and end apart: 15, of which 6 were waited for; matrix products, arithmetic and copies ran while one was open for 3% of the time, Pallas kernels for 50%

profile of v7, /device:TPU:3, one launch (start us, length us, event | category | flops | bytes accessed | tf_op | source)
XLA Modules:
  0.0 160.5 jit_solution(4962540572926206748)
XLA Ops:
  7.2 3.0 %collective-permute-start = (bf16[384,1536]{1,0:T(8,128)(2,1)}, bf16[384,1536]{1,0:T(8,128)(2,1)}, u32[]{:S(2)}, u32[]{:S(2)}) collective-permute-start(bf16[384,1536]{1,0:T(8,128)(2,1)} %bitcast.21), channel_id=1, source_target_pairs={{1,2},{3,4},{5,6},{2,1},{4,3},{6,5},{9,10},{11,12},{13,14},{10,9},... | collective-permute-start | bytes 3538952 | tf_op jit(solution)/shard_map/ppermute | solution.py:291
  10.2 4.2 %collective-permute-start.2 = (bf16[384,1536]{1,0:T(8,128)(2,1)}, bf16[384,1536]{1,0:T(8,128)(2,1)}, u32[]{:S(2)}, u32[]{:S(2)}) collective-permute-start(bf16[384,1536]{1,0:T(8,128)(2,1)} %bitcast.22), channel_id=1, source_target_pairs={{0,8},{8,16},{16,24},{1,9},{9,17},{17,25},{2,10},{10,18},{18,26},{... | collective-permute-start | bytes 3538952 | tf_op jit(solution)/shard_map/ppermute | solution.py:292
  15.7 4.1 %fusion = (bf16[1,1,1,2,384,1536]{5,4,3,2,1,0:T(8,128)(2,1)}, bf16[2,384,1536]{2,1,0:T(8,128)(2,1)}) fusion(bf16[1,1,3,2,384,1536]{5,4,3,2,1,0:T(8,128)(2,1)} %param.4), kind=kLoop, calls=%fused_computation.1 | loop fusion | bytes 7077888 | tf_op jit(solution)/shard_map/slice | solution.py:294
  21.9 16.0 %own.1 = (f32[1728,384]{1,0:T(8,128)}, s32[8]{0:T(128)}) custom-call(s32[8]{0:T(128)} %stack.51.flags, bf16[2,384,1536]{2,1,0:T(8,128)(2,1)} %get-tuple-element.56.refs_0_, s32[24]{0:T(128)} %reshape.15.refs_1_.offsets, bf16[384,1536]{1,0:T(8,128)(2,1)} %bitcast.24, bf16[3,2,384,1536]{3,2,1,0:T(8,128)(2,1)} %bitcast.14, ...), custom_call_target="tpu_custom_call" | custom-call | flops 1000 | bytes 1000 | tf_op jit(solution)/shard_map/own/pallas_call | solution.py:119
  37.9 4.8 %collective-permute-done.q_ref = bf16[384,1536]{1,0:T(8,128)(2,1)} collective-permute-done((bf16[384,1536]{1,0:T(8,128)(2,1)}, bf16[384,1536]{1,0:T(8,128)(2,1)}, u32[]{:S(2)}, u32[]{:S(2)}) %collective-permute-start) | collective-permute-done | bytes 1179680 | tf_op jit(solution)/shard_map/ppermute | solution.py:291
  42.6 4.3 %collective-permute-start.4 = (bf16[384,1536]{1,0:T(8,128)(2,1)}, bf16[384,1536]{1,0:T(8,128)(2,1)}, u32[]{:S(2)}, u32[]{:S(2)}) collective-permute-start(bf16[384,1536]{1,0:T(8,128)(2,1)} %collective-permute-done.q_ref), channel_id=1, source_target_pairs={{0,8},{8,16},{16,24},{1,9},{9,17},{17,25},{2,10},{10,18},{18,26},{... | collective-permute-start | bytes 3538952 | tf_op jit(solution)/shard_map/ppermute | solution.py:300
  47.0 1.5 collective-permute-start.5
  48.4 22.5 %rows.1 = (bf16[1728,384]{1,0:T(8,128)(2,1)}, bf16[1728,384]{1,0:T(8,128)(2,1)}, s32[8]{0:T(128)}) custom-call(s32[8]{0:T(128)} %get-tuple-element.31.flags, bf16[384,1536]{1,0:T(8,128)(2,1)} %collective-permute-done.2.refs_0_, bf16[384,1536]{1,0:T(8,128)(2,1)} %collective-permute-done.3.refs_1_, bf16[3,2,384,1536]{3,2,1,0:T(8,128)(2,1)} %bitcast.15, ...), custom_call_target="tpu_custom_call" | custom-call | flops 9999999827968 | bytes 1000 | tf_op jit(solution)/shard_map/rows/pallas_call | solution.py:119
  70.9 4.0 %collective-permute-done.5.refs_1_ = bf16[384,1536]{1,0:T(8,128)(2,1)} collective-permute-done((bf16[384,1536]{1,0:T(8,128)(2,1)}, bf16[384,1536]{1,0:T(8,128)(2,1)}, u32[]{:S(2)}, u32[]{:S(2)}) %collective-permute-start.5) | collective-permute-done | bytes 1179680 | tf_op jit(solution)/shard_map/ppermute | solution.py:301
  74.9 7.7 %side_rows.2 = (bf16[864,384]{1,0:T(8,128)(2,1)}, bf16[864,384]{1,0:T(8,128)(2,1)}, s32[8]{0:T(128)}) custom-call(s32[8]{0:T(128)} %get-tuple-element.34.flags, bf16[384,1536]{1,0:T(8,128)(2,1)} %collective-permute-done.4.refs_0_, bf16[384,1536]{1,0:T(8,128)(2,1)} %collective-permute-done.5.refs_1_, bf16[3,2,384,1536]{3,2,1,0:T(8,128)(2,1)} %bitcast.16), custom_call_target="tpu_custom_call" | custom-call | flops 1000 | bytes 1000 | tf_op jit(solution)/shard_map/side_rows/pallas_call | solution.py:119
  82.6 3.2 %collective-permute-start.6 = (bf16[864,384]{1,0:T(8,128)(2,1)}, bf16[864,384]{1,0:T(8,128)(2,1)}, u32[]{:S(2)}, u32[]{:S(2)}) collective-permute-start(bf16[864,384]{1,0:T(8,128)(2,1)} %get-tuple-element.39), channel_id=1, source_target_pairs={{0,8},{8,16},{16,24},{1,9},{9,17},{17,25},{2,10},{10,18},{18,26},{... | collective-permute-start | bytes 1990664 | tf_op jit(solution)/shard_map/ppermute | solution.py:307
  87.1 7.7 %side_rows.3 = (bf16[864,384]{1,0:T(8,128)(2,1)}, bf16[864,384]{1,0:T(8,128)(2,1)}, s32[8]{0:T(128)}) custom-call(s32[8]{0:T(128)} %get-tuple-element.36.flags, bf16[384,1536]{1,0:T(8,128)(2,1)} %collective-permute-done.4.refs_0_, bf16[384,1536]{1,0:T(8,128)(2,1)} %collective-permute-done.5.refs_1_, bf16[3,2,384,1536]{3,2,1,0:T(8,128)(2,1)} %bitcast.17), custom_call_target="tpu_custom_call" | custom-call | flops 1000 | bytes 1000 | tf_op jit(solution)/shard_map/side_rows/pallas_call | solution.py:119
  94.7 4.8 %collective-permute-start.8 = (bf16[864,384]{1,0:T(8,128)(2,1)}, bf16[864,384]{1,0:T(8,128)(2,1)}, u32[]{:S(2)}, u32[]{:S(2)}) collective-permute-start(bf16[864,384]{1,0:T(8,128)(2,1)} %get-tuple-element.42), channel_id=1, source_target_pairs={{0,8},{8,16},{16,24},{1,9},{9,17},{17,25},{2,10},{10,18},{18,26},{... | collective-permute-start | bytes 1990664 | tf_op jit(solution)/shard_map/ppermute | solution.py:307
  100.9 5.1 %collective-permute-start.10 = (bf16[1728,384]{1,0:T(8,128)(2,1)}, bf16[1728,384]{1,0:T(8,128)(2,1)}, u32[]{:S(2)}, u32[]{:S(2)}) collective-permute-start(bf16[1728,384]{1,0:T(8,128)(2,1)} %get-tuple-element.48), channel_id=1, source_target_pairs={{0,8},{8,16},{16,24},{1,9},{9,17},{17,25},{2,10},{10,18},{18,26},{... | collective-permute-start | bytes 3981320 | tf_op jit(solution)/shard_map/ppermute | solution.py:315
  106.0 1.5 collective-permute-start.11
  107.5 6.4 %side.2 = (bf16[864,384]{1,0:T(8,128)(2,1)}, s32[8]{0:T(128)}) custom-call(s32[8]{0:T(128)} %get-tuple-element.38.flags, bf16[384,1536]{1,0:T(8,128)(2,1)} %collective-permute-done.q_ref, bf16[3,2,384,1536]{3,2,1,0:T(8,128)(2,1)} %bitcast.18, bf16[864,384]{1,0:T(8,128)(2,1)} %collective-permute-done.6.lo_ref, bf16[864,384]{1,0:T(8,128)(2,1)} %collective-permute-done.7.hi_ref), custom_call_target="tpu_custom_call" | custom-call | flops 1000 | bytes 1000 | tf_op jit(solution)/shard_map/side/pallas_call | solution.py:166
  113.9 3.6 %collective-permute-start.12 = (bf16[864,384]{1,0:T(8,128)(2,1)}, bf16[864,384]{1,0:T(8,128)(2,1)}, u32[]{:S(2)}, u32[]{:S(2)}) collective-permute-start(bf16[864,384]{1,0:T(8,128)(2,1)} %get-tuple-element.50), channel_id=1, source_target_pairs={{1,2},{3,4},{5,6},{2,1},{4,3},{6,5},{9,10},{11,12},{13,14},{10,9},... | collective-permute-start | bytes 1990664 | tf_op jit(solution)/shard_map/ppermute | solution.py:318
  118.6 6.4 %side.3 = (bf16[864,384]{1,0:T(8,128)(2,1)}, s32[8]{0:T(128)}) custom-call(s32[8]{0:T(128)} %get-tuple-element.41.flags, bf16[384,1536]{1,0:T(8,128)(2,1)} %collective-permute-done.q_ref, bf16[3,2,384,1536]{3,2,1,0:T(8,128)(2,1)} %bitcast.19, bf16[864,384]{1,0:T(8,128)(2,1)} %collective-permute-done.8.lo_ref, bf16[864,384]{1,0:T(8,128)(2,1)} %collective-permute-done.9.hi_ref), custom_call_target="tpu_custom_call" | custom-call | flops 8000000000 | bytes 1000 | tf_op jit(solution)/shard_map/side/pallas_call | solution.py:166
  125.1 4.0 %collective-permute-start.13 = (bf16[864,384]{1,0:T(8,128)(2,1)}, bf16[864,384]{1,0:T(8,128)(2,1)}, u32[]{:S(2)}, u32[]{:S(2)}) collective-permute-start(bf16[864,384]{1,0:T(8,128)(2,1)} %get-tuple-element.52), channel_id=1, source_target_pairs={{1,2},{3,4},{5,6},{2,1},{4,3},{6,5},{9,10},{11,12},{13,14},{10,9},... | collective-permute-start | bytes 1990664 | tf_op jit(solution)/shard_map/ppermute | solution.py:320
  129.2 9.7 %far.1 = (f32[1728,384]{1,0:T(8,128)}, s32[8]{0:T(128)}) custom-call(s32[8]{0:T(128)} %get-tuple-element.44.flags, s32[24]{0:T(128)} %reshape.15.refs_1_.offsets, bf16[384,1536]{1,0:T(8,128)(2,1)} %bitcast.25, bf16[8,2,384,1536]{3,2,1,0:T(8,128)(2,1)} %bitcast.20), custom_call_target="tpu_custom_call" | custom-call | flops 1000 | bytes 1000 | tf_op jit(solution)/shard_map/far/pallas_call | solution.py:218
  138.9 2.6 %collective-permute-done.10.refs_2_ = bf16[1728,384]{1,0:T(8,128)(2,1)} collective-permute-done((bf16[1728,384]{1,0:T(8,128)(2,1)}, bf16[1728,384]{1,0:T(8,128)(2,1)}, u32[]{:S(2)}, u32[]{:S(2)}) %collective-permute-start.10) | collective-permute-done | bytes 1327136 | tf_op jit(solution)/shard_map/ppermute | solution.py:315
  141.5 4.9 %collective-permute-done.11.refs_3_ = bf16[1728,384]{1,0:T(8,128)(2,1)} collective-permute-done((bf16[1728,384]{1,0:T(8,128)(2,1)}, bf16[1728,384]{1,0:T(8,128)(2,1)}, u32[]{:S(2)}, u32[]{:S(2)}) %collective-permute-start.11) | collective-permute-done | bytes 1327136 | tf_op jit(solution)/shard_map/ppermute | solution.py:316
  146.4 3.5 %final.2 = (bf16[384,1536]{1,0:T(8,128)(2,1)}, s32[8]{0:T(128)}) custom-call(s32[8]{0:T(128)} %get-tuple-element.45.flags, f32[1728,384]{1,0:T(8,128)} %get-tuple-element.46.refs_0_, f32[1728,384]{1,0:T(8,128)} %get-tuple-element.47.refs_1_, bf16[1728,384]{1,0:T(8,128)(2,1)} %collective-permute-done.10.refs_2_, ...), custom_call_target="tpu_custom_call" | custom-call | flops 30000001024 | bytes 1000 | tf_op jit(solution)/shard_map/final/pallas_call | solution.py:256
  150.2 3.4 %final.3 = (bf16[384,1536]{1,0:T(8,128)(2,1)}, s32[8]{0:T(128)}) custom-call(s32[8]{0:T(128)} %get-tuple-element.51.flags, f32[1728,384]{1,0:T(8,128)} %get-tuple-element.46.refs_0_, f32[1728,384]{1,0:T(8,128)} %get-tuple-element.47.refs_1_, bf16[1728,384]{1,0:T(8,128)(2,1)} %collective-permute-done.10.refs_2_, ...), custom_call_target="tpu_custom_call", output_to_operand_aliasing={{0}: (6, {})} | custom-call | flops 1000 | bytes 1000 | tf_op jit(solution)/shard_map/final/pallas_call | solution.py:256
  (22 shorter events, 8.0 us)
Async XLA Ops:
  6.5 122.6 %all-gather.3.cloned.1.call-start = ((), (), s32[]{:S(2)}) async-start(), calls=%async_computation | async-start | bytes 21233664 | tf_op jit(solution)/shard_map/all_gather | solution.py:298
  6.5 15.4 %collective-permute-start.1 = (bf16[3,2,384,1536]{3,2,1,0:T(8,128)(2,1)}, bf16[3,2,384,1536]{3,2,1,0:T(8,128)(2,1)}, u32[]{:S(2)}, u32[]{:S(2)}) collective-permute-start(bf16[3,2,384,1536]{3,2,1,0:T(8,128)(2,1)} %bitcast.13), channel_id=1, source_target_pairs={{0,1},{1,0},{2,3},{3,2},{4,5},{5,4},{6,7},{7,6},{8,9},{9,8},{10,11... | collective-permute-start | bytes 21233672 | tf_op jit(solution)/shard_map/ppermute | solution.py:290
  7.2 35.4 %collective-permute-start = (bf16[384,1536]{1,0:T(8,128)(2,1)}, bf16[384,1536]{1,0:T(8,128)(2,1)}, u32[]{:S(2)}, u32[]{:S(2)}) collective-permute-start(bf16[384,1536]{1,0:T(8,128)(2,1)} %bitcast.21), channel_id=1, source_target_pairs={{1,2},{3,4},{5,6},{2,1},{4,3},{6,5},{9,10},{11,12},{13,14},{10,9},... | collective-permute-start | bytes 3538952 | tf_op jit(solution)/shard_map/ppermute | solution.py:291
  10.2 38.2 %collective-permute-start.2 = (bf16[384,1536]{1,0:T(8,128)(2,1)}, bf16[384,1536]{1,0:T(8,128)(2,1)}, u32[]{:S(2)}, u32[]{:S(2)}) collective-permute-start(bf16[384,1536]{1,0:T(8,128)(2,1)} %bitcast.22), channel_id=1, source_target_pairs={{0,8},{8,16},{16,24},{1,9},{9,17},{17,25},{2,10},{10,18},{18,26},{... | collective-permute-start | bytes 3538952 | tf_op jit(solution)/shard_map/ppermute | solution.py:292
  14.4 34.0 %collective-permute-start.3 = (bf16[384,1536]{1,0:T(8,128)(2,1)}, bf16[384,1536]{1,0:T(8,128)(2,1)}, u32[]{:S(2)}, u32[]{:S(2)}) collective-permute-start(bf16[384,1536]{1,0:T(8,128)(2,1)} %bitcast.23), channel_id=1, source_target_pairs={{8,0},{16,8},{24,16},{9,1},{17,9},{25,17},{10,2},{18,10},{26,18},{... | collective-permute-start | bytes 3538952 | tf_op jit(solution)/shard_map/ppermute | solution.py:293
  19.9 0.7 copy-start
  42.6 28.3 %collective-permute-start.4 = (bf16[384,1536]{1,0:T(8,128)(2,1)}, bf16[384,1536]{1,0:T(8,128)(2,1)}, u32[]{:S(2)}, u32[]{:S(2)}) collective-permute-start(bf16[384,1536]{1,0:T(8,128)(2,1)} %collective-permute-done.q_ref), channel_id=1, source_target_pairs={{0,8},{8,16},{16,24},{1,9},{9,17},{17,25},{2,10},{10,18},{18,26},{... | collective-permute-start | bytes 3538952 | tf_op jit(solution)/shard_map/ppermute | solution.py:300
  47.0 28.0 %collective-permute-start.5 = (bf16[384,1536]{1,0:T(8,128)(2,1)}, bf16[384,1536]{1,0:T(8,128)(2,1)}, u32[]{:S(2)}, u32[]{:S(2)}) collective-permute-start(bf16[384,1536]{1,0:T(8,128)(2,1)} %collective-permute-done.q_ref), channel_id=1, source_target_pairs={{8,0},{16,8},{24,16},{9,1},{17,9},{25,17},{10,2},{18,10},{26,18},{... | collective-permute-start | bytes 3538952 | tf_op jit(solution)/shard_map/ppermute | solution.py:301
  82.6 23.4 %collective-permute-start.6 = (bf16[864,384]{1,0:T(8,128)(2,1)}, bf16[864,384]{1,0:T(8,128)(2,1)}, u32[]{:S(2)}, u32[]{:S(2)}) collective-permute-start(bf16[864,384]{1,0:T(8,128)(2,1)} %get-tuple-element.39), channel_id=1, source_target_pairs={{0,8},{8,16},{16,24},{1,9},{9,17},{17,25},{2,10},{10,18},{18,26},{... | collective-permute-start | bytes 1990664 | tf_op jit(solution)/shard_map/ppermute | solution.py:307
  85.8 21.7 %collective-permute-start.7 = (bf16[864,384]{1,0:T(8,128)(2,1)}, bf16[864,384]{1,0:T(8,128)(2,1)}, u32[]{:S(2)}, u32[]{:S(2)}) collective-permute-start(bf16[864,384]{1,0:T(8,128)(2,1)} %get-tuple-element.40), channel_id=1, source_target_pairs={{8,0},{16,8},{24,16},{9,1},{17,9},{25,17},{10,2},{18,10},{26,18},{... | collective-permute-start | bytes 1990664 | tf_op jit(solution)/shard_map/ppermute | solution.py:307
  94.7 22.8 %collective-permute-start.8 = (bf16[864,384]{1,0:T(8,128)(2,1)}, bf16[864,384]{1,0:T(8,128)(2,1)}, u32[]{:S(2)}, u32[]{:S(2)}) collective-permute-start(bf16[864,384]{1,0:T(8,128)(2,1)} %get-tuple-element.42), channel_id=1, source_target_pairs={{0,8},{8,16},{16,24},{1,9},{9,17},{17,25},{2,10},{10,18},{18,26},{... | collective-permute-start | bytes 1990664 | tf_op jit(solution)/shard_map/ppermute | solution.py:307
  99.6 19.0 %collective-permute-start.9 = (bf16[864,384]{1,0:T(8,128)(2,1)}, bf16[864,384]{1,0:T(8,128)(2,1)}, u32[]{:S(2)}, u32[]{:S(2)}) collective-permute-start(bf16[864,384]{1,0:T(8,128)(2,1)} %get-tuple-element.43), channel_id=1, source_target_pairs={{8,0},{16,8},{24,16},{9,1},{17,9},{25,17},{10,2},{18,10},{26,18},{... | collective-permute-start | bytes 1990664 | tf_op jit(solution)/shard_map/ppermute | solution.py:307
  100.9 40.6 %collective-permute-start.10 = (bf16[1728,384]{1,0:T(8,128)(2,1)}, bf16[1728,384]{1,0:T(8,128)(2,1)}, u32[]{:S(2)}, u32[]{:S(2)}) collective-permute-start(bf16[1728,384]{1,0:T(8,128)(2,1)} %get-tuple-element.48), channel_id=1, source_target_pairs={{0,8},{8,16},{16,24},{1,9},{9,17},{17,25},{2,10},{10,18},{18,26},{... | collective-permute-start | bytes 3981320 | tf_op jit(solution)/shard_map/ppermute | solution.py:315
  106.0 40.4 %collective-permute-start.11 = (bf16[1728,384]{1,0:T(8,128)(2,1)}, bf16[1728,384]{1,0:T(8,128)(2,1)}, u32[]{:S(2)}, u32[]{:S(2)}) collective-permute-start(bf16[1728,384]{1,0:T(8,128)(2,1)} %get-tuple-element.49), channel_id=1, source_target_pairs={{8,0},{16,8},{24,16},{9,1},{17,9},{25,17},{10,2},{18,10},{26,18},{... | collective-permute-start | bytes 3981320 | tf_op jit(solution)/shard_map/ppermute | solution.py:316
  113.9 25.0 %collective-permute-start.12 = (bf16[864,384]{1,0:T(8,128)(2,1)}, bf16[864,384]{1,0:T(8,128)(2,1)}, u32[]{:S(2)}, u32[]{:S(2)}) collective-permute-start(bf16[864,384]{1,0:T(8,128)(2,1)} %get-tuple-element.50), channel_id=1, source_target_pairs={{1,2},{3,4},{5,6},{2,1},{4,3},{6,5},{9,10},{11,12},{13,14},{10,9},... | collective-permute-start | bytes 1990664 | tf_op jit(solution)/shard_map/ppermute | solution.py:318
  125.1 25.1 %collective-permute-start.13 = (bf16[864,384]{1,0:T(8,128)(2,1)}, bf16[864,384]{1,0:T(8,128)(2,1)}, u32[]{:S(2)}, u32[]{:S(2)}) collective-permute-start(bf16[864,384]{1,0:T(8,128)(2,1)} %get-tuple-element.52), channel_id=1, source_target_pairs={{1,2},{3,4},{5,6},{2,1},{4,3},{6,5},{9,10},{11,12},{13,14},{10,9},... | collective-permute-start | bytes 1990664 | tf_op jit(solution)/shard_map/ppermute | solution.py:320
Sparse Core Ops, SparseCore 0:
  20.0 105.3 all-gather.2
